TPU v7x, 32 devices: a whole 2x2x4 slice. The times are simulated.
32 devices in a mesh: fsdp: 16 (over z, y, core), rep: 2 (over x).
Axes of the slice: x: 2, y: 2, z: 4, core: 2. Of those that a mesh axis runs over, the one named last changes fastest.
Arguments:
- token_ids: int32 [16384], P(('fsdp', 'rep')), may hold values from 0 to 30719
- boxes: int32 [4, 16384], P(None, ('fsdp', 'rep')), may hold values from 0 to 999
- lengths: int32 [32], P(('fsdp', 'rep')), may hold values from 40 to 512, as said below
- slots: int32 [32, 128], P(('fsdp', 'rep')), may hold values from 0 to 255, as said below
- labels: int32 [32, 128], P(('fsdp', 'rep')), may hold values from 0 to 30719
- table: float32 [30720, 768], P('fsdp')
- mats: float32 [7, 768, 768], P(None, 'fsdp')
- up: float32 [768, 3072], P('fsdp'), may hold values from -0.21875 to 0.21875
- down: float32 [3072, 768], P('fsdp'), may hold values from -0.109375 to 0.109375
- vectors: float32 [11, 768], P(None, 'fsdp')
- up_bias: float32 [3072], P('fsdp'), may hold values from -1.8 to 1.8
- table_rows: float32 [30720], P('fsdp'), may hold values from 3.0825835e-11 to 4.6238754e-10
- table_cols: float32 [768], replicated, may hold values from 3.0825835e-11 to 4.6238754e-10
- mats_rows: float32 [7, 768], P(None, 'fsdp'), may hold values from 3.0825835e-11 to 4.6238754e-10
- mats_cols: float32 [7, 768], replicated, may hold values from 3.0825835e-11 to 4.6238754e-10
- up_rows: float32 [768], P('fsdp'), may hold values from 3.0825835e-11 to 4.6238754e-10
- up_cols: float32 [3072], replicated, may hold values from 3.0825835e-11 to 4.6238754e-10
- down_rows: float32 [3072], P('fsdp'), may hold values from 3.0825835e-11 to 4.6238754e-10
- down_cols: float32 [768], replicated, may hold values from 3.0825835e-11 to 4.6238754e-10
- vectors_second: float32 [11, 768], P(None, 'fsdp'), may hold values from 1.5412918e-10 to 2.3119378e-09
- up_bias_second: float32 [3072], P('fsdp'), may hold values from 1.5412917e-11 to 6.165167e-11
Outputs:
- table_grad: float32 [30720, 768], P('fsdp')
- table_rows_new: float32 [30720], P('fsdp')
- table_cols_new: float32 [768], replicated
- table_new: float32 [30720, 768], P('fsdp')
- mats_grad: float32 [7, 768, 768], P(None, 'fsdp')
- mats_rows_new: float32 [7, 768], P(None, 'fsdp')
- mats_cols_new: float32 [7, 768], replicated
- mats_new: float32 [7, 768, 768], P(None, 'fsdp')
- up_grad: float32 [768, 3072], P('fsdp')
- up_rows_new: float32 [768], P('fsdp')
- up_cols_new: float32 [3072], replicated
- up_new: float32 [768, 3072], P('fsdp')
- down_grad: float32 [3072, 768], P('fsdp')
- down_rows_new: float32 [3072], P('fsdp')
- down_cols_new: float32 [768], replicated
- down_new: float32 [3072, 768], P('fsdp')
- vectors_grad: float32 [11, 768], P(None, 'fsdp')
- vectors_second_new: float32 [11, 768], P(None, 'fsdp')
- vectors_new: float32 [11, 768], P(None, 'fsdp')
- up_bias_grad: float32 [3072], P('fsdp')
- up_bias_second_new: float32 [3072], P('fsdp')
- up_bias_new: float32 [3072], P('fsdp')
- grad_norm: float32 [], replicated
- loss_parts: float32 [4], replicated
Inputs may be any that keep to these rules, and one draw needn't show every extreme that they name: `lengths`: real tokens of each page; some page has exactly 512 and some exactly 40. `slots`: a slot's place along its page's real tokens, in 256ths of its length.
All inputs are finite; a program needn't handle non-finite values.
Results may differ from a plain program's by a relative error of at most 0.013.
The roundings to bfloat16 on the way count: a program that leaves them out, or rounds other values in their place, can miss the bound.
Values may be sent and summed in bfloat16 or wider, within the bound.
No kernel may reach another device: no remote copies, remote signals or barrier semaphores. Data moves between devices by JAX's collectives and lax.ppermute only.
A program may use at most 320 MiB of HBM per device.

v0:
```python
from functools import partial
import math

import jax
import jax.numpy as jnp
from jax import lax
from jax.sharding import PartitionSpec as P

HEAD_DIM = 64
PAGE_LEN = 512
M_TOK = 64
M_AREA = 64
STEP = 10


EPSILON = 1e-05
CLIP_NORM = 0.1
LEARN_RATE = 0.02
VECTOR_RATE = 0.3
TINY_TERM = 1e-30
NEGATIVE = -1e30
BFLOAT = jnp.bfloat16
FLOAT = jnp.float32


def combined_all(part, axis, combine):
    gathered = jax.tree.map(lambda a: lax.all_gather(a, axis), part)

    def take(source):
        return jax.tree.map(lambda a: lax.dynamic_index_in_dim(a, source, 0, False), gathered)

    return lax.fori_loop(
        1, lax.axis_size(axis), lambda source, state: combine(state, take(source)), take(0)
    )


def layer_norm(value, gain, shift):
    center = value - jnp.mean(value, axis=-1, keepdims=True)
    spread = jnp.mean(center * center, axis=-1, keepdims=True)
    return center * lax.rsqrt(spread + EPSILON) * gain + shift


def box_features(boxes, width):
    count = width // 8
    freqs = jnp.exp(-math.log(10000.0) * jnp.arange(count, dtype=FLOAT) / count)
    angle = boxes.astype(FLOAT)[:, :, None] * freqs[None, None, :]
    waves = jnp.concatenate([jnp.sin(angle), jnp.cos(angle)], axis=2)
    return jnp.transpose(waves, (1, 0, 2)).reshape(boxes.shape[1], width)


def slot_info(lengths, slots):
    n_tok = jnp.minimum(M_TOK, 1 + lengths * M_TOK // PAGE_LEN)
    n_area = jnp.minimum(M_AREA, 1 + lengths * (3 * M_AREA) // (4 * PAGE_LEN))
    index = jnp.arange(M_TOK + M_AREA, dtype=jnp.int32)[None, :]
    valid = jnp.where(index < M_TOK, index < n_tok[:, None], index - M_TOK < n_area[:, None])
    where_at = slots * lengths[:, None] // 256
    return (valid, where_at)


def product(left, right):
    return jnp.dot(left, right, preferred_element_type=FLOAT)


def contract_rows(left, right):
    return lax.dot_general(left, right, (((0,), (0,)), ((), ())), preferred_element_type=FLOAT)


def times_transposed(left, right):
    return lax.dot_general(left, right, (((1,), (1,)), ((), ())), preferred_element_type=FLOAT)


def combine_mass(first, second):
    peak = jnp.maximum(first[0], second[0])
    return (peak, first[1] * jnp.exp(first[0] - peak) + second[1] * jnp.exp(second[0] - peak))


def page_scores(query, keys, box_query, box_key, keep):
    scale = query.shape[-1] ** (-0.5)
    raw = jnp.einsum("qhe,khe->hqk", query, keys, preferred_element_type=FLOAT)
    raw = raw + jnp.einsum("qhe,khe->hqk", query, box_key, preferred_element_type=FLOAT)
    raw = raw + jnp.einsum("qhe,khe->hqk", box_query, keys, preferred_element_type=FLOAT)
    return jnp.where(keep[None, None, :], raw * scale, NEGATIVE)


def attend(items):
    query, keys, values, box_query, box_key, keep = items
    score = page_scores(query, keys, box_query, box_key, keep)
    peak = jnp.max(score, axis=-1, keepdims=True)
    expo = jnp.exp(score - peak)
    mass = jnp.sum(expo, axis=-1, keepdims=True)
    prob = (expo / mass).astype(BFLOAT)
    mixed = jnp.einsum("hqk,khe->qhe", prob, values, preferred_element_type=FLOAT).astype(BFLOAT)
    return (mixed, peak[..., 0] + jnp.log(mass[..., 0]))


def attend_back(items):
    query, keys, values, box_query, box_key, keep, log_total, grad_mixed = items
    score = page_scores(query, keys, box_query, box_key, keep)
    prob = jnp.exp(score - log_total[..., None])
    grad_values = jnp.einsum(
        "hqk,qhe->khe", prob.astype(BFLOAT), grad_mixed, preferred_element_type=FLOAT
    )
    grad_prob = jnp.einsum("qhe,khe->hqk", grad_mixed, values, preferred_element_type=FLOAT)
    grad_score = prob * (grad_prob - jnp.sum(prob * grad_prob, axis=-1, keepdims=True))
    grad_low = grad_score.astype(BFLOAT) * jnp.asarray(query.shape[-1] ** (-0.5), BFLOAT)
    with_keys = jnp.einsum("hqk,khe->qhe", grad_low, keys, preferred_element_type=FLOAT)
    with_query = jnp.einsum("hqk,qhe->khe", grad_low, query, preferred_element_type=FLOAT)
    grad_query = with_keys + jnp.einsum(
        "hqk,khe->qhe", grad_low, box_key, preferred_element_type=FLOAT
    )
    grad_keys = with_query + jnp.einsum(
        "hqk,qhe->khe", grad_low, box_query, preferred_element_type=FLOAT
    )
    return (
        grad_query.astype(BFLOAT),
        grad_keys.astype(BFLOAT),
        grad_values.astype(BFLOAT),
        with_keys.astype(BFLOAT),
        with_query.astype(BFLOAT),
    )


def layer_forward(weights, embedded, features_low, keep):
    mats, up, down, vectors, up_bias = weights
    gains = vectors.astype(FLOAT)
    pages, page_len = keep.shape
    tokens, width = embedded.shape

    def split(value):
        return value.reshape(pages, page_len, width // HEAD_DIM, HEAD_DIM)

    start_state = layer_norm(embedded, gains[0], gains[1])
    act = start_state.astype(BFLOAT)
    place = (product(features_low, mats[0]) + gains[9]).astype(BFLOAT)
    query = (product(act, mats[1]) + gains[6]).astype(BFLOAT)
    keys = product(act, mats[2]).astype(BFLOAT)
    values = (product(act, mats[3]) + gains[7]).astype(BFLOAT)
    box_query = product(place, mats[4]).astype(BFLOAT)
    box_key = product(place, mats[5]).astype(BFLOAT)
    mixed, log_total = lax.map(
        attend, (split(query), split(keys), split(values), split(box_query), split(box_key), keep)
    )
    mixed = mixed.reshape(tokens, width)
    first_sum = start_state + (product(mixed, mats[6]) + gains[8])
    middle = layer_norm(first_sum, gains[2], gains[3])
    middle_low = middle.astype(BFLOAT)
    upper = product(middle_low, up) + up_bias.astype(FLOAT)
    active = jax.nn.gelu(upper, approximate=False).astype(BFLOAT)
    second_sum = middle + (product(active, down) + gains[10])
    kept = (
        embedded,
        act,
        place,
        query,
        keys,
        values,
        box_query,
        box_key,
        log_total,
        mixed,
        first_sum,
        middle_low,
        upper,
        active,
        second_sum,
    )
    return (layer_norm(second_sum, gains[4], gains[5]), kept)


def layer_backward(weights, features_low, keep, kept, grad_out):
    mats, up, down, vectors, up_bias = weights
    gains = vectors.astype(FLOAT)
    (
        embedded,
        act,
        place,
        query,
        keys,
        values,
        box_query,
        box_key,
        log_total,
        mixed,
        first_sum,
        middle_low,
        upper,
        active,
        second_sum,
    ) = kept
    pages, page_len = keep.shape
    tokens, width = embedded.shape

    def split(value):
        return value.reshape(pages, page_len, width // HEAD_DIM, HEAD_DIM)

    def column_sum(value):
        return jnp.sum(value.astype(FLOAT), axis=0)

    grad_second, gain_four, gain_five = jax.vjp(layer_norm, second_sum, gains[4], gains[5])[1](
        grad_out
    )
    grad_feed = grad_second.astype(BFLOAT)
    grad_down = contract_rows(active, grad_feed)
    grad_active = times_transposed(grad_feed, down)
    grad_upper = jax.vjp(partial(jax.nn.gelu, approximate=False), upper)[1](grad_active)[0].astype(
        BFLOAT
    )
    grad_up = contract_rows(middle_low, grad_upper)
    grad_middle = grad_second + times_transposed(grad_upper, up)
    grad_first, gain_two, gain_three = jax.vjp(layer_norm, first_sum, gains[2], gains[3])[1](
        grad_middle
    )
    grad_attended = grad_first.astype(BFLOAT)
    grad_output = contract_rows(mixed, grad_attended)
    grad_mixed = times_transposed(grad_attended, mats[6]).astype(BFLOAT)
    pieces = lax.map(
        attend_back,
        (
            split(query),
            split(keys),
            split(values),
            split(box_query),
            split(box_key),
            keep,
            log_total,
            split(grad_mixed),
        ),
    )
    grad_query, grad_keys, grad_values, grad_box_query, grad_box_key = tuple(
        (item.reshape(tokens, width) for item in pieces)
    )
    grad_place = (
        times_transposed(grad_box_query, mats[4]) + times_transposed(grad_box_key, mats[5])
    ).astype(BFLOAT)
    grad_start = (
        grad_first + times_transposed(grad_query, mats[1]) + times_transposed(grad_keys, mats[2])
    )
    grad_start = grad_start + times_transposed(grad_values, mats[3])
    grad_embedded, gain_zero, gain_one = jax.vjp(layer_norm, embedded, gains[0], gains[1])[1](
        grad_start
    )
    grad_mats = jnp.stack(
        [
            contract_rows(features_low, grad_place),
            contract_rows(act, grad_query),
            contract_rows(act, grad_keys),
            contract_rows(act, grad_values),
            contract_rows(place, grad_box_query),
            contract_rows(place, grad_box_key),
            grad_output,
        ]
    )
    grad_vectors = jnp.stack(
        [
            gain_zero,
            gain_one,
            gain_two,
            gain_three,
            gain_four,
            gain_five,
            column_sum(grad_query),
            column_sum(grad_values),
            column_sum(grad_attended),
            column_sum(grad_place),
            column_sum(grad_feed),
        ]
    )
    return ((grad_mats, grad_up, grad_down, grad_vectors, column_sum(grad_upper)), grad_embedded)


def body(
    token_ids,
    boxes,
    lengths,
    slots,
    labels,
    table,
    mats,
    up,
    down,
    vectors,
    up_bias,
    table_rows,
    table_cols,
    mats_rows,
    mats_cols,
    up_rows,
    up_cols,
    down_rows,
    down_cols,
    vectors_second,
    up_bias_second,
):
    pages = lengths.shape[0]
    tokens = token_ids.shape[0]
    page_len = tokens // pages
    width = table.shape[1]
    shard_rows = table.shape[0]
    groups = lax.axis_size("fsdp")
    mats_low = mats.astype(BFLOAT)
    up_low = up.astype(BFLOAT)
    down_low = down.astype(BFLOAT)
    vectors_low = vectors.astype(BFLOAT)
    bias_low = up_bias.astype(BFLOAT)
    gathered = (
        lax.all_gather(mats_low, "fsdp", axis=1, tiled=True),
        lax.all_gather(up_low, "fsdp", axis=0, tiled=True),
        lax.all_gather(down_low, "fsdp", axis=0, tiled=True),
        lax.all_gather(vectors_low, "fsdp", axis=1, tiled=True),
        lax.all_gather(bias_low, "fsdp", axis=0, tiled=True),
    )
    valid, where_at = slot_info(lengths, slots)
    slot_count = valid.shape[1]
    table_low = table.astype(BFLOAT)
    lookup_ids = jnp.concatenate([token_ids, labels.reshape(-1)])
    piece = lax.all_gather(table_low, "fsdp", axis=0, tiled=True)
    local = lookup_ids
    inside = (local >= 0) & (local < piece.shape[0])
    found = jnp.take(piece, jnp.clip(local, 0, piece.shape[0] - 1), axis=0).astype(FLOAT)
    looked = jnp.where(inside[:, None], found, 0.0)
    embedded = looked[:tokens]
    label_rows = looked[tokens:]
    keep = jnp.arange(page_len)[None, :] < lengths[:, None]
    features_low = box_features(boxes, width).astype(BFLOAT)
    top_state, kept = layer_forward(gathered, embedded, features_low, keep)
    picked = jnp.take_along_axis(
        top_state.reshape(pages, page_len, width), where_at[:, :, None], axis=1
    )
    rows_low = picked.reshape(pages * slot_count, width).astype(BFLOAT)
    validf = valid.reshape(-1).astype(FLOAT)
    flags = validf.astype(BFLOAT)
    rows_all, flags_all = (
        lax.all_gather(rows_low, "fsdp", axis=0, tiled=True),
        lax.all_gather(flags, "fsdp", axis=0, tiled=True),
    )
    logits = times_transposed(rows_all, table_low)
    peak = jnp.max(logits, axis=1)
    mass = jnp.sum(jnp.exp(logits - peak[:, None]), axis=1)
    peak_all, mass_all = combined_all((peak, mass), "fsdp", combine_mass)
    log_total = peak_all + jnp.log(mass_all)
    own = rows_low.shape[0]
    own_total = lax.dynamic_slice_in_dim(log_total, lax.axis_index("fsdp") * own, own)
    target = jnp.sum(rows_low.astype(FLOAT) * label_rows, axis=1)
    loss_rows = (own_total - target) * validf
    is_token = jnp.tile(jnp.arange(slot_count) < M_TOK, pages)
    local_parts = jnp.stack(
        [
            jnp.sum(jnp.where(is_token, loss_rows, 0.0)),
            jnp.sum(jnp.where(is_token, validf, 0.0)),
            jnp.sum(jnp.where(is_token, 0.0, loss_rows)),
            jnp.sum(jnp.where(is_token, 0.0, validf)),
        ]
    )
    loss_parts = lax.psum(local_parts, ("fsdp", "rep"))
    share = jnp.where(jnp.arange(slot_count) < M_TOK, 1.0 / loss_parts[1], 1.0 / loss_parts[3])
    weight_all = flags_all.astype(FLOAT) * jnp.tile(share, rows_all.shape[0] // slot_count)
    weight_own = validf * jnp.tile(share, pages)
    grad_logits = (jnp.exp(logits - log_total[:, None]) * weight_all[:, None]).astype(BFLOAT)
    head_grad = contract_rows(grad_logits, rows_all)
    grad_rows = (
        lax.psum_scatter(product(grad_logits, table_low), "fsdp", scatter_dimension=0, tiled=True)
        - weight_own[:, None] * label_rows
    )
    grad_top = jnp.zeros((pages, page_len, width), FLOAT)
    grad_top = grad_top.at[jnp.arange(pages)[:, None], where_at].add(
        grad_rows.reshape(pages, slot_count, width)
    )
    layer_grads, grad_embedded = layer_backward(
        gathered, features_low, keep, kept, grad_top.reshape(tokens, width)
    )
    lookup_terms = jnp.concatenate([grad_embedded, -weight_own[:, None] * rows_low.astype(FLOAT)])
    grad_mats, grad_up, grad_down, grad_vectors, grad_bias = layer_grads
    table_part = head_grad
    local = lookup_ids
    inside = (local >= 0) & (local < shard_rows * lax.axis_size("fsdp"))
    table_part = table_part + lax.psum_scatter(
        jax.ops.segment_sum(
            jnp.where(inside[:, None], lookup_terms, 0.0),
            jnp.where(inside, local, 0),
            num_segments=shard_rows * lax.axis_size("fsdp"),
        ),
        "fsdp",
        scatter_dimension=0,
        tiled=True,
    )
    mats_part, up_part, down_part, vectors_part, bias_part = (
        lax.psum_scatter(grad_mats, "fsdp", scatter_dimension=1, tiled=True),
        lax.psum_scatter(grad_up, "fsdp", scatter_dimension=0, tiled=True),
        lax.psum_scatter(grad_down, "fsdp", scatter_dimension=0, tiled=True),
        lax.psum_scatter(grad_vectors, "fsdp", scatter_dimension=1, tiled=True),
        lax.psum_scatter(grad_bias, "fsdp", scatter_dimension=0, tiled=True),
    )
    table_grad, mats_grad, up_grad, down_grad, vectors_grad, bias_grad = (
        lax.psum(table_part.astype(jnp.bfloat16), "rep").astype(jnp.float32),
        lax.psum(mats_part.astype(jnp.bfloat16), "rep").astype(jnp.float32),
        lax.psum(up_part.astype(jnp.bfloat16), "rep").astype(jnp.float32),
        lax.psum(down_part.astype(jnp.bfloat16), "rep").astype(jnp.float32),
        lax.psum(vectors_part.astype(jnp.bfloat16), "rep").astype(jnp.float32),
        lax.psum(bias_part.astype(jnp.bfloat16), "rep").astype(jnp.float32),
    )
    decay = 1.0 - STEP ** (-0.8)
    items = (
        (table_grad[None], table[None], table_rows[None], table_cols[None]),
        (mats_grad, mats, mats_rows, mats_cols),
        (up_grad[None], up[None], up_rows[None], up_cols[None]),
        (down_grad[None], down[None], down_rows[None], down_cols[None]),
    )
    full_rows = jnp.concatenate(
        [jnp.full((item[0].shape[0],), item[0].shape[1] * groups, FLOAT) for item in items]
    )
    squares = jnp.concatenate(
        [jnp.sum(item[0] * item[0], axis=(1, 2)) for item in items]
        + [jnp.stack([jnp.sum(vectors_grad * vectors_grad), jnp.sum(bias_grad * bias_grad)])]
    )

    def fresh_rows(clip):
        clipped = [item[0] * clip for item in items]
        square = [value * value + TINY_TERM for value in clipped]
        rows_new = [
            decay * item[2] + (1.0 - decay) * jnp.mean(value, axis=2)
            for item, value in zip(items, square)
        ]
        return (clipped, square, rows_new)

    square_total = lax.psum(squares, "fsdp")
    grad_norm = jnp.sqrt(jnp.sum(square_total))
    clip = jnp.minimum(1.0, CLIP_NORM / grad_norm)
    clipped, square, rows_new = fresh_rows(clip)
    local_cols = [jnp.sum(value, axis=1) for value in square]
    row_sums = jnp.concatenate([jnp.sum(value, axis=1) for value in rows_new])
    cols_table, cols_mats, cols_up, cols_down, row_total = lax.psum(
        (local_cols[0], local_cols[1], local_cols[2], local_cols[3], row_sums), "fsdp"
    )
    col_totals = [cols_table, cols_mats, cols_up, cols_down]
    row_means = row_total / full_rows
    results = []
    offset_rows = 0
    for index in range(4):
        grad, weight, rows_old, cols_old = items[index]
        batch = grad.shape[0]
        cols_new = decay * cols_old + (1.0 - decay) * col_totals[index] / (grad.shape[1] * groups)
        means = row_means[offset_rows : offset_rows + batch]
        second = rows_new[index][:, :, None] * cols_new[:, None, :] / means[:, None, None]
        results.append(
            (
                clipped[index],
                rows_new[index],
                cols_new,
                weight - LEARN_RATE * clipped[index] * lax.rsqrt(second),
            )
        )
        offset_rows += batch
    clipped_vectors = vectors_grad * clip
    vectors_second_new = decay * vectors_second + (1.0 - decay) * (
        clipped_vectors * clipped_vectors + TINY_TERM
    )
    vectors_new = vectors - VECTOR_RATE * clipped_vectors * lax.rsqrt(vectors_second_new)
    clipped_bias = bias_grad * clip
    bias_second_new = decay * up_bias_second + (1.0 - decay) * (
        clipped_bias * clipped_bias + TINY_TERM
    )
    bias_new = up_bias - VECTOR_RATE * clipped_bias * lax.rsqrt(bias_second_new)
    table_out, mats_out, up_out, down_out = results
    return (
        table_out[0][0],
        table_out[1][0],
        table_out[2][0],
        table_out[3][0],
        mats_out[0],
        mats_out[1],
        mats_out[2],
        mats_out[3],
        up_out[0][0],
        up_out[1][0],
        up_out[2][0],
        up_out[3][0],
        down_out[0][0],
        down_out[1][0],
        down_out[2][0],
        down_out[3][0],
        clipped_vectors,
        vectors_second_new,
        vectors_new,
        clipped_bias,
        bias_second_new,
        bias_new,
        grad_norm,
        loss_parts,
    )


def solution(mesh):
    return jax.shard_map(
        body,
        mesh=mesh,
        in_specs=(
            P(("fsdp", "rep")),
            P(None, ("fsdp", "rep")),
            P(("fsdp", "rep")),
            P(("fsdp", "rep"), None),
            P(("fsdp", "rep"), None),
            P("fsdp", None),
            P(None, "fsdp", None),
            P("fsdp", None),
            P("fsdp", None),
            P(None, "fsdp"),
            P("fsdp"),
            P("fsdp"),
            P(),
            P(None, "fsdp"),
            P(),
            P("fsdp"),
            P(),
            P("fsdp"),
            P(),
            P(None, "fsdp"),
            P("fsdp"),
        ),
        out_specs=(
            P("fsdp", None),
            P("fsdp"),
            P(),
            P("fsdp", None),
            P(None, "fsdp", None),
            P(None, "fsdp"),
            P(),
            P(None, "fsdp", None),
            P("fsdp", None),
            P("fsdp"),
            P(),
            P("fsdp", None),
            P("fsdp", None),
            P("fsdp"),
            P(),
            P("fsdp", None),
            P(None, "fsdp"),
            P(None, "fsdp"),
            P(None, "fsdp"),
            P("fsdp"),
            P("fsdp"),
            P("fsdp"),
            P(),
            P(),
        ),
        check_vma=False,
    )
```

profile of v0, /device:TPU:0, one launch (start us, length us, event | category | flops | bytes accessed | tf_op | source)
XLA Modules:
  0.0 2325.5 jit_solution(15252397211497957168)
XLA Ops:
  17.6 23.8 %all-gather.2 = bf16[16,48,11]{1,2,0:T(8,128)(2,1)S(1)} all-gather(bf16[1,48,11]{1,2,0:T(8,128)(2,1)S(1)} %convert_bitcast_fusion), channel_id=1, replica_groups=mesh['fsdp'=16,'rep'=2] {'fsdp'}, dimensions={0}, use_global_device_ids=true | all-gather | bytes 17952 | tf_op jit(solution)/shard_map/all_gather | solution.py:309
  43.7 31.6 %all-reduce.1 = bf16[3072]{0:T(1024)(128)(2,1)S(1)} all-reduce(bf16[3072]{0:T(1024)(128)(2,1)S(1)} %dynamic-update-slice), channel_id=1, replica_groups=mesh['fsdp'=16,'rep'=2] {'fsdp'}, use_global_device_ids=true, to_apply=%add.1 | all-reduce | flops 3072 | bytes 12288
  79.2 9.5 all-gather.12.cloned.1.call-done
  96.9 224.9 %all-gather.10.cloned.1.call-done = bf16[30720,768]{1,0:T(8,128)(2,1)} async-done(((bf16[1920,768]{1,0:T(8,128)(2,1)}), bf16[30720,768]{1,0:T(8,128)(2,1)}) %all-gather.10.cloned.1.call-update) | async-done | bytes 47185936 | tf_op jit(solution)/shard_map/all_gather | solution.py:316
  321.8 10.1 gather_fusion
  357.4 12.7 fusion.123
  380.4 19.7 multiply_convert_fusion.2
  400.2 32.6 %all-gather.16.cloned.1.call-done = bf16[3072,768]{1,0:T(8,128)(2,1)} async-done(((bf16[192,768]{1,0:T(8,128)(2,1)}), bf16[3072,768]{1,0:T(8,128)(2,1)}) %all-gather.16.cloned.1.call-update) | async-done | bytes 4718608 | tf_op jit(solution)/shard_map/all_gather | solution.py:308
  446.8 19.8 all-gather.3
  466.6 23.7 %all-gather.18.cloned.1.call-done = bf16[2048,768]{1,0:T(8,128)(2,1)} async-done(((bf16[128,768]{1,0:T(8,128)(2,1)}), bf16[2048,768]{1,0:T(8,128)(2,1)}) %all-gather.18.cloned.1.call-update) | async-done | bytes 3145744 | tf_op jit(solution)/shard_map/all_gather | solution.py:333
  490.3 12.2 fusion.126
  510.1 20.9 all-gather.1
  533.4 19.2 all-gather
  554.8 14.0 while.11
  574.2 38.0 %psum.91 = f32[4]{0:T(128)S(1)} all-reduce(f32[4]{0:T(128)S(1)} %pad_maximum_fusion), channel_id=1, replica_groups=mesh['fsdp'=16,'rep'=2] {'fsdp','rep'}, use_global_device_ids=true, to_apply=%region_17.18 | all-reduce | flops 4 | bytes 32 | tf_op jit(solution)/shard_map/psum | solution.py:354
  616.0 13.0 fusion.62
  630.3 84.6 %reduce-scatter.9.cloned.1.call-done = f32[128,768]{1,0:T(8,128)} async-done(((f32[2048,768]{1,0:T(8,128)}), f32[128,768]{1,0:T(8,128)}) %reduce-scatter.9.cloned.1.call-update) | async-done | bytes 393232 | tf_op jit(solution)/shard_map/reduce_scatter | solution.py:361
  724.2 9.4 convert_reduce_fusion
  740.9 8.8 fusion.138
  776.1 20.1 fusion.127
  796.2 20.3 fusion.130
  816.5 20.8 convert_reduce_fusion.5
  837.3 20.3 add_convert_fusion.3
  898.5 29.9 %broadcast_in_dim.201 = f32[30720,768]{1,0:T(8,128)} broadcast(f32[]{:T(128)} %constant.308.clone.1), dimensions={} | broadcast | bytes 94371840 | tf_op jit(solution)/shard_map/broadcast_in_dim | solution.py:377
  928.4 83.9 %scatter_fusion = f32[30720,768]{1,0:T(8,128)} fusion(f32[30720,768]{1,0:T(8,128)} %broadcast_in_dim.201, s32[640]{0:T(1024)S(1)} %copy-done.70, f32[640,768]{1,0:T(8,128)S(1)} %maximum_select_fusion), kind=kCustom, calls=%fused_computation.3 | custom fusion | flops 491520 | bytes 5900800 | tf_op jit(solution)/shard_map/scatter-add | solution.py:377
  1018.1 130.1 %reduce-scatter.13.cloned.1.call-done = f32[7,48,768]{2,1,0:T(8,128)} async-done(((f32[7,768,768]{2,1,0:T(8,128)}), f32[7,48,768]{2,1,0:T(8,128)}) %reduce-scatter.13.cloned.1.call-update) | async-done | bytes 1032208 | tf_op jit(solution)/shard_map/reduce_scatter | solution.py:387
  1150.2 857.0 %reduce-scatter.11.cloned.1.call-done = f32[1920,768]{1,0:T(8,128)} async-done(((f32[30720,768]{1,0:T(8,128)}), f32[1920,768]{1,0:T(8,128)}) %reduce-scatter.11.cloned.1.call-update) | async-done | bytes 5898256 | tf_op jit(solution)/shard_map/reduce_scatter | solution.py:376
  2007.2 12.9 add_convert_fusion.1
  2022.0 59.5 %all-reduce.2 = bf16[3072]{0:T(1024)(128)(2,1)S(1)} all-reduce(f32[3072]{0:T(1024)S(1)} %copy-done.78), channel_id=10, replica_groups=mesh['fsdp'=16,'rep'=2] {'fsdp'}, use_global_device_ids=true, to_apply=%region_55.56.clone | all-reduce | flops 3072 | bytes 18432
  2088.8 86.3 %all-reduce.8.cloned.1.call-done = (bf16[1920,768]{1,0:T(8,128)(2,1)}, bf16[7,48,768]{2,1,0:T(8,128)(2,1)}, bf16[48,3072]{1,0:T(8,128)(2,1)}, bf16[192,768]{1,0:T(8,128)(2,1)}) async-done(((bf16[1920,768]{1,0:T(8,128)(2,1)}, bf16[7,48,768]{2,1,0:T(8,128)(2,1)}, bf16[48,3072]{1,0:T(8,128)(2,1)}, bf16[192,768]{1,0:T(8,128)(2,1)}), (bf16[1920,768]{1,0:T(8,128)(2,1)}, bf16[7,48,768]{2,1,0:T(8,128)(2,1)}, ...) | async-done | bytes 4055056 | tf_op jit(solution)/shard_map/psum | solution.py:394
  2187.8 33.4 %psum.98 = f32[12]{0:T(128)S(1)} all-reduce(f32[12]{0:T(128)S(1)} %concatenate.67), channel_id=1, replica_groups=mesh['fsdp'=16,'rep'=2] {'fsdp'}, use_global_device_ids=true, to_apply=%region_58.59 | all-reduce | flops 12 | bytes 96 | tf_op jit(solution)/shard_map/psum | solution.py:425
  2237.2 58.2 %all-reduce.3 = (f32[1,768]{1,0:T(1,128)S(1)}, f32[10]{0:T(128)S(1)}, f32[7,768]{1,0:T(8,128)S(1)}, f32[1,3072]{1,0:T(1,128)S(1)}, f32[1,768]{1,0:T(1,128)S(1)}) all-reduce(f32[1,768]{1,0:T(1,128)S(1)} %reduce_sum.595, f32[10]{0:T(128)S(1)} %pad_maximum_fusion.1, ...), channel_id=1, replica_groups=mesh['fsdp'=16,'rep'=2] {'fsdp'}, use_global_device_ids=true, to_apply=%region_62.63 | all-reduce | flops 9994 | bytes 79952 | tf_op jit(solution)/shard_map/psum | solution.py:431
  (441 shorter events, 256.6 us)
Async XLA Ops:
  7.2 81.5 %all-gather.12.cloned.1.call-start = ((), (), s32[]{:S(2)}) async-start(), calls=%async_computation.7 | async-start | bytes 8773632 | tf_op jit(solution)/shard_map/all_gather | solution.py:306
  9.4 312.3 %all-gather.10.cloned.1.call-start = ((), (), s32[]{:S(2)}) async-start(), calls=%async_computation.6 | async-start | bytes 50135040 | tf_op jit(solution)/shard_map/all_gather | solution.py:316
  14.1 366.2 %all-gather.14.cloned.1.call-start = ((), (), s32[]{:S(2)}) async-start(), calls=%async_computation.8 | async-start | bytes 5013504 | tf_op jit(solution)/shard_map/all_gather | solution.py:307
  15.0 417.8 %all-gather.16.cloned.1.call-start = ((), (), s32[]{:S(2)}) async-start(), calls=%async_computation.9 | async-start | bytes 5013504 | tf_op jit(solution)/shard_map/all_gather | solution.py:308
  15.8 474.5 %all-gather.18.cloned.1.call-start = ((), (), s32[]{:S(2)}) async-start(), calls=%async_computation.10 | async-start | bytes 3342336 | tf_op jit(solution)/shard_map/all_gather | solution.py:333
  42.1 335.2 %copy-start.38 = (f32[768]{0:T(1024)}, f32[768]{0:T(1024)S(1)}, u32[]{:S(2)}) copy-start(f32[768]{0:T(1024)S(1)} %get-tuple-element.256) | copy-start | bytes 9220
  42.1 338.3 %copy-start.93 = (f32[768]{0:T(1024)}, f32[768]{0:T(1024)S(1)}, u32[]{:S(2)}) copy-start(f32[768]{0:T(1024)S(1)} %get-tuple-element.249) | copy-start | bytes 9220
  42.1 390.6 %copy-start.72 = (f32[768]{0:T(1024)}, f32[768]{0:T(1024)S(1)}, u32[]{:S(2)}) copy-start(f32[768]{0:T(1024)S(1)} %get-tuple-element.250) | copy-start | bytes 9220
  42.1 397.6 %copy-start.43 = (f32[768]{0:T(1024)}, f32[768]{0:T(1024)S(1)}, u32[]{:S(2)}) copy-start(f32[768]{0:T(1024)S(1)} %get-tuple-element.246) | copy-start | bytes 9220
  75.3 305.1 %copy-start.76 = (f32[3072]{0:T(1024)}, f32[3072]{0:T(1024)S(1)}, u32[]{:S(2)}) copy-start(f32[3072]{0:T(1024)S(1)} %convert_element_type.235) | copy-start | bytes 36868
  75.4 256.6 %copy-start.81 = (pred[640]{0:T(1024)(128)(4,1)}, pred[640]{0:T(1024)(128)(4,1)S(1)}, u32[]{:S(2)}) copy-start(pred[640]{0:T(1024)(128)(4,1)S(1)} %get-tuple-element.329) | copy-start | bytes 1924
  90.8 231.0 %copy-start.23 = (bf16[512,768]{1,0:T(8,128)(2,1)}, bf16[512,768]{1,0:T(8,128)(2,1)S(1)}, u32[]{:S(2)}) copy-start(bf16[512,768]{1,0:T(8,128)(2,1)S(1)} %add_convert_fusion.5) | copy-start | bytes 2359300
  93.4 254.2 %copy-start.17 = (bf16[512,768]{0,1:T(8,128)(2,1)}, bf16[512,768]{0,1:T(8,128)(2,1)S(1)}, u32[]{:S(2)}) copy-start(bf16[512,768]{0,1:T(8,128)(2,1)S(1)} %copy.96) | copy-start | bytes 2359300
  446.2 268.6 %reduce-scatter.9.cloned.1.call-start = ((), (), s32[]{:S(2)}) async-start(), calls=%async_computation.11 | async-start | bytes 6684672 | tf_op jit(solution)/shard_map/reduce_scatter | solution.py:361
  629.0 89.4 %copy-start.44 = (f32[768]{0:T(1024)S(1)}, f32[768]{0:T(1024)}, u32[]{:S(2)}) copy-start(f32[768]{0:T(1024)} %copy-done.43) | copy-start | bytes 9220
  629.0 89.4 %copy-start.46 = (f32[512]{0:T(512)S(1)}, f32[512]{0:T(512)}, u32[]{:S(2)}) copy-start(f32[512]{0:T(512)} %copy-done.45) | copy-start | bytes 6148
  629.0 89.4 %copy-start.53 = (f32[512]{0:T(512)S(1)}, f32[512]{0:T(512)}, u32[]{:S(2)}) copy-start(f32[512]{0:T(512)} %copy-done.52) | copy-start | bytes 6148
  629.0 92.0 %copy-start.61 = (f32[512]{0:T(512)S(1)}, f32[512]{0:T(512)}, u32[]{:S(2)}) copy-start(f32[512]{0:T(512)} %copy-done.60) | copy-start | bytes 6148
  629.0 385.4 %reduce-scatter.15.cloned.1.call-start = ((), (), s32[]{:S(2)}) async-start(), calls=%async_computation.14 | async-start | bytes 10027008 | tf_op jit(solution)/shard_map/reduce_scatter | solution.py:388
  740.8 275.4 %reduce-scatter.17.cloned.1.call-start = ((), (), s32[]{:S(2)}) async-start(), calls=%async_computation.15 | async-start | bytes 10027008 | tf_op jit(solution)/shard_map/reduce_scatter | solution.py:389
  749.7 398.5 %reduce-scatter.13.cloned.1.call-start = ((), (), s32[]{:S(2)}) async-start(), calls=%async_computation.13 | async-start | bytes 17547264 | tf_op jit(solution)/shard_map/reduce_scatter | solution.py:387
  887.4 1119.8 %reduce-scatter.11.cloned.1.call-start = ((), (), s32[]{:S(2)}) async-start(), calls=%async_computation.12 | async-start | bytes 100270080 | tf_op jit(solution)/shard_map/reduce_scatter | solution.py:376
  1012.4 994.8 %copy-start.80 = (f32[2048]{0:T(1024)S(1)}, f32[2048]{0:T(1024)}, u32[]{:S(2)}) copy-start(f32[2048]{0:T(1024)} %copy-done.79) | copy-start | bytes 24580
  1012.4 994.8 %copy-start.88 = (f32[2048]{0:T(1024)S(1)}, f32[2048]{0:T(1024)}, u32[]{:S(2)}) copy-start(f32[2048]{0:T(1024)} %copy-done.87) | copy-start | bytes 24580
  1012.4 1069.2 %reduce-scatter.19.cloned.1.call-start = ((), (), s32[]{:S(2)}) async-start(), calls=%async_computation.16 | async-start | bytes 417792
  1014.4 1160.7 %all-reduce.8.cloned.1.call-start = ((), (), s32[]{:S(2)}) async-start(), calls=%async_computation.17 | async-start | bytes 8110080 | tf_op jit(solution)/shard_map/psum | solution.py:394
  1150.2 870.6 %copy-start.99 = (f32[768]{0:T(1024)S(1)}, f32[768]{0:T(1024)}, u32[]{:S(2)}) copy-start(f32[768]{0:T(1024)} %param.41) | copy-start | bytes 9220
  1150.2 871.2 %copy-start.75 = (f32[3072]{0:T(1024)S(1)}, f32[3072]{0:T(1024)}, u32[]{:S(2)}) copy-start(f32[3072]{0:T(1024)} %param.39) | copy-start | bytes 36868
  1150.2 871.8 %copy-start.78 = (f32[3072]{0:T(1024)S(1)}, f32[3072]{0:T(1024)}, u32[]{:S(2)}) copy-start(f32[3072]{0:T(1024)} %get-tuple-element.304) | copy-start | bytes 36868
  2020.1 167.0 %copy-start.100 = (f32[768]{0:T(1024)S(1)}, f32[768]{0:T(1024)}, u32[]{:S(2)}) copy-start(f32[768]{0:T(1024)} %param.35) | copy-start | bytes 9220
  2087.6 95.0 %copy-start.107 = (bf16[192]{0:T(256)(128)(2,1)}, bf16[192]{0:T(256)(128)(2,1)S(1)}, u32[]{:S(2)}) copy-start(bf16[192]{0:T(256)(128)(2,1)S(1)} %get-tuple-element.279) | copy-start | bytes 1156
  2233.4 83.6 %copy-start.64 = (f32[7,48]{1,0:T(8,128)}, f32[7,48]{1,0:T(8,128)S(1)}, u32[]{:S(2)}) copy-start(f32[7,48]{1,0:T(8,128)S(1)} %get-tuple-element.295) | copy-start | bytes 4036
  (91 other events, 1437.2 us)
Sparse Core Ops, SparseCore 0:
  10.9 77.7 all-gather.11
  90.8 230.8 all-gather.9
  324.6 53.3 all-gather.13
  380.8 51.9 all-gather.15
  446.3 43.9 all-gather.17
  629.1 85.6 reduce-scatter.8
  741.0 110.6 reduce-scatter.14
  855.8 111.1 reduce-scatter.16
  971.8 176.2 reduce-scatter.12
  1152.2 854.9 reduce-scatter.10
  2011.3 54.7 reduce-scatter.18
  2069.9 105.0 all-reduce.7
where the time goes:
time: 2340 us; the launch traced here: 2330 us
  waiting for transfers between devices  1450 us (62%)
  blocking collectives  310 us (13%)
  matrix products  271 us (12%)
  other arithmetic  188 us (8%)
  local copies, waits for them, and re-layouts  85.5 us (4%)
    reduce_scatter x1, waiting for transfers between devices, body(): lax.psum_scatter(jax.ops.segment_sum(jnp.where(inside[:, None], lookup_te...  857 us
    all_gather x1, waiting for transfers between devices, body(): piece = lax.all_gather(table_low, 'fsdp', axis=0, tiled=True)  225 us
    reduce_scatter x1, waiting for transfers between devices, body(): lax.psum_scatter(grad_mats, 'fsdp', scatter_dimension=1, tiled=True)  130 us
    unnamed x2, blocking collectives  91.1 us
    psum x1, waiting for transfers between devices, body(): lax.psum(table_part.astype(jnp.bfloat16), 'rep').astype(jnp.float32)  86.3 us
    reduce_scatter x1, waiting for transfers between devices, body(): lax.psum_scatter(product(grad_logits, table_low), 'fsdp', scatter_dimensi...  84.6 us
    scatter-add x1, other arithmetic, body(): jax.ops.segment_sum(jnp.where(inside[:, None], lookup_terms, 0.0), jnp.wh...  83.9 us
    psum x1, blocking collectives, body(): lax.psum((local_cols[0], local_cols[1], local_cols[2], local_cols[3], row...  58.2 us
  transfers between devices with their start and end apart: 12, of which 8 were waited for; matrix products, arithmetic and copies ran while one was open for 17% of the time, Pallas kernels for 0%

commit v1 on v0

v1 whole, which is shorter than its diff:
```python
from functools import partial
import math
from typing import NamedTuple

import jax
import jax.numpy as jnp
from jax import lax
from jax.experimental import pallas as pl
from jax.experimental.pallas import tpu as pltpu
from jax.sharding import PartitionSpec as P

HEAD_DIM = 64
PAGE_LEN = 512
M_TOK = 64
M_AREA = 64
STEP = 10


EPSILON = 1e-05
CLIP_NORM = 0.1
LEARN_RATE = 0.02
VECTOR_RATE = 0.3
TINY_TERM = 1e-30
NEGATIVE = -1e30
BFLOAT = jnp.bfloat16
FLOAT = jnp.float32
LANES = 128
DECAY = 1.0 - STEP ** (-0.8)


class Line(NamedTuple):
    axis: str
    total: int
    stride: int
    count: int


def lines_of(groups, copies):
    cores = min(2, groups)
    rest = (groups // cores).bit_length() - 1
    y_count = 1 << (rest // 2)
    z_count = groups // (cores * y_count)
    return {
        "z": Line("fsdp", groups, cores * y_count, z_count),
        "y": Line("fsdp", groups, cores, y_count),
        "core": Line("fsdp", groups, 1, cores),
        "x": Line("rep", copies, 1, copies),
    }


def place_on(line):
    return lax.axis_index(line.axis) // line.stride % line.count


def hop(value, line, step, senders):
    pairs = [
        (i, i + step * line.stride)
        for i in range(line.total)
        if i // line.stride % line.count in senders
    ]
    return lax.ppermute(value, line.axis, pairs)


def swap(value, line):
    pairs = [
        (i, i + line.stride if i // line.stride % 2 == 0 else i - line.stride)
        for i in range(line.total)
    ]
    return lax.ppermute(value, line.axis, pairs)


def gather_line(value, line, axis):
    count = line.count
    if count == 1:
        return value
    here = place_on(line)
    if count == 2:
        other = swap(value, line)
        first = jnp.where(here == 0, value, other)
        second = jnp.where(here == 0, other, value)
        return jnp.concatenate([first, second], axis=axis)
    lower, upper = [value], [value]
    for step in range(1, count):
        lower.append(hop(lower[-1], line, 1, range(step - 1, count - 1)))
        upper.append(hop(upper[-1], line, -1, range(1, count - step + 1)))
    blocks = []
    for place in range(count):
        choices = [upper[place - i] if i <= place else lower[i - place] for i in range(count)]
        blocks.append(lax.select_n(here, *choices))
    return jnp.concatenate(blocks, axis=axis)


def reduce_line(value, line, axis):
    count = line.count
    if count == 1:
        return value.astype(FLOAT)
    here = place_on(line)
    size = value.shape[axis] // count

    def block(place):
        return lax.dynamic_slice_in_dim(value, place * size, size, axis)

    if count == 2:
        return block(here).astype(FLOAT) + swap(block(1 - here).astype(BFLOAT), line).astype(FLOAT)
    lower = upper = None
    for step in range(count - 1):
        to_upper = block(jnp.minimum(here + count - 1 - step, count - 1)).astype(FLOAT)
        to_lower = block(jnp.maximum(here - (count - 1 - step), 0)).astype(FLOAT)
        if lower is not None:
            to_upper = to_upper + lower
            to_lower = to_lower + upper
        lower = hop(to_upper.astype(BFLOAT), line, 1, range(0, step + 1)).astype(FLOAT)
        upper = hop(to_lower.astype(BFLOAT), line, -1, range(count - 1 - step, count)).astype(FLOAT)
    return block(here).astype(FLOAT) + (lower + upper)


def paired(value, axis, combine):
    size = lax.axis_size(axis)
    bit = 1
    while bit < size:
        pairs = [(i, i ^ bit) for i in range(size)]
        value = combine(value, jax.tree.map(lambda v: lax.ppermute(v, axis, pairs), value))
        bit *= 2
    return value


def gather_weight(value, lines, order):
    x = lines["x"]
    part = value.shape[2] // x.count
    piece = lax.dynamic_slice_in_dim(value, place_on(x) * part, part, 2)
    piece = piece[:, None, None, None]
    axes = {"z": 1, "y": 2, "core": 3, "x": 5}
    for name in order:
        piece = gather_line(piece, lines[name], axes[name])
    count, rows, columns = value.shape
    return piece.reshape(count, -1, columns)


def reduce_weight(value, lines, order):
    count, _, columns = value.shape
    z, y, core = lines["z"].count, lines["y"].count, lines["core"].count
    piece = value.reshape(count, z, y, core, -1, columns)
    axes = {"z": 1, "y": 2, "core": 3, "x": 5}
    for name in order:
        piece = reduce_line(piece, lines[name], axes[name]).astype(BFLOAT)
    return gather_line(piece[:, 0, 0, 0], lines["x"], 2).astype(FLOAT)


def layer_norm(value, gain, shift):
    center = value - jnp.mean(value, axis=-1, keepdims=True)
    spread = jnp.mean(center * center, axis=-1, keepdims=True)
    return center * lax.rsqrt(spread + EPSILON) * gain + shift


def box_features(boxes, width):
    count = width // 8
    freqs = jnp.exp(-math.log(10000.0) * jnp.arange(count, dtype=FLOAT) / count)
    angle = boxes.astype(FLOAT)[:, :, None] * freqs[None, None, :]
    waves = jnp.concatenate([jnp.sin(angle), jnp.cos(angle)], axis=2)
    return jnp.transpose(waves, (1, 0, 2)).reshape(boxes.shape[1], width)


def valid_slots(lengths, slot_count):
    n_tok = jnp.minimum(M_TOK, 1 + lengths * M_TOK // PAGE_LEN)
    n_area = jnp.minimum(M_AREA, 1 + lengths * (3 * M_AREA) // (4 * PAGE_LEN))
    index = jnp.arange(slot_count, dtype=jnp.int32)[None, :]
    return jnp.where(index < M_TOK, index < n_tok[:, None], index - M_TOK < n_area[:, None])


def product(left, right):
    return jnp.dot(left, right, preferred_element_type=FLOAT)


def contract_rows(left, right):
    return lax.dot_general(left, right, (((0,), (0,)), ((), ())), preferred_element_type=FLOAT)


def times_transposed(left, right):
    return lax.dot_general(left, right, (((1,), (1,)), ((), ())), preferred_element_type=FLOAT)


def two_parts(value):
    high = value.astype(BFLOAT)
    return high, (value - high.astype(FLOAT)).astype(BFLOAT)


def side(index):
    lane = lax.broadcasted_iota(jnp.int32, (1, LANES), 1)
    return lane // HEAD_DIM == index


def only(mask, value):
    return jnp.where(mask, value, jnp.zeros_like(value))


def attend_kernel(length_ref, query_ref, key_ref, value_ref, box_query_ref, box_key_ref, out_ref):
    length = length_ref[pl.program_id(0)]
    query, key, box_query, box_key = query_ref[...], key_ref[...], box_query_ref[...], box_key_ref[...]
    keys = jnp.concatenate([key, box_key, key], axis=1)
    keep = lax.broadcasted_iota(jnp.int32, (1, key.shape[0]), 1) < length
    mixed = jnp.zeros(out_ref.shape, FLOAT)
    for head in range(LANES // HEAD_DIM):
        mask = side(head)
        own = only(mask, query)
        score = times_transposed(jnp.concatenate([own, own, only(mask, box_query)], axis=1), keys)
        score = jnp.where(keep, score * HEAD_DIM ** (-0.5), NEGATIVE)
        expo = jnp.exp(score - jnp.max(score, axis=1, keepdims=True))
        prob = (expo * (1.0 / jnp.sum(expo, axis=1, keepdims=True))).astype(BFLOAT)
        mixed = jnp.where(mask, product(prob, value_ref[...]), mixed)
    out_ref[...] = mixed.astype(BFLOAT)


def attend_back_kernel(
    length_ref,
    query_ref,
    key_ref,
    value_ref,
    box_query_ref,
    box_key_ref,
    grad_ref,
    grad_query_ref,
    grad_key_ref,
    grad_value_ref,
    grad_box_query_ref,
    grad_box_key_ref,
):
    length = length_ref[pl.program_id(0)]
    query, key, value, box_query, box_key = (
        query_ref[...],
        key_ref[...],
        value_ref[...],
        box_query_ref[...],
        box_key_ref[...],
    )
    grad = grad_ref[...]
    rows = key.shape[0]
    keys = jnp.concatenate([key, box_key, key], axis=1)
    both_queries = jnp.concatenate([query, box_query], axis=1)
    both_keys = jnp.concatenate([key, box_key], axis=1)
    keep = lax.broadcasted_iota(jnp.int32, (rows, 1), 0) < length
    outs = [jnp.zeros((rows, LANES), FLOAT) for _ in range(5)]
    for head in range(LANES // HEAD_DIM):
        mask = side(head)
        own = only(mask, query)
        score = times_transposed(keys, jnp.concatenate([own, own, only(mask, box_query)], axis=1))
        score = jnp.where(keep, score * HEAD_DIM ** (-0.5), NEGATIVE)
        expo = jnp.exp(score - jnp.max(score, axis=0, keepdims=True))
        prob = expo * (1.0 / jnp.sum(expo, axis=0, keepdims=True))
        grad_value = product(prob.astype(BFLOAT), grad)
        grad_prob = times_transposed(only(mask, value), grad)
        grad_score = prob * (grad_prob - jnp.sum(prob * grad_prob, axis=0, keepdims=True))
        low = grad_score.astype(BFLOAT) * jnp.asarray(HEAD_DIM ** (-0.5), BFLOAT)
        with_queries = product(low, both_queries)
        with_keys = contract_rows(low, both_keys)
        fresh = (
            with_keys[:, :LANES] + with_keys[:, LANES:],
            with_queries[:, :LANES] + with_queries[:, LANES:],
            grad_value,
            with_keys[:, :LANES],
            with_queries[:, :LANES],
        )
        outs = [jnp.where(mask, new, old) for new, old in zip(fresh, outs)]
    for ref, out in zip(
        (grad_query_ref, grad_key_ref, grad_value_ref, grad_box_query_ref, grad_box_key_ref), outs
    ):
        ref[...] = out.astype(BFLOAT)


def attention_call(kernel, lengths, arrays, out_count):
    tokens, width = arrays[0].shape
    pages = lengths.shape[0]
    spec = pl.BlockSpec((tokens // pages, LANES), lambda page, pair: (page, pair))
    out = jax.ShapeDtypeStruct((tokens, width), BFLOAT)
    return pl.pallas_call(
        kernel,
        grid=(pages, width // LANES),
        in_specs=[pl.BlockSpec(memory_space=pltpu.SMEM)] + [spec] * len(arrays),
        out_specs=[spec] * out_count,
        out_shape=[out] * out_count,
        compiler_params=pltpu.CompilerParams(vmem_limit_bytes=48 * 1024 * 1024),
    )(lengths, *arrays)


class Buckets(NamedTuple):
    owner: jax.Array
    row: jax.Array
    first: jax.Array
    rank: jax.Array
    fullest: jax.Array


def bucket_ids(ids, shard_rows):
    owner, row = ids // shard_rows, ids % shard_rows
    index = jnp.arange(ids.shape[0], dtype=jnp.int32)
    earlier = index[None, :] < index[:, None]
    same = ids[:, None] == ids[None, :]
    first = ~jnp.any(same & earlier, axis=1)
    before = (owner[:, None] == owner[None, :]) & earlier & first[None, :]
    rank = jnp.sum(before.astype(jnp.int32), axis=1)
    rank = jnp.sum(jnp.where(same & first[None, :], rank[None, :], 0), axis=1)
    return Buckets(owner, row, first, rank, jnp.max(rank) + 1)


def bucket_places(buckets, capacity, turn):
    shifted = buckets.rank - turn * capacity
    inside = (shifted >= 0) & (shifted < capacity)
    return jnp.where(inside, buckets.owner * capacity + shifted, -1)


def bucket_requests(buckets, places, groups, capacity):
    hit = (places[:, None] == jnp.arange(groups * capacity)[None, :]) & buckets.first[:, None]
    return jnp.sum(jnp.where(hit, buckets.row[:, None], 0), axis=0).reshape(groups, capacity)


def one_hot(index, count):
    return (index[:, None] == jnp.arange(count, dtype=jnp.int32)[None, :]).astype(BFLOAT)


def layer_forward(weights, embedded, place, box_query, box_key, lengths):
    mats, up, down, gains, up_bias = weights
    start_state = layer_norm(embedded, gains[0], gains[1])
    act = start_state.astype(BFLOAT)
    query = (product(act, mats[1]) + gains[6]).astype(BFLOAT)
    keys = product(act, mats[2]).astype(BFLOAT)
    values = (product(act, mats[3]) + gains[7]).astype(BFLOAT)
    (mixed,) = attention_call(attend_kernel, lengths, (query, keys, values, box_query, box_key), 1)
    first_sum = start_state + (product(mixed, mats[6]) + gains[8])
    middle = layer_norm(first_sum, gains[2], gains[3])
    middle_low = middle.astype(BFLOAT)
    upper = product(middle_low, up) + up_bias
    active = jax.nn.gelu(upper, approximate=False).astype(BFLOAT)
    second_sum = middle + (product(active, down) + gains[10])
    kept = (
        embedded,
        act,
        place,
        query,
        keys,
        values,
        box_query,
        box_key,
        mixed,
        first_sum,
        middle_low,
        upper,
        active,
        second_sum,
    )
    return (layer_norm(second_sum, gains[4], gains[5]), kept)


def layer_backward(weights, features_low, lengths, kept, grad_out, lines):
    mats, up, down, gains, up_bias = weights
    (
        embedded,
        act,
        place,
        query,
        keys,
        values,
        box_query,
        box_key,
        mixed,
        first_sum,
        middle_low,
        upper,
        active,
        second_sum,
    ) = kept

    def column_sum(value):
        return jnp.sum(value.astype(FLOAT), axis=0)

    grad_second, gain_four, gain_five = jax.vjp(layer_norm, second_sum, gains[4], gains[5])[1](
        grad_out
    )
    order = ("core", "y", "z", "x")
    grad_feed = grad_second.astype(BFLOAT)
    grad_down = reduce_weight(contract_rows(active, grad_feed)[None], lines, order)
    grad_active = times_transposed(grad_feed, down)
    grad_upper = jax.vjp(partial(jax.nn.gelu, approximate=False), upper)[1](grad_active)[0].astype(
        BFLOAT
    )
    grad_up = reduce_weight(contract_rows(middle_low, grad_upper)[None], lines, order)
    grad_middle = grad_second + times_transposed(grad_upper, up)
    grad_first, gain_two, gain_three = jax.vjp(layer_norm, first_sum, gains[2], gains[3])[1](
        grad_middle
    )
    grad_attended = grad_first.astype(BFLOAT)
    grad_output = contract_rows(mixed, grad_attended)
    grad_mixed = times_transposed(grad_attended, mats[6]).astype(BFLOAT)
    grad_query, grad_keys, grad_values, grad_box_query, grad_box_key = attention_call(
        attend_back_kernel, lengths, (query, keys, values, box_query, box_key, grad_mixed), 5
    )
    grad_place = (
        times_transposed(grad_box_query, mats[4]) + times_transposed(grad_box_key, mats[5])
    ).astype(BFLOAT)
    grad_start = (
        grad_first + times_transposed(grad_query, mats[1]) + times_transposed(grad_keys, mats[2])
    )
    grad_start = grad_start + times_transposed(grad_values, mats[3])
    grad_embedded, gain_zero, gain_one = jax.vjp(layer_norm, embedded, gains[0], gains[1])[1](
        grad_start
    )
    grad_mats = jnp.stack(
        [
            contract_rows(features_low, grad_place),
            contract_rows(act, grad_query),
            contract_rows(act, grad_keys),
            contract_rows(act, grad_values),
            contract_rows(place, grad_box_query),
            contract_rows(place, grad_box_key),
            grad_output,
        ]
    )
    grad_mats = reduce_weight(grad_mats, lines, order)
    grad_vectors = jnp.stack(
        [
            gain_zero,
            gain_one,
            gain_two,
            gain_three,
            gain_four,
            gain_five,
            column_sum(grad_query),
            column_sum(grad_values),
            column_sum(grad_attended),
            column_sum(grad_place),
            column_sum(grad_feed),
        ]
    )
    layer_grads = (grad_mats, grad_up[0], grad_down[0], grad_vectors, column_sum(grad_upper))
    return (layer_grads, grad_embedded)


def combine_mass(first, second):
    peak = jnp.maximum(first[0], second[0])
    mass = first[1] * jnp.exp(first[0] - peak) + second[1] * jnp.exp(second[0] - peak)
    return (peak, mass, first[2] + second[2])


def add_trees(first, second):
    return jax.tree.map(jnp.add, first, second)


def body(
    token_ids,
    boxes,
    lengths,
    slots,
    labels,
    table,
    mats,
    up,
    down,
    vectors,
    up_bias,
    table_rows,
    table_cols,
    mats_rows,
    mats_cols,
    up_rows,
    up_cols,
    down_rows,
    down_cols,
    vectors_second,
    up_bias_second,
):
    pages = lengths.shape[0]
    tokens = token_ids.shape[0]
    page_len = tokens // pages
    width = table.shape[1]
    shard_rows = table.shape[0]
    slot_count = slots.shape[1]
    groups, copies = lax.axis_size("fsdp"), lax.axis_size("rep")
    group, copy = lax.axis_index("fsdp"), lax.axis_index("rep")
    lines = lines_of(groups, copies)
    depth = mats.shape[0]
    table_low = table.astype(BFLOAT)

    capacity = 16 + -(-tokens // (16 * groups)) * 16
    buckets = bucket_ids(token_ids, shard_rows)
    places = bucket_places(buckets, capacity, 0)
    requests = bucket_requests(buckets, places, groups, capacity)
    own_news = jnp.concatenate([labels.reshape(-1), lengths, buckets.fullest[None]])
    news = jnp.concatenate(
        [
            jnp.repeat(requests, copies, axis=0),
            jnp.broadcast_to(own_news[None], (groups * copies, own_news.shape[0])),
        ],
        axis=1,
    )
    news = lax.all_to_all(news, ("fsdp", "rep"), 0, 0, tiled=True)
    asked = news[:, :capacity].reshape(groups, copies, capacity)
    asked = jnp.transpose(asked, (1, 0, 2)).reshape(copies, groups * capacity)
    labels_all = news[:, capacity : capacity + pages * slot_count]
    labels_all = labels_all.reshape(groups, copies, pages * slot_count)
    labels_all = lax.dynamic_index_in_dim(labels_all, copy, 1, False).reshape(-1)
    lengths_all = news[:, capacity + pages * slot_count : -1]
    turns = (jnp.max(news[:, -1]) + capacity - 1) // capacity

    def fetch(spots, wanted):
        rows = product(one_hot(wanted, shard_rows), table_low).astype(BFLOAT)
        rows = lax.all_to_all(rows.reshape(groups, capacity, width), "fsdp", 0, 0, tiled=True)
        return product(one_hot(spots, groups * capacity), rows.reshape(groups * capacity, width))

    def ask(turn):
        spots = bucket_places(buckets, capacity, turn)
        wanted = bucket_requests(buckets, spots, groups, capacity)
        return spots, lax.all_to_all(wanted, "fsdp", 0, 0, tiled=True).reshape(-1)

    embedded = fetch(places, lax.dynamic_index_in_dim(asked, copy, 0, False))
    embedded = lax.while_loop(
        lambda state: state[0] < turns,
        lambda state: (state[0] + 1, state[1] + fetch(*ask(state[0]))),
        (jnp.int32(1), embedded),
    )[1]

    mats_low = mats.astype(BFLOAT)
    small = jnp.concatenate([vectors.astype(BFLOAT).reshape(-1), up_bias.astype(BFLOAT)])[None]

    def lay(first, second, bit):
        low = (group & bit) == 0
        return jnp.concatenate([jnp.where(low, first, second), jnp.where(low, second, first)])

    bit = 1
    while bit < groups:
        pairs = [(i, i ^ bit) for i in range(groups)]
        small = lay(small, lax.ppermute(small, "fsdp", pairs), bit)
        bit *= 2
    split = vectors.size
    gains = small[:, :split].reshape(groups, vectors.shape[0], -1)
    gains = jnp.transpose(gains, (1, 0, 2)).reshape(vectors.shape[0], width).astype(FLOAT)
    bias = small[:, split:].reshape(-1).astype(FLOAT)
    box_mats = gather_weight(
        jnp.stack([mats_low[0], mats_low[4], mats_low[5]]), lines, ("z", "x", "y", "core")
    )
    token_mats = gather_weight(mats_low[1:4], lines, ("z", "y", "x", "core"))
    out_mat = gather_weight(mats_low[6:7], lines, ("z", "y", "x", "core"))
    up_low = gather_weight(up.astype(BFLOAT)[None], lines, ("z", "x", "y", "core"))[0]
    down_low = gather_weight(down.astype(BFLOAT)[None], lines, ("z", "y", "x", "core"))[0]
    layer_mats = (
        box_mats[0],
        token_mats[0],
        token_mats[1],
        token_mats[2],
        box_mats[1],
        box_mats[2],
        out_mat[0],
    )
    weights = (layer_mats, up_low, down_low, gains, bias)

    features_low = box_features(boxes, width).astype(BFLOAT)
    place = (product(features_low, layer_mats[0]) + gains[9]).astype(BFLOAT)
    box_query = product(place, layer_mats[4]).astype(BFLOAT)
    box_key = product(place, layer_mats[5]).astype(BFLOAT)
    top_state, kept = layer_forward(weights, embedded, place, box_query, box_key, lengths)

    where_at = slots * lengths[:, None] // 256 + jnp.arange(pages)[:, None] * page_len
    pick = one_hot(where_at.reshape(-1), tokens)
    rows_low = product(pick, top_state.astype(BFLOAT)).astype(BFLOAT)
    rows_all = rows_low[None, None, None]
    for axis, name in enumerate(("z", "y", "core")):
        rows_all = gather_line(rows_all, lines[name], axis)
    rows_all = rows_all.reshape(-1, width)
    logits = times_transposed(rows_all, table_low)
    mine = labels_all[:, None] - group * shard_rows == jnp.arange(shard_rows)[None, :]
    peak = jnp.max(logits, axis=1)
    mass = jnp.sum(jnp.exp(logits - peak[:, None]), axis=1)
    target = jnp.sum(jnp.where(mine, logits, 0.0), axis=1)
    peak, mass, target = paired((peak, mass, target), "fsdp", combine_mass)
    log_total = peak + jnp.log(mass)

    is_token = jnp.arange(slot_count) < M_TOK
    valid_all = valid_slots(lengths_all.reshape(-1), slot_count).astype(FLOAT)
    count_token = jnp.sum(jnp.where(is_token, valid_all, 0.0))
    count_area = jnp.sum(jnp.where(is_token, 0.0, valid_all))
    valid = valid_all.reshape(groups, copies, pages, slot_count)
    valid = lax.dynamic_index_in_dim(valid, copy, 1, False).reshape(-1, slot_count)
    loss_rows = (log_total - target).reshape(-1, slot_count) * valid
    sums = jnp.stack(
        [jnp.sum(jnp.where(is_token, loss_rows, 0.0)), jnp.sum(jnp.where(is_token, 0.0, loss_rows))]
    )
    sums = paired(sums, "rep", jnp.add)
    loss_parts = jnp.stack([sums[0], count_token, sums[1], count_area])
    share = jnp.where(is_token, 1.0 / count_token, 1.0 / count_area)
    weight = (valid * share[None, :]).reshape(-1)
    grad_logits = (jnp.exp(logits - log_total[:, None]) - mine.astype(FLOAT)).astype(BFLOAT)
    grad_rows = product(grad_logits, table_low) * weight[:, None]
    grad_rows = grad_rows.reshape(
        lines["z"].count, lines["y"].count, lines["core"].count, -1, width
    )
    for axis, name in ((2, "core"), (1, "y"), (0, "z")):
        grad_rows = reduce_line(grad_rows.astype(BFLOAT), lines[name], axis)
    grad_rows = grad_rows.reshape(-1, width)
    head_grad = contract_rows(
        grad_logits, (rows_all.astype(FLOAT) * weight[:, None]).astype(BFLOAT)
    ).astype(BFLOAT)
    if copies == 2:
        head_grad = head_grad.astype(FLOAT) + swap(head_grad, lines["x"]).astype(FLOAT)
    else:
        head_grad = lax.psum(head_grad, "rep").astype(FLOAT)
    grad_top = sum(contract_rows(pick, part) for part in two_parts(grad_rows))

    layer_grads, grad_embedded = layer_backward(
        weights, features_low, lengths, kept, grad_top, lines
    )
    mats_grad, up_grad, down_grad, vectors_sum, bias_sum = layer_grads
    vectors_sum, bias_sum = paired(
        paired((vectors_sum, bias_sum), "fsdp", add_trees), "rep", add_trees
    )
    vectors_grad = lax.dynamic_slice_in_dim(
        vectors_sum, group * vectors.shape[1], vectors.shape[1], 1
    )
    bias_grad = lax.dynamic_slice_in_dim(bias_sum, group * up_bias.shape[0], up_bias.shape[0], 0)

    embedded_parts = two_parts(grad_embedded)

    def give(spots):
        spread = one_hot(spots, groups * capacity)
        rows = sum(contract_rows(spread, part) for part in embedded_parts).astype(BFLOAT)
        rows = lax.all_to_all(rows.reshape(groups, capacity, width), "fsdp", 0, 0, tiled=True)
        return gather_line(rows.reshape(1, groups * capacity, width), lines["x"], 0)

    def spread_rows(wanted, rows):
        return contract_rows(
            one_hot(wanted.reshape(-1), shard_rows), rows.reshape(-1, width)
        )

    table_grad = head_grad + spread_rows(asked, give(places))

    def another(state):
        turn, total = state
        spots, wanted = ask(turn)
        wanted = gather_line(wanted[None], lines["x"], 0)
        return turn + 1, total + spread_rows(wanted, give(spots))

    table_grad = lax.while_loop(lambda state: state[0] < turns, another, (jnp.int32(1), table_grad))[1]

    items = (
        (table_grad[None], table[None], table_rows[None], table_cols[None]),
        (mats_grad, mats, mats_rows, mats_cols),
        (up_grad[None], up[None], up_rows[None], up_cols[None]),
        (down_grad[None], down[None], down_rows[None], down_cols[None]),
    )
    row_squares = [jnp.sum(item[0] * item[0], axis=2) for item in items]
    col_squares = [jnp.sum(item[0] * item[0], axis=1) for item in items]
    sums = jnp.concatenate(
        [value.reshape(-1) for value in col_squares]
        + [jnp.sum(item[2], axis=1) for item in items]
        + [jnp.stack([jnp.sum(vectors_grad * vectors_grad), jnp.sum(bias_grad * bias_grad)])]
    )
    length = sums.shape[0]
    padded = -(-length // (8 * LANES)) * 8 * LANES
    sums = jnp.pad(sums, (0, padded - length)).reshape(-1, LANES)
    sums = paired(sums, "fsdp", jnp.add).reshape(-1)[:length]
    col_totals, row_totals, offset = [], [], 0
    for value in col_squares:
        col_totals.append(sums[offset : offset + value.size].reshape(value.shape))
        offset += value.size
    for value in col_squares:
        row_totals.append(sums[offset : offset + value.shape[0]])
        offset += value.shape[0]
    square_totals = [jnp.sum(value, axis=1) for value in col_totals]
    grad_norm = jnp.sqrt(sum(jnp.sum(value) for value in square_totals) + jnp.sum(sums[offset:]))
    clip = jnp.minimum(1.0, CLIP_NORM / grad_norm)
    results = []
    for item, row_square, col_total, row_total, square_total in zip(
        items, row_squares, col_totals, row_totals, square_totals
    ):
        grad, param, rows_old, cols_old = item
        rows_count, cols_count = grad.shape[1] * groups, grad.shape[2]

        def renewed(old, square):
            return DECAY * old + (1.0 - DECAY) * (square + TINY_TERM)

        square = clip * clip
        rows_new = renewed(rows_old, square * row_square / cols_count)
        cols_new = renewed(cols_old, square * col_total / rows_count)
        mean = renewed(row_total / rows_count, square * square_total / (rows_count * cols_count))
        clipped = grad * clip
        second = rows_new[:, :, None] * cols_new[:, None, :] / mean[:, None, None]
        results.append((clipped, rows_new, cols_new, param - LEARN_RATE * clipped * lax.rsqrt(second)))
    clipped_vectors = vectors_grad * clip
    vectors_second_new = DECAY * vectors_second + (1.0 - DECAY) * (
        clipped_vectors * clipped_vectors + TINY_TERM
    )
    vectors_new = vectors - VECTOR_RATE * clipped_vectors * lax.rsqrt(vectors_second_new)
    clipped_bias = bias_grad * clip
    bias_second_new = DECAY * up_bias_second + (1.0 - DECAY) * (
        clipped_bias * clipped_bias + TINY_TERM
    )
    bias_new = up_bias - VECTOR_RATE * clipped_bias * lax.rsqrt(bias_second_new)
    table_out, mats_out, up_out, down_out = results
    return (
        table_out[0][0],
        table_out[1][0],
        table_out[2][0],
        table_out[3][0],
        mats_out[0],
        mats_out[1],
        mats_out[2],
        mats_out[3],
        up_out[0][0],
        up_out[1][0],
        up_out[2][0],
        up_out[3][0],
        down_out[0][0],
        down_out[1][0],
        down_out[2][0],
        down_out[3][0],
        clipped_vectors,
        vectors_second_new,
        vectors_new,
        clipped_bias,
        bias_second_new,
        bias_new,
        grad_norm,
        loss_parts,
    )


def solution(mesh):
    return jax.shard_map(
        body,
        mesh=mesh,
        in_specs=(
            P(("fsdp", "rep")),
            P(None, ("fsdp", "rep")),
            P(("fsdp", "rep")),
            P(("fsdp", "rep"), None),
            P(("fsdp", "rep"), None),
            P("fsdp", None),
            P(None, "fsdp", None),
            P("fsdp", None),
            P("fsdp", None),
            P(None, "fsdp"),
            P("fsdp"),
            P("fsdp"),
            P(),
            P(None, "fsdp"),
            P(),
            P("fsdp"),
            P(),
            P("fsdp"),
            P(),
            P(None, "fsdp"),
            P("fsdp"),
        ),
        out_specs=(
            P("fsdp", None),
            P("fsdp"),
            P(),
            P("fsdp", None),
            P(None, "fsdp", None),
            P(None, "fsdp"),
            P(),
            P(None, "fsdp", None),
            P("fsdp", None),
            P("fsdp"),
            P(),
            P("fsdp", None),
            P("fsdp", None),
            P("fsdp"),
            P(),
            P("fsdp", None),
            P(None, "fsdp"),
            P(None, "fsdp"),
            P(None, "fsdp"),
            P("fsdp"),
            P("fsdp"),
            P("fsdp"),
            P(),
            P(),
        ),
        check_vma=False,
    )
```

time: 2340 us -> 826 us (0.35)
  waiting for transfers between devices: 1450 us -> 237 us
  blocking collectives: 310 us -> 0 us
  starting transfers between devices: 0.75 us -> 211 us
  matrix products: 271 us -> 110 us
  other arithmetic: 188 us -> 123 us
  Pallas kernels: 0 us -> 30.2 us
    reduce_scatter x5 -> x0, waiting for transfers between devices: 1070 us -> none  [the longest x1 857 us: body(): lax.psum_scatter(jax.ops.segment_sum(jnp.where(inside[:, None], lookup_te...]
    all_gather x5 -> x0, waiting for transfers between devices: 291 us -> none  [the longest x1 225 us: body(): piece = lax.all_gather(table_low, 'fsdp', axis=0, tiled=True)]
    ppermute x0 -> x124, waiting for transfers between devices: none -> 237 us  [the longest x33 153 us: swap(): return lax.ppermute(value, line.axis, pairs)]
    ppermute x0 -> x124, starting transfers between devices: none -> 193 us  [the longest x60 118 us: hop(): return lax.ppermute(value, line.axis, pairs)]
    psum x4 -> x0, blocking collectives: 135 us -> none  [the longest x1 58.2 us: body(): lax.psum((local_cols[0], local_cols[1], local_cols[2], local_cols[3], row...]
    dot_general x10 -> x0, matrix products: 126 us -> none  [the longest x1 20.8 us: attend_back(): jnp.einsum('hqk,khe->qhe', grad_low, box_key, preferred_element_type=FLOAT)]
    unnamed x2 -> x0, blocking collectives: 91.1 us -> none
    scatter-add x2 -> x0, other arithmetic: 87.5 us -> none  [the longest x1 83.9 us: body(): jax.ops.segment_sum(jnp.where(inside[:, None], lookup_terms, 0.0), jnp.wh...]
  transfers between devices with their start and end apart: 12 -> 127, of which waited for: 8 -> 45; matrix products, arithmetic and copies ran while one was open for 17% -> 26% of each run, Pallas kernels for 0% -> 4%
where the time goes in v1:
time: 826 us; the launch traced here: 814 us
  waiting for transfers between devices  237 us (29%)
  starting transfers between devices  211 us (26%)
  other arithmetic  123 us (15%)
  matrix products  110 us (13%)
  local copies, waits for them, and re-layouts  85.8 us (10%)
  Pallas kernels  30.2 us (4%)
  between operations  16.7 us (2%)
    ppermute x33, waiting for transfers between devices, swap(): return lax.ppermute(value, line.axis, pairs)  153 us
    ppermute x60, starting transfers between devices, hop(): return lax.ppermute(value, line.axis, pairs)  118 us
    ppermute x60, waiting for transfers between devices, hop(): return lax.ppermute(value, line.axis, pairs)  66.3 us
    dot_general x13, matrix products, product(): return jnp.dot(left, right, preferred_element_type=FLOAT)  45.5 us
    ppermute x27, starting transfers between devices, paired(): lax.ppermute(v, axis, pairs)  41.4 us
    dot_general x15, matrix products, contract_rows(): lax.dot_general(left, right, (((0,), (0,)), ((), ())), preferred_element_...  39.6 us
    unnamed x348, local copies, waits for them, and re-layouts  37.9 us
    pallas_call x2, Pallas kernels, attention_call(): pl.pallas_call(kernel, grid=(pages, width // LANES), in_specs=[pl.BlockSp...  30.2 us
  transfers between devices with their start and end apart: 127, of which 45 were waited for; matrix products, arithmetic and copies ran while one was open for 26% of the time, Pallas kernels for 4%

profile of v1, /device:TPU:0, one launch (start us, length us, event | category | flops | bytes accessed | tf_op | source)
XLA Modules:
  0.0 814.1 jit_solution(13025325412199249418)
XLA Ops:
  4.0 6.2 collective-permute-start.24
  57.3 5.7 all-to-all-start.4
  117.2 9.3 %collective-permute-start.33 = (bf16[1,1,1,1,48,1536]{5,4,3,2,1,0:T(8,128)(2,1)}, bf16[1,1,1,1,48,1536]{5,4,3,2,1,0:T(8,128)(2,1)S(1)}, u32[]{:S(2)}, u32[]{:S(2)}) collective-permute-start(bf16[1,1,1,1,48,1536]{5,4,3,2,1,0:T(8,128)(2,1)} %fusion.60), channel_id=1, source_target_pairs={{0,8},{2,10},{4,12},{6,14},{8,16},{10,18},{12,20},{14,22},{16,24},... | collective-permute-start | bytes 442376 | tf_op jit(solution)/shard_map/ppermute | solution.py:61
  153.4 7.0 collective-permute-done.12
  164.1 8.9 %collective-permute-done.48 = bf16[1,4,1,1,192,384]{5,4,3,2,1,0:T(8,128)(2,1)S(1)} collective-permute-done((bf16[1,4,1,1,192,384]{5,4,3,2,1,0:T(8,128)(2,1)S(1)}, bf16[1,4,1,1,192,384]{5,4,3,2,1,0:T(8,128)(2,1)S(1)}, u32[]{:S(2)}, u32[]{:S(2)}) %collective-permute-start.48) | collective-permute-done | bytes 589856 | tf_op jit(solution)/shard_map/ppermute | solution.py:69
  178.3 14.2 %collective-permute-done.13 = bf16[3,4,2,1,48,384]{5,4,0,3,2,1:T(8,128)(2,1)S(1)} collective-permute-done((bf16[3,4,2,1,48,384]{5,4,0,3,2,1:T(8,128)(2,1)S(1)}, bf16[3,4,2,1,48,384]{5,4,0,3,2,1:T(8,128)(2,1)S(1)}, u32[]{:S(2)}, u32[]{:S(2)}) %collective-permute-start.13) | collective-permute-done | bytes 884768 | tf_op jit(solution)/shard_map/ppermute | solution.py:69
  202.8 10.4 %collective-permute-done.49 = bf16[1,4,2,1,192,384]{5,4,3,2,1,0:T(8,128)(2,1)} collective-permute-done((bf16[1,4,2,1,192,384]{5,4,3,2,1,0:T(8,128)(2,1)}, bf16[1,4,2,1,192,384]{5,4,3,2,1,0:T(8,128)(2,1)}, u32[]{:S(2)}, u32[]{:S(2)}) %collective-permute-start.49) | collective-permute-done | bytes 1179680 | tf_op jit(solution)/shard_map/ppermute | solution.py:69
  240.5 11.6 %shard_map.388 = bf16[512,768]{1,0:T(8,128)(2,1)S(1)} custom-call(s32[1]{0:T(128)} %copy.75.length_ref, bf16[512,768]{1,0:T(8,128)(2,1)S(1)} %add_convert_fusion.15.query_ref, bf16[512,768]{1,0:T(8,128)(2,1)S(1)} %convolution_convert_fusion.4.key_ref, bf16[512,768]{1,0:T(8,128)(2,1)S(1)} %add_convert_fusion.14.value_ref, ...), custom_call_target="tpu_custom_call" | custom-call | tf_op jit(solution)/shard_map/pallas_call | solution.py:274
  262.8 18.4 %multiply_convert_fusion.2 = (bf16[512,3072]{1,0:T(8,128)(2,1)S(1)}, f32[512,3072]{1,0:T(8,128)}, f32[512,3072]{1,0:T(8,128)}) fusion(f32[3072]{0:T(1024)S(1)} %copy-done.137, bf16[768,3072]{1,0:T(8,128)(2,1)S(1)} %bitcast.250, f32[512,768]{1,0:T(8,128)S(1)} %get-tuple-element.431, f32[768]{0:T(1024)S(1)} %copy-done.150, f32[768]{0:T(1024)S(1)} %copy-done.136, ...), kind=kOutput, calls=%fused_computation.43 | convolution fusion | flops 2521694208 | bytes 22042624 | tf_op jit(solution)/shard_map/dot_general | solution.py:171
  297.3 6.6 collective-permute-done.55
  306.2 5.6 collective-permute-done.56
  313.0 16.6 %collective-permute-done.57 = bf16[4,1,1,128,768]{4,3,2,1,0:T(8,128)(2,1)S(1)} collective-permute-done((bf16[4,1,1,128,768]{4,3,2,1,0:T(8,128)(2,1)S(1)}, bf16[4,1,1,128,768]{4,3,2,1,0:T(8,128)(2,1)S(1)}, u32[]{:S(2)}, u32[]{:S(2)}) %collective-permute-start.57) | collective-permute-done | bytes 786464 | tf_op jit(solution)/shard_map/ppermute | solution.py:69
  339.4 6.3 fusion.113
  365.3 6.2 collective-permute-start.124
  379.0 12.2 %multiply_convert_fusion = bf16[2048,768]{1,0:T(8,128)(2,1)S(1)} fusion(bf16[1920,768]{1,0:T(8,128)(2,1)} %get-tuple-element.636, f32[2048]{0:T(1024)S(1)} %get-tuple-element.419, f32[2048,1920]{0,1:T(8,128)} %copy-done.15, s32[2048]{0:T(1024)S(1)} %bitcast.289, f32[2048]{0:T(1024)S(1)} %get-tuple-element.275), kind=kOutput, calls=%fused_computation.41 | convolution fusion | flops 6062604288 | bytes 21848064 | tf_op jit(solution)/shard_map/dot_general | solution.py:171
  402.2 18.1 %collective-permute-done.69 = bf16[4,1,1,128,768]{4,3,2,1,0:T(8,128)(2,1)S(1)} collective-permute-done((bf16[4,1,1,128,768]{4,3,2,1,0:T(8,128)(2,1)S(1)}, bf16[4,1,1,128,768]{4,3,2,1,0:T(8,128)(2,1)S(1)}, u32[]{:S(2)}, u32[]{:S(2)}) %collective-permute-start.69) | collective-permute-done | bytes 786464 | tf_op jit(solution)/shard_map/ppermute | solution.py:69
  446.3 14.1 %convolution_convert_fusion = bf16[1920,768]{1,0:T(8,128)(2,1)} fusion(bf16[2048,768]{1,0:T(8,128)(2,1)} %bitcast.255, f32[2048]{0:T(1024)S(1)} %get-tuple-element.419, f32[2048,1920]{0,1:T(8,128)} %copy-done.15, s32[2048]{0:T(1024)S(1)} %bitcast.290, f32[2048]{0:T(1024)S(1)} %get-tuple-element.275), kind=kOutput, calls=%fused_computation.79 | convolution fusion | flops 6065651712 | bytes 21848064 | tf_op jit(solution)/shard_map/dot_general | solution.py:175
  464.7 8.8 %convert_reduce_fusion = (f32[3072]{0:T(1024)S(1)}, bf16[512,3072]{1,0:T(8,128)(2,1)S(1)}) fusion(f32[512,3072]{1,0:T(8,128)} %get-tuple-element.313, f32[512,3072]{1,0:T(8,128)} %get-tuple-element.432, f32[3072]{0:T(1024)S(1)} %copy-done.137, bf16[512,768]{1,0:T(8,128)(2,1)S(1)} %get-tuple-element.293, bf16[3072,768]{1,0:T(8,128)(2,1)} %bitcast.249), kind=kOutput, calls=%fused_computation.39 | convolution fusion | flops 2442654720 | bytes 21258240 | tf_op jit(solution)/shard_map/dot_general | solution.py:179
  480.7 18.5 %shard_map.389 = (bf16[512,768]{1,0:T(8,128)(2,1)S(1)}, bf16[512,768]{1,0:T(8,128)(2,1)S(1)}, bf16[512,768]{1,0:T(8,128)(2,1)S(1)}, bf16[512,768]{1,0:T(8,128)(2,1)S(1)}, bf16[512,768]{1,0:T(8,128)(2,1)S(1)}) custom-call(s32[1]{0:T(128)} %copy.75.length_ref, bf16[512,768]{1,0:T(8,128)(2,1)S(1)} %copy-done.8, bf16[512,768]{1,0:T(8,128)(2,1)S(1)} %copy-done.5, ...), custom_call_target="tpu_custom_call" | custom-call | tf_op jit(solution)/shard_map/pallas_call | solution.py:274
  524.4 5.7 copy-done.16
  532.1 7.1 all-to-all-start.6
  572.7 5.9 dynamic-slice_convert_fusion
  590.9 18.3 %collective-permute-done.76 = bf16[1,768,768]{2,1,0:T(8,128)(2,1)S(1)} collective-permute-done((bf16[1,768,768]{2,1,0:T(8,128)(2,1)}, bf16[1,768,768]{2,1,0:T(8,128)(2,1)S(1)}, u32[]{:S(2)}, u32[]{:S(2)}) %collective-permute-start.76) | collective-permute-done | bytes 1179680 | tf_op jit(solution)/shard_map/ppermute | solution.py:69
  610.9 10.1 %add_add_fusion = f32[1920,768]{1,0:T(8,128)} fusion(bf16[1920,768]{1,0:T(8,128)(2,1)} %collective-permute-done.67, bf16[1920,768]{1,0:T(8,128)(2,1)} %convolution_convert_fusion, bf16[1536,768]{1,0:T(8,128)(2,1)S(1)} %bitcast.260, s32[1536]{0:T(1024)S(1)} %eq.348), kind=kOutput, calls=%fused_computation.59 | convolution fusion | flops 4538695680 | bytes 14161920 | tf_op jit(solution)/shard_map/dot_general | solution.py:175
  624.9 13.6 %collective-permute-done.98 = bf16[1,4,1,1,192,768]{5,4,3,2,1,0:T(8,128)(2,1)S(1)} collective-permute-done((bf16[1,4,1,1,192,768]{5,4,3,2,1,0:T(8,128)(2,1)S(1)}, bf16[1,4,1,1,192,768]{5,4,3,2,1,0:T(8,128)(2,1)S(1)}, u32[]{:S(2)}, u32[]{:S(2)}) %collective-permute-start.98) | collective-permute-done | bytes 1179680 | tf_op jit(solution)/shard_map/ppermute | solution.py:69
  642.7 5.9 add_convert_fusion.1
  674.3 23.5 %collective-permute-done.78 = bf16[7,4,1,1,48,768]{5,4,3,2,1,0:T(8,128)(2,1)} collective-permute-done((bf16[7,4,1,1,48,768]{5,4,3,2,1,0:T(8,128)(2,1)}, bf16[7,4,1,1,48,768]{5,4,3,2,1,0:T(8,128)(2,1)}, u32[]{:S(2)}, u32[]{:S(2)}) %collective-permute-start.78) | collective-permute-done | bytes 2064416 | tf_op jit(solution)/shard_map/ppermute | solution.py:69
  704.2 7.1 collective-permute-done.79
  716.7 8.8 %collective-permute-done.80 = bf16[7,1,1,1,48,768]{5,4,3,2,1,0:T(8,128)(2,1)S(1)} collective-permute-done((bf16[7,1,1,1,48,768]{5,4,3,2,1,0:T(8,128)(2,1)S(1)}, bf16[7,1,1,1,48,768]{5,4,3,2,1,0:T(8,128)(2,1)S(1)}, u32[]{:S(2)}, u32[]{:S(2)}) %collective-permute-start.80) | collective-permute-done | bytes 516128 | tf_op jit(solution)/shard_map/ppermute | solution.py:61
  741.6 9.1 %collective-permute-done.84 = bf16[7,1,1,1,48,768]{5,4,3,2,1,0:T(8,128)(2,1)S(1)} collective-permute-done((bf16[7,1,1,1,48,768]{5,4,3,2,1,0:T(8,128)(2,1)S(1)}, bf16[7,1,1,1,48,768]{5,4,3,2,1,0:T(8,128)(2,1)S(1)}, u32[]{:S(2)}, u32[]{:S(2)}) %collective-permute-start.84) | collective-permute-done | bytes 516128 | tf_op jit(solution)/shard_map/ppermute | solution.py:61
  752.7 7.2 collective-permute-done.85
  799.1 8.1 multiply_subtract_fusion
  (875 shorter events, 462.2 us)
Async XLA Ops:
  2.7 45.9 %collective-permute-start.27 = (bf16[1,1,1,1,48,384]{5,4,3,2,1,0:T(8,128)(2,1)}, bf16[1,1,1,1,48,384]{5,4,3,2,1,0:T(8,128)(2,1)}, u32[]{:S(2)}, u32[]{:S(2)}) collective-permute-start(bf16[1,1,1,1,48,384]{5,4,3,2,1,0:T(8,128)(2,1)} %dynamic-slice_bitcast_fusion.1), channel_id=1, source_target_pairs={{8,0},{10,2},{12,4},{14,6},{16,8},{18,10},{20,12},{22,14},{24,16},... | collective-permute-start | bytes 110600 | tf_op jit(solution)/shard_map/ppermute | solution.py:61
  4.0 45.9 %collective-permute-start.24 = (bf16[1,1,1,1,48,384]{5,4,3,2,1,0:T(8,128)(2,1)}, bf16[1,1,1,1,48,384]{5,4,3,2,1,0:T(8,128)(2,1)}, u32[]{:S(2)}, u32[]{:S(2)}) collective-permute-start(bf16[1,1,1,1,48,384]{5,4,3,2,1,0:T(8,128)(2,1)} %dynamic-slice_bitcast_fusion.1), channel_id=1, source_target_pairs={{0,8},{2,10},{4,12},{6,14},{8,16},{10,18},{12,20},{14,22},{16,24},... | collective-permute-start | bytes 110600 | tf_op jit(solution)/shard_map/ppermute | solution.py:61
  11.2 88.8 %collective-permute-start.9 = (bf16[3,1,1,1,48,384]{5,4,0,3,2,1:T(8,128)(2,1)}, bf16[3,1,1,1,48,384]{5,4,0,3,2,1:T(8,128)(2,1)}, u32[]{:S(2)}, u32[]{:S(2)}) collective-permute-start(bf16[3,1,1,1,48,384]{5,4,0,3,2,1:T(8,128)(2,1)} %dynamic-slice_bitcast_fusion), channel_id=1, source_target_pairs={{8,0},{10,2},{12,4},{14,6},{16,8},{18,10},{20,12},{22,14},{24,16},... | collective-permute-start | bytes 331784 | tf_op jit(solution)/shard_map/ppermute | solution.py:61
  40.5 60.8 %collective-permute-start.6 = (bf16[3,1,1,1,48,384]{5,4,0,3,2,1:T(8,128)(2,1)}, bf16[3,1,1,1,48,384]{5,4,0,3,2,1:T(8,128)(2,1)}, u32[]{:S(2)}, u32[]{:S(2)}) collective-permute-start(bf16[3,1,1,1,48,384]{5,4,0,3,2,1:T(8,128)(2,1)} %dynamic-slice_bitcast_fusion), channel_id=1, source_target_pairs={{0,8},{2,10},{4,12},{6,14},{8,16},{10,18},{12,20},{14,22},{16,24},... | collective-permute-start | bytes 331784 | tf_op jit(solution)/shard_map/ppermute | solution.py:61
  54.7 30.8 %collective-permute-start.29 = (bf16[1,1,1,1,48,384]{5,4,3,2,1,0:T(8,128)(2,1)}, bf16[1,1,1,1,48,384]{5,4,3,2,1,0:T(8,128)(2,1)}, u32[]{:S(2)}, u32[]{:S(2)}) collective-permute-start(bf16[1,1,1,1,48,384]{5,4,3,2,1,0:T(8,128)(2,1)} %collective-permute-done.28), channel_id=1, source_target_pairs={{8,0},{10,2},{12,4},{14,6},{9,1},{11,3},{13,5},{15,7}} | collective-permute-start | bytes 110600 | tf_op jit(solution)/shard_map/ppermute | solution.py:61
  56.0 29.5 %collective-permute-start.26 = (bf16[1,1,1,1,48,384]{5,4,3,2,1,0:T(8,128)(2,1)}, bf16[1,1,1,1,48,384]{5,4,3,2,1,0:T(8,128)(2,1)}, u32[]{:S(2)}, u32[]{:S(2)}) collective-permute-start(bf16[1,1,1,1,48,384]{5,4,3,2,1,0:T(8,128)(2,1)} %collective-permute-done.25), channel_id=1, source_target_pairs={{16,24},{18,26},{20,28},{22,30},{17,25},{19,27},{21,29},{23,31}} | collective-permute-start | bytes 110600 | tf_op jit(solution)/shard_map/ppermute | solution.py:61
  160.7 31.8 %collective-permute-start.13 = (bf16[3,4,2,1,48,384]{5,4,0,3,2,1:T(8,128)(2,1)S(1)}, bf16[3,4,2,1,48,384]{5,4,0,3,2,1:T(8,128)(2,1)S(1)}, u32[]{:S(2)}, u32[]{:S(2)}) collective-permute-start(bf16[3,4,2,1,48,384]{5,4,0,3,2,1:T(8,128)(2,1)S(1)} %pad_maximum_fusion.15), channel_id=1, source_target_pairs={{0,1},{1,0},{2,3},{3,2},{4,5},{5,4},{6,7},{7,6},{8,9},{9,8},{10,11... | collective-permute-start | bytes 2654216 | tf_op jit(solution)/shard_map/ppermute | solution.py:69
  162.8 36.5 %collective-permute-start.22 = (bf16[3,4,1,1,48,768]{5,4,0,3,2,1:T(8,128)(2,1)}, bf16[3,4,1,1,48,768]{5,4,0,3,2,1:T(8,128)(2,1)}, u32[]{:S(2)}, u32[]{:S(2)}) collective-permute-start(bf16[3,4,1,1,48,768]{5,4,0,3,2,1:T(8,128)(2,1)} %pad_maximum_fusion.16), channel_id=1, source_target_pairs={{0,4},{2,6},{4,0},{6,2},{8,12},{10,14},{12,8},{14,10},{16,20},{18,... | collective-permute-start | bytes 2654216 | tf_op jit(solution)/shard_map/ppermute | solution.py:69
  174.4 38.8 %collective-permute-start.49 = (bf16[1,4,2,1,192,384]{5,4,3,2,1,0:T(8,128)(2,1)}, bf16[1,4,2,1,192,384]{5,4,3,2,1,0:T(8,128)(2,1)}, u32[]{:S(2)}, u32[]{:S(2)}) collective-permute-start(bf16[1,4,2,1,192,384]{5,4,3,2,1,0:T(8,128)(2,1)} %pad_maximum_fusion.14), channel_id=1, source_target_pairs={{0,1},{1,0},{2,3},{3,2},{4,5},{5,4},{6,7},{7,6},{8,9},{9,8},{10,11... | collective-permute-start | bytes 3538952 | tf_op jit(solution)/shard_map/ppermute | solution.py:69
  176.6 43.6 %collective-permute-start.40 = (bf16[1,4,1,1,48,3072]{5,4,3,2,1,0:T(8,128)(2,1)}, bf16[1,4,1,1,48,3072]{5,4,3,2,1,0:T(8,128)(2,1)}, u32[]{:S(2)}, u32[]{:S(2)}) collective-permute-start(bf16[1,4,1,1,48,3072]{5,4,3,2,1,0:T(8,128)(2,1)} %pad_maximum_fusion.13), channel_id=1, source_target_pairs={{0,4},{2,6},{4,0},{6,2},{8,12},{10,14},{12,8},{14,10},{16,20},{18,... | collective-permute-start | bytes 3538952 | tf_op jit(solution)/shard_map/ppermute | solution.py:69
  192.7 31.4 %all-to-all-start.5 = ((bf16[16,48,768]{2,1,0:T(8,128)(2,1)}), bf16[16,48,768]{2,1,0:T(8,128)(2,1)}, u32[]{:S(2)}, u32[]{:S(2)}) async-start(bf16[16,48,768]{2,1,0:T(8,128)(2,1)} %bitcast.276), calls=%async_computation.5 | async-start | bytes 2359296 | tf_op jit(solution)/shard_map/all_to_all | solution.py:504
  199.0 34.4 %collective-permute-start.14 = (bf16[3,4,2,1,48,768]{5,4,0,3,2,1:T(8,128)(2,1)}, bf16[3,4,2,1,48,768]{5,4,0,3,2,1:T(8,128)(2,1)}, u32[]{:S(2)}, u32[]{:S(2)}) collective-permute-start(bf16[3,4,2,1,48,768]{5,4,0,3,2,1:T(8,128)(2,1)} %pad_maximum_fusion.7), channel_id=1, source_target_pairs={{0,2},{2,0},{4,6},{6,4},{8,10},{10,8},{12,14},{14,12},{16,18},{18,... | collective-permute-start | bytes 5308424 | tf_op jit(solution)/shard_map/ppermute | solution.py:69
  202.6 25.2 %collective-permute-start.23 = (bf16[3,4,2,1,48,768]{5,4,0,3,2,1:T(8,128)(2,1)}, bf16[3,4,2,1,48,768]{5,4,0,3,2,1:T(8,128)(2,1)}, u32[]{:S(2)}, u32[]{:S(2)}) collective-permute-start(bf16[3,4,2,1,48,768]{5,4,0,3,2,1:T(8,128)(2,1)} %pad_maximum_fusion.8), channel_id=1, source_target_pairs={{0,2},{2,0},{4,6},{6,4},{8,10},{10,8},{12,14},{14,12},{16,18},{18,... | collective-permute-start | bytes 5308424 | tf_op jit(solution)/shard_map/ppermute | solution.py:69
  216.9 36.5 %collective-permute-start.50 = (bf16[1,4,2,1,192,768]{5,4,3,2,1,0:T(8,128)(2,1)}, bf16[1,4,2,1,192,768]{5,4,3,2,1,0:T(8,128)(2,1)}, u32[]{:S(2)}, u32[]{:S(2)}) collective-permute-start(bf16[1,4,2,1,192,768]{5,4,3,2,1,0:T(8,128)(2,1)} %pad_maximum_fusion.5), channel_id=1, source_target_pairs={{0,2},{2,0},{4,6},{6,4},{8,10},{10,8},{12,14},{14,12},{16,18},{18,... | collective-permute-start | bytes 7077896 | tf_op jit(solution)/shard_map/ppermute | solution.py:69
  224.1 34.1 %collective-permute-start.41 = (bf16[1,4,2,1,48,3072]{5,4,3,2,1,0:T(8,128)(2,1)}, bf16[1,4,2,1,48,3072]{5,4,3,2,1,0:T(8,128)(2,1)}, u32[]{:S(2)}, u32[]{:S(2)}) collective-permute-start(bf16[1,4,2,1,48,3072]{5,4,3,2,1,0:T(8,128)(2,1)} %pad_maximum_fusion.4), channel_id=1, source_target_pairs={{0,2},{2,0},{4,6},{6,4},{8,10},{10,8},{12,14},{14,12},{16,18},{18,... | collective-permute-start | bytes 7077896 | tf_op jit(solution)/shard_map/ppermute | solution.py:69
  460.4 150.4 %collective-permute-start.67 = (bf16[1920,768]{1,0:T(8,128)(2,1)}, bf16[1920,768]{1,0:T(8,128)(2,1)}, u32[]{:S(2)}, u32[]{:S(2)}) collective-permute-start(bf16[1920,768]{1,0:T(8,128)(2,1)} %convolution_convert_fusion), channel_id=1, source_target_pairs={{0,1},{1,0},{2,3},{3,2},{4,5},{5,4},{6,7},{7,6},{8,9},{9,8},{10,11... | collective-permute-start | bytes 8847368 | tf_op jit(solution)/shard_map/ppermute | solution.py:69
  510.1 35.6 %collective-permute-start.112 = (f32[3072]{0:T(1024)S(1)}, f32[3072]{0:T(1024)S(1)}, u32[]{:S(2)}, u32[]{:S(2)}) collective-permute-start(f32[3072]{0:T(1024)S(1)} %get-tuple-element.290), channel_id=1, source_target_pairs={{0,2},{2,0},{4,6},{6,4},{8,10},{10,8},{12,14},{14,12},{16,18},{18,... | collective-permute-start | bytes 36872 | tf_op jit(solution)/shard_map/ppermute | solution.py:122
  519.7 61.4 %collective-permute-start.87 = (bf16[1,4,2,1,48,3072]{5,4,3,2,1,0:T(8,128)(2,1)}, bf16[1,4,2,1,48,3072]{5,4,3,2,1,0:T(8,128)(2,1)}, u32[]{:S(2)}, u32[]{:S(2)}) collective-permute-start(bf16[1,4,2,1,48,3072]{5,4,3,2,1,0:T(8,128)(2,1)} %dynamic-slice_convert_fusion.2), channel_id=1, source_target_pairs={{0,2},{2,0},{4,6},{6,4},{8,10},{10,8},{12,14},{14,12},{16,18},{18,... | collective-permute-start | bytes 7077896 | tf_op jit(solution)/shard_map/ppermute | solution.py:69
  521.6 65.0 %collective-permute-start.97 = (bf16[1,4,2,1,192,768]{5,4,3,2,1,0:T(8,128)(2,1)}, bf16[1,4,2,1,192,768]{5,4,3,2,1,0:T(8,128)(2,1)}, u32[]{:S(2)}, u32[]{:S(2)}) collective-permute-start(bf16[1,4,2,1,192,768]{5,4,3,2,1,0:T(8,128)(2,1)} %dynamic-slice_convert_fusion.1), channel_id=1, source_target_pairs={{0,2},{2,0},{4,6},{6,4},{8,10},{10,8},{12,14},{14,12},{16,18},{18,... | collective-permute-start | bytes 7077896 | tf_op jit(solution)/shard_map/ppermute | solution.py:69
  532.1 48.5 %all-to-all-start.6 = ((bf16[16,48,768]{2,1,0:T(8,128)(2,1)}), bf16[16,48,768]{2,1,0:T(8,128)(2,1)}, u32[]{:S(2)}, u32[]{:S(2)}) async-start(bf16[16,48,768]{2,1,0:T(8,128)(2,1)} %bitcast.277), calls=%async_computation.6 | async-start | bytes 2359296 | tf_op jit(solution)/shard_map/all_to_all | solution.py:622
  579.3 63.4 %collective-permute-start.77 = (bf16[7,4,2,1,48,768]{5,4,3,2,1,0:T(8,128)(2,1)}, bf16[7,4,2,1,48,768]{5,4,3,2,1,0:T(8,128)(2,1)}, u32[]{:S(2)}, u32[]{:S(2)}) collective-permute-start(bf16[7,4,2,1,48,768]{5,4,3,2,1,0:T(8,128)(2,1)} %dynamic-slice_convert_fusion), channel_id=1, source_target_pairs={{0,2},{2,0},{4,6},{6,4},{8,10},{10,8},{12,14},{14,12},{16,18},{18,... | collective-permute-start | bytes 12386312 | tf_op jit(solution)/shard_map/ppermute | solution.py:69
  580.6 28.6 %collective-permute-start.76 = (bf16[1,768,768]{2,1,0:T(8,128)(2,1)}, bf16[1,768,768]{2,1,0:T(8,128)(2,1)S(1)}, u32[]{:S(2)}, u32[]{:S(2)}) collective-permute-start(bf16[1,768,768]{2,1,0:T(8,128)(2,1)} %bitcast.41), channel_id=1, source_target_pairs={{0,1},{1,0},{2,3},{3,2},{4,5},{5,4},{6,7},{7,6},{8,9},{9,8},{10,11... | collective-permute-start | bytes 3538952 | tf_op jit(solution)/shard_map/ppermute | solution.py:69
  585.0 35.9 %collective-permute-start.88 = (bf16[1,4,1,1,48,3072]{5,4,3,2,1,0:T(8,128)(2,1)S(1)}, bf16[1,4,1,1,48,3072]{5,4,3,2,1,0:T(8,128)(2,1)S(1)}, u32[]{:S(2)}, u32[]{:S(2)}) collective-permute-start(bf16[1,4,1,1,48,3072]{5,4,3,2,1,0:T(8,128)(2,1)S(1)} %constant_dynamic-slice_fusion.8), channel_id=1, source_target_pairs={{0,4},{2,6},{4,0},{6,2},{8,12},{10,14},{12,8},{14,10},{16,20},{18,... | collective-permute-start | bytes 3538952 | tf_op jit(solution)/shard_map/ppermute | solution.py:69
  590.3 48.2 %collective-permute-start.98 = (bf16[1,4,1,1,192,768]{5,4,3,2,1,0:T(8,128)(2,1)S(1)}, bf16[1,4,1,1,192,768]{5,4,3,2,1,0:T(8,128)(2,1)S(1)}, u32[]{:S(2)}, u32[]{:S(2)}) collective-permute-start(bf16[1,4,1,1,192,768]{5,4,3,2,1,0:T(8,128)(2,1)S(1)} %constant_dynamic-slice_fusion.4), channel_id=1, source_target_pairs={{0,4},{2,6},{4,0},{6,2},{8,12},{10,14},{12,8},{14,10},{16,20},{18,... | collective-permute-start | bytes 3538952 | tf_op jit(solution)/shard_map/ppermute | solution.py:69
  623.5 38.1 %collective-permute-start.92 = (bf16[1,1,1,1,48,3072]{5,4,3,2,1,0:T(8,128)(2,1)}, bf16[1,1,1,1,48,3072]{5,4,3,2,1,0:T(8,128)(2,1)}, u32[]{:S(2)}, u32[]{:S(2)}) collective-permute-start(bf16[1,1,1,1,48,3072]{5,4,3,2,1,0:T(8,128)(2,1)} %get-tuple-element.357), channel_id=1, source_target_pairs={{24,16},{26,18},{28,20},{30,22},{25,17},{27,19},{29,21},{31,23}} | collective-permute-start | bytes 884744 | tf_op jit(solution)/shard_map/ppermute | solution.py:61
  651.3 46.6 %collective-permute-start.78 = (bf16[7,4,1,1,48,768]{5,4,3,2,1,0:T(8,128)(2,1)}, bf16[7,4,1,1,48,768]{5,4,3,2,1,0:T(8,128)(2,1)}, u32[]{:S(2)}, u32[]{:S(2)}) collective-permute-start(bf16[7,4,1,1,48,768]{5,4,3,2,1,0:T(8,128)(2,1)} %constant_dynamic-slice_fusion.12), channel_id=1, source_target_pairs={{0,4},{2,6},{4,0},{6,2},{8,12},{10,14},{12,8},{14,10},{16,20},{18,... | collective-permute-start | bytes 6193160 | tf_op jit(solution)/shard_map/ppermute | solution.py:69
  662.8 49.3 %collective-permute-start.91 = (bf16[1,1,1,1,48,3072]{5,4,3,2,1,0:T(8,128)(2,1)S(1)}, bf16[1,1,1,1,48,3072]{5,4,3,2,1,0:T(8,128)(2,1)S(1)}, u32[]{:S(2)}, u32[]{:S(2)}) collective-permute-start(bf16[1,1,1,1,48,3072]{5,4,3,2,1,0:T(8,128)(2,1)S(1)} %get-tuple-element.354), channel_id=1, source_target_pairs={{0,8},{2,10},{4,12},{6,14},{8,16},{10,18},{12,20},{14,22},{16,24},... | collective-permute-start | bytes 884744 | tf_op jit(solution)/shard_map/ppermute | solution.py:61
  665.7 35.7 %collective-permute-start.93 = (bf16[1,1,1,1,48,3072]{5,4,3,2,1,0:T(8,128)(2,1)S(1)}, bf16[1,1,1,1,48,3072]{5,4,3,2,1,0:T(8,128)(2,1)S(1)}, u32[]{:S(2)}, u32[]{:S(2)}) collective-permute-start(bf16[1,1,1,1,48,3072]{5,4,3,2,1,0:T(8,128)(2,1)S(1)} %get-tuple-element.355), channel_id=1, source_target_pairs={{16,8},{18,10},{20,12},{22,14},{24,16},{26,18},{28,20},{30,22},{17... | collective-permute-start | bytes 884744 | tf_op jit(solution)/shard_map/ppermute | solution.py:61
  669.2 59.1 %collective-permute-start.101 = (bf16[1,1,1,1,192,768]{5,4,3,2,1,0:T(8,128)(2,1)S(1)}, bf16[1,1,1,1,192,768]{5,4,3,2,1,0:T(8,128)(2,1)S(1)}, u32[]{:S(2)}, u32[]{:S(2)}) collective-permute-start(bf16[1,1,1,1,192,768]{5,4,3,2,1,0:T(8,128)(2,1)S(1)} %get-tuple-element.350), channel_id=1, source_target_pairs={{0,8},{2,10},{4,12},{6,14},{8,16},{10,18},{12,20},{14,22},{16,24},... | collective-permute-start | bytes 884744 | tf_op jit(solution)/shard_map/ppermute | solution.py:61
  673.6 29.2 %collective-permute-start.103 = (bf16[1,1,1,1,192,768]{5,4,3,2,1,0:T(8,128)(2,1)S(1)}, bf16[1,1,1,1,192,768]{5,4,3,2,1,0:T(8,128)(2,1)S(1)}, u32[]{:S(2)}, u32[]{:S(2)}) collective-permute-start(bf16[1,1,1,1,192,768]{5,4,3,2,1,0:T(8,128)(2,1)S(1)} %get-tuple-element.351), channel_id=1, source_target_pairs={{16,8},{18,10},{20,12},{22,14},{24,16},{26,18},{28,20},{30,22},{17... | collective-permute-start | bytes 884744 | tf_op jit(solution)/shard_map/ppermute | solution.py:61
  702.9 25.4 %collective-permute-start.104 = (bf16[1,1,1,1,192,768]{5,4,3,2,1,0:T(8,128)(2,1)S(1)}, bf16[1,1,1,1,192,768]{5,4,3,2,1,0:T(8,128)(2,1)S(1)}, u32[]{:S(2)}, u32[]{:S(2)}) collective-permute-start(bf16[1,1,1,1,192,768]{5,4,3,2,1,0:T(8,128)(2,1)S(1)} %add_convert_fusion.26), channel_id=1, source_target_pairs={{8,0},{10,2},{12,4},{14,6},{16,8},{18,10},{20,12},{22,14},{24,16},... | collective-permute-start | bytes 884744 | tf_op jit(solution)/shard_map/ppermute | solution.py:61
  737.2 24.4 %collective-permute-start.106 = (bf16[1,192,384]{2,1,0:T(8,128)(2,1)S(1)}, bf16[1,192,384]{2,1,0:T(8,128)(2,1)S(1)}, u32[]{:S(2)}, u32[]{:S(2)}) collective-permute-start(bf16[1,192,384]{2,1,0:T(8,128)(2,1)S(1)} %fusion.59), channel_id=1, source_target_pairs={{0,1},{1,0},{2,3},{3,2},{4,5},{5,4},{6,7},{7,6},{8,9},{9,8},{10,11... | collective-permute-start | bytes 442376 | tf_op jit(solution)/shard_map/ppermute | solution.py:69
  (266 other events, 2613.9 us)

commit v2 on v1

--- a/solution.py
+++ b/solution.py
@@ -1,4 +1,3 @@
-from functools import partial
 import math
 from typing import NamedTuple
 
@@ -52,20 +51,11 @@
     return lax.axis_index(line.axis) // line.stride % line.count
 
 
-def hop(value, line, step, senders):
-    pairs = [
-        (i, i + step * line.stride)
-        for i in range(line.total)
-        if i // line.stride % line.count in senders
-    ]
-    return lax.ppermute(value, line.axis, pairs)
-
-
-def swap(value, line):
-    pairs = [
-        (i, i + line.stride if i // line.stride % 2 == 0 else i - line.stride)
-        for i in range(line.total)
-    ]
+def shifted(value, line, step):
+    pairs = []
+    for i in range(line.total):
+        place = i // line.stride % line.count
+        pairs.append((i, i + ((place + step) % line.count - place) * line.stride))
     return lax.ppermute(value, line.axis, pairs)
 
 
@@ -74,44 +64,38 @@
     if count == 1:
         return value
     here = place_on(line)
-    if count == 2:
-        other = swap(value, line)
-        first = jnp.where(here == 0, value, other)
-        second = jnp.where(here == 0, other, value)
-        return jnp.concatenate([first, second], axis=axis)
-    lower, upper = [value], [value]
-    for step in range(1, count):
-        lower.append(hop(lower[-1], line, 1, range(step - 1, count - 1)))
-        upper.append(hop(upper[-1], line, -1, range(1, count - step + 1)))
+    pieces = [value] + [shifted(value, line, step) for step in range(1, count)]
     blocks = []
     for place in range(count):
-        choices = [upper[place - i] if i <= place else lower[i - place] for i in range(count)]
-        blocks.append(lax.select_n(here, *choices))
+        blocks.append(lax.select_n(here, *[pieces[(i - place) % count] for i in range(count)]))
     return jnp.concatenate(blocks, axis=axis)
 
 
-def reduce_line(value, line, axis):
-    count = line.count
-    if count == 1:
-        return value.astype(FLOAT)
+def sends(value, line, axis):
+    size = value.shape[axis] // line.count
     here = place_on(line)
-    size = value.shape[axis] // count
 
     def block(place):
         return lax.dynamic_slice_in_dim(value, place * size, size, axis)
 
-    if count == 2:
-        return block(here).astype(FLOAT) + swap(block(1 - here).astype(BFLOAT), line).astype(FLOAT)
-    lower = upper = None
-    for step in range(count - 1):
-        to_upper = block(jnp.minimum(here + count - 1 - step, count - 1)).astype(FLOAT)
-        to_lower = block(jnp.maximum(here - (count - 1 - step), 0)).astype(FLOAT)
-        if lower is not None:
-            to_upper = to_upper + lower
-            to_lower = to_lower + upper
-        lower = hop(to_upper.astype(BFLOAT), line, 1, range(0, step + 1)).astype(FLOAT)
-        upper = hop(to_lower.astype(BFLOAT), line, -1, range(count - 1 - step, count)).astype(FLOAT)
-    return block(here).astype(FLOAT) + (lower + upper)
+    return block(here), [
+        block((here + step) % line.count).astype(BFLOAT) for step in range(1, line.count)
+    ]
+
+
+def received(own, blocks, line):
+    total = own.astype(FLOAT)
+    for step, value in enumerate(blocks, 1):
+        total = total + shifted(value, line, step).astype(FLOAT)
+    return total
+
+
+def reduce_line(value, line, axis):
+    return received(*sends(value, line, axis), line)
+
+
+def after(value, *others):
+    return lax.optimization_barrier((value, *others))[0]
 
 
 def paired(value, axis, combine):
@@ -124,26 +108,32 @@
     return value
 
 
-def gather_weight(value, lines, order):
-    x = lines["x"]
-    part = value.shape[2] // x.count
-    piece = lax.dynamic_slice_in_dim(value, place_on(x) * part, part, 2)
-    piece = piece[:, None, None, None]
-    axes = {"z": 1, "y": 2, "core": 3, "x": 5}
-    for name in order:
-        piece = gather_line(piece, lines[name], axes[name])
-    count, rows, columns = value.shape
-    return piece.reshape(count, -1, columns)
-
-
-def reduce_weight(value, lines, order):
+def by_owner(value, lines):
     count, _, columns = value.shape
-    z, y, core = lines["z"].count, lines["y"].count, lines["core"].count
-    piece = value.reshape(count, z, y, core, -1, columns)
-    axes = {"z": 1, "y": 2, "core": 3, "x": 5}
-    for name in order:
-        piece = reduce_line(piece, lines[name], axes[name]).astype(BFLOAT)
-    return gather_line(piece[:, 0, 0, 0], lines["x"], 2).astype(FLOAT)
+    return value.reshape(count, lines["z"].count, lines["y"].count, lines["core"].count, -1, columns)
+
+
+AXES = {"z": 1, "y": 2, "core": 3, "x": 5}
+
+
+def part_sends(value, lines, name):
+    return sends(value, lines[name], AXES[name])
+
+
+def part_received(pair, lines, name):
+    return received(*pair, lines[name]).astype(BFLOAT)
+
+
+def both_copies(value, lines):
+    if lines["x"].count == 2:
+        return value.astype(FLOAT) + shifted(value, lines["x"], 1).astype(FLOAT)
+    return lax.psum(value, "rep").astype(FLOAT)
+
+
+def from_other_copies(value, lines):
+    if lines["x"].count == 2:
+        return shifted(value, lines["x"], 1)
+    return (lax.psum(value, "rep").astype(FLOAT) - value.astype(FLOAT)).astype(BFLOAT)
 
 
 def layer_norm(value, gain, shift):
@@ -316,8 +306,151 @@
     return (index[:, None] == jnp.arange(count, dtype=jnp.int32)[None, :]).astype(BFLOAT)
 
 
+def feed_kernel(middle_ref, up_ref, bias_ref, down_ref, active_ref, slope_ref, out_ref):
+    value = product(middle_ref[...], up_ref[...]) + bias_ref[...]
+    share = 0.5 * (1.0 + lax.erf(value * math.sqrt(0.5)))
+    density = jnp.exp(-0.5 * value * value) * (1.0 / math.sqrt(2.0 * math.pi))
+    active = (value * share).astype(BFLOAT)
+    active_ref[...] = active
+    slope_ref[...] = share + value * density
+    out = product(active, down_ref[...])
+
+    @pl.when(pl.program_id(0) == 0)
+    def _():
+        out_ref[...] = out
+
+    @pl.when(pl.program_id(0) > 0)
+    def _():
+        out_ref[...] += out
+
+
+def feed_forward(middle_low, packed, bias, down):
+    tokens, width = middle_low.shape
+    hidden = down.shape[0]
+    whole = pl.BlockSpec((tokens, width), lambda j: (0, 0))
+    columns = pl.BlockSpec((tokens, width), lambda j: (0, j))
+    return pl.pallas_call(
+        feed_kernel,
+        grid=(hidden // width,),
+        in_specs=[
+            whole,
+            pl.BlockSpec((None, width, width), lambda j: (j, 0, 0)),
+            pl.BlockSpec((1, width), lambda j: (0, j)),
+            pl.BlockSpec((width, width), lambda j: (j, 0)),
+        ],
+        out_specs=[columns, columns, whole],
+        out_shape=[
+            jax.ShapeDtypeStruct((tokens, hidden), BFLOAT),
+            jax.ShapeDtypeStruct((tokens, hidden), FLOAT),
+            jax.ShapeDtypeStruct((tokens, width), FLOAT),
+        ],
+        compiler_params=pltpu.CompilerParams(vmem_limit_bytes=48 * 1024 * 1024),
+    )(middle_low, packed, bias[None], down)
+
+
+def feed_back_kernel(
+    grad_ref,
+    middle_ref,
+    active_ref,
+    slope_ref,
+    up_ref,
+    down_ref,
+    grad_up_ref,
+    grad_down_ref,
+    grad_bias_ref,
+    out_ref,
+):
+    grad = grad_ref[...]
+    grad_upper = (times_transposed(grad, down_ref[...]) * slope_ref[...]).astype(BFLOAT)
+    grad_bias_ref[...] = jnp.sum(grad_upper.astype(FLOAT), axis=0, keepdims=True)
+    grad_down_ref[...] = contract_rows(active_ref[...], grad).astype(BFLOAT)
+    grad_up_ref[...] = contract_rows(middle_ref[...], grad_upper).astype(BFLOAT)
+    out = times_transposed(grad_upper, up_ref[...])
+
+    @pl.when(pl.program_id(0) == 0)
+    def _():
+        out_ref[...] = out
+
+    @pl.when(pl.program_id(0) > 0)
+    def _():
+        out_ref[...] += out
+
+
+def feed_backward(grad_feed, middle_low, active, slope, packed, down):
+    tokens, width = middle_low.shape
+    hidden = down.shape[0]
+    whole = pl.BlockSpec((tokens, width), lambda j: (0, 0))
+    columns = pl.BlockSpec((tokens, width), lambda j: (0, j))
+    return pl.pallas_call(
+        feed_back_kernel,
+        grid=(hidden // width,),
+        in_specs=[
+            whole,
+            whole,
+            columns,
+            columns,
+            pl.BlockSpec((None, width, width), lambda j: (j, 0, 0)),
+            pl.BlockSpec((width, width), lambda j: (j, 0)),
+        ],
+        out_specs=[
+            pl.BlockSpec((width, width), lambda j: (0, j)),
+            pl.BlockSpec((width, width), lambda j: (j, 0)),
+            pl.BlockSpec((1, width), lambda j: (0, j)),
+            whole,
+        ],
+        out_shape=[
+            jax.ShapeDtypeStruct((width, hidden), BFLOAT),
+            jax.ShapeDtypeStruct((hidden, width), BFLOAT),
+            jax.ShapeDtypeStruct((1, hidden), FLOAT),
+            jax.ShapeDtypeStruct((tokens, width), FLOAT),
+        ],
+        compiler_params=pltpu.CompilerParams(vmem_limit_bytes=48 * 1024 * 1024),
+    )(grad_feed, middle_low, active, slope, packed, down)
+
+
+def logits_kernel(rows_ref, table_ref, label_ref, expo_ref, stats_ref):
+    logits = times_transposed(rows_ref[...], table_ref[...])
+    peak = jnp.max(logits, axis=1, keepdims=True)
+    expo = jnp.exp(logits - peak)
+    expo_ref[...] = expo.astype(BFLOAT)
+    mass = jnp.sum(expo, axis=1, keepdims=True)
+    column = lax.broadcasted_iota(jnp.int32, logits.shape, 1)
+    target = jnp.sum(jnp.where(column == label_ref[...], logits, 0.0), axis=1, keepdims=True)
+    lane = lax.broadcasted_iota(jnp.int32, (logits.shape[0], LANES), 1)
+    stats = jnp.where(lane == 0, peak, jnp.where(lane == 1, mass, target))
+    stats_ref[...] = stats.T[:8]
+
+
+def head_logits(rows_all, table_low, own_labels):
+    count, width = rows_all.shape
+    shard_rows = table_low.shape[0]
+    step = 256
+    return pl.pallas_call(
+        logits_kernel,
+        grid=(count // step,),
+        in_specs=[
+            pl.BlockSpec((step, width), lambda i: (i, 0)),
+            pl.BlockSpec((shard_rows, width), lambda i: (0, 0)),
+            pl.BlockSpec((step, 1), lambda i: (i, 0)),
+        ],
+        out_specs=[
+            pl.BlockSpec((step, shard_rows), lambda i: (i, 0)),
+            pl.BlockSpec((8, step), lambda i: (0, i)),
+        ],
+        out_shape=[
+            jax.ShapeDtypeStruct((count, shard_rows), BFLOAT),
+            jax.ShapeDtypeStruct((8, count), FLOAT),
+        ],
+        compiler_params=pltpu.CompilerParams(vmem_limit_bytes=48 * 1024 * 1024),
+    )(rows_all, table_low, own_labels[:, None])
+
+
+def column_sum(value):
+    return jnp.sum(value.astype(FLOAT), axis=0)
+
+
 def layer_forward(weights, embedded, place, box_query, box_key, lengths):
-    mats, up, down, gains, up_bias = weights
+    mats, packed, down, gains, up_bias = weights
     start_state = layer_norm(embedded, gains[0], gains[1])
     act = start_state.astype(BFLOAT)
     query = (product(act, mats[1]) + gains[6]).astype(BFLOAT)
@@ -327,9 +460,8 @@
     first_sum = start_state + (product(mixed, mats[6]) + gains[8])
     middle = layer_norm(first_sum, gains[2], gains[3])
     middle_low = middle.astype(BFLOAT)
-    upper = product(middle_low, up) + up_bias
-    active = jax.nn.gelu(upper, approximate=False).astype(BFLOAT)
-    second_sum = middle + (product(active, down) + gains[10])
+    active, slope, feed = feed_forward(middle_low, packed, up_bias, down)
+    second_sum = middle + (feed + gains[10])
     kept = (
         embedded,
         act,
@@ -342,15 +474,15 @@
         mixed,
         first_sum,
         middle_low,
-        upper,
+        slope,
         active,
         second_sum,
     )
     return (layer_norm(second_sum, gains[4], gains[5]), kept)
 
 
-def layer_backward(weights, features_low, lengths, kept, grad_out, lines):
-    mats, up, down, gains, up_bias = weights
+def layer_backward(weights, features_low, lengths, kept, grad_out, head_parts, lines, tools):
+    mats, packed, down, gains, up_bias = weights
     (
         embedded,
         act,
@@ -363,57 +495,89 @@
         mixed,
         first_sum,
         middle_low,
-        upper,
+        slope,
         active,
         second_sum,
     ) = kept
-
-    def column_sum(value):
-        return jnp.sum(value.astype(FLOAT), axis=0)
+    compacted, give, over_copies = tools
+
+    def send(value, name):
+        own, blocks = sends(value, lines[name], AXES[name])
+        return own, blocks
+
+    def travel(pair, name, until=None):
+        line = lines[name]
+        moved = [shifted(block, line, step) for step, block in enumerate(pair[1], 1)]
+        if until is not None:
+            moved = list(after(tuple(moved), until))
+        total = pair[0].astype(FLOAT)
+        for value in moved:
+            total = total + value.astype(FLOAT)
+        return total.astype(BFLOAT)
 
     grad_second, gain_four, gain_five = jax.vjp(layer_norm, second_sum, gains[4], gains[5])[1](
         grad_out
     )
-    order = ("core", "y", "z", "x")
     grad_feed = grad_second.astype(BFLOAT)
-    grad_down = reduce_weight(contract_rows(active, grad_feed)[None], lines, order)
-    grad_active = times_transposed(grad_feed, down)
-    grad_upper = jax.vjp(partial(jax.nn.gelu, approximate=False), upper)[1](grad_active)[0].astype(
-        BFLOAT
-    )
-    grad_up = reduce_weight(contract_rows(middle_low, grad_upper)[None], lines, order)
-    grad_middle = grad_second + times_transposed(grad_upper, up)
+    grad_up, grad_down, grad_bias, fed_back = feed_backward(
+        grad_feed, middle_low, active, slope, packed, down
+    )
+    down_core = send(by_owner(grad_down[None], lines), "core")
+    up_core = send(by_owner(grad_up[None], lines), "core")
+    fed_back = after(fed_back, *down_core[1], *up_core[1], head_parts[1])
     grad_first, gain_two, gain_three = jax.vjp(layer_norm, first_sum, gains[2], gains[3])[1](
-        grad_middle
+        grad_second + fed_back
     )
     grad_attended = grad_first.astype(BFLOAT)
-    grad_output = contract_rows(mixed, grad_attended)
+    down_y = send(travel(down_core, "core", grad_attended), "y")
+    grad_attended = after(grad_attended, *down_y[1])
     grad_mixed = times_transposed(grad_attended, mats[6]).astype(BFLOAT)
-    grad_query, grad_keys, grad_values, grad_box_query, grad_box_key = attention_call(
+    up_x = send(travel(up_core, "core", grad_mixed), "x")
+    grad_mixed = after(grad_mixed, *up_x[1])
+    pieces = attention_call(
         attend_back_kernel, lengths, (query, keys, values, box_query, box_key, grad_mixed), 5
     )
+    down_z = send(travel(down_y, "y", pieces[0]), "z")
+    pieces = after(tuple(pieces), *down_z[1], *head_parts[2:])
+    grad_query, grad_keys, grad_values, grad_box_query, grad_box_key = pieces
+    grad_start = (
+        grad_first + times_transposed(grad_query, mats[1]) + times_transposed(grad_keys, mats[2])
+    )
+    grad_start = grad_start + times_transposed(grad_values, mats[3])
+    grad_embedded, gain_zero, gain_one = jax.vjp(layer_norm, embedded, gains[0], gains[1])[1](
+        grad_start
+    )
+    parts = two_parts(grad_embedded)
+    compact = compacted(parts)
+    returned = give(compact)
+    pieces = after(tuple(pieces), compact)
+    grad_query, grad_keys, grad_values, grad_box_query, grad_box_key = pieces
+    token_part = jnp.stack(
+        [
+            contract_rows(act, grad_query),
+            contract_rows(act, grad_keys),
+            contract_rows(act, grad_values),
+            contract_rows(mixed, grad_attended),
+        ]
+    ).astype(BFLOAT)
+    token_core = send(by_owner(token_part, lines), "core")
+    grad_box_query = after(grad_box_query, *token_core[1])
     grad_place = (
         times_transposed(grad_box_query, mats[4]) + times_transposed(grad_box_key, mats[5])
     ).astype(BFLOAT)
-    grad_start = (
-        grad_first + times_transposed(grad_query, mats[1]) + times_transposed(grad_keys, mats[2])
-    )
-    grad_start = grad_start + times_transposed(grad_values, mats[3])
-    grad_embedded, gain_zero, gain_one = jax.vjp(layer_norm, embedded, gains[0], gains[1])[1](
-        grad_start
-    )
-    grad_mats = jnp.stack(
+    token_y = send(travel(token_core, "core", grad_place), "y")
+    features_low, grad_place = after((features_low, grad_place), *token_y[1])
+    box_part = jnp.stack(
         [
             contract_rows(features_low, grad_place),
-            contract_rows(act, grad_query),
-            contract_rows(act, grad_keys),
-            contract_rows(act, grad_values),
             contract_rows(place, grad_box_query),
             contract_rows(place, grad_box_key),
-            grad_output,
         ]
-    )
-    grad_mats = reduce_weight(grad_mats, lines, order)
+    ).astype(BFLOAT)
+    box_core = send(by_owner(box_part, lines), "core")
+    up_y = send(travel(up_x, "x", box_core[1][0]), "y")
+    box_x = send(travel(box_core, "core", up_y[1][0]), "x")
+    down_sum = travel(down_z, "z", box_x[1][0])[:, 0, 0, 0]
     grad_vectors = jnp.stack(
         [
             gain_zero,
@@ -429,18 +593,31 @@
             column_sum(grad_feed),
         ]
     )
-    layer_grads = (grad_mats, grad_up[0], grad_down[0], grad_vectors, column_sum(grad_upper))
-    return (layer_grads, grad_embedded)
+    small = jnp.concatenate([grad_vectors.reshape(-1), grad_bias[0]])
+    returned = after(returned, down_sum, small)
+    lookup_rows = over_copies(returned)
+    small = after(small, returned)
+    token_x = send(travel(token_y, "y", returned), "x")
+    up_z = send(travel(up_y, "y", token_x[1][0]), "z")
+    box_y = send(travel(box_x, "x", token_x[1][0]), "y")
+    token_z = send(travel(token_x, "x", box_y[1][0]), "z")
+    box_z = send(travel(box_y, "y", token_z[1][0]), "z")
+    grad_down = both_copies(down_sum, lines)
+    up_half = travel(up_z, "z", box_y[1][0])[:, 0, 0, 0]
+    token_half = travel(token_z, "z", box_z[1][0])[:, 0, 0, 0]
+    box_half = travel(box_z, "z")[:, 0, 0, 0]
+    grad_up = gather_line(up_half, lines["x"], 2)
+    token_mats = gather_line(token_half, lines["x"], 2)
+    box_mats = gather_line(box_half, lines["x"], 2)
+    grad_mats = jnp.concatenate([box_mats[:1], token_mats[:3], box_mats[1:], token_mats[3:]])
+    layer_grads = (grad_mats.astype(FLOAT), grad_up[0].astype(FLOAT), grad_down[0], small)
+    return (layer_grads, lookup_rows, parts)
 
 
 def combine_mass(first, second):
     peak = jnp.maximum(first[0], second[0])
     mass = first[1] * jnp.exp(first[0] - peak) + second[1] * jnp.exp(second[0] - peak)
-    return (peak, mass, first[2] + second[2])
-
-
-def add_trees(first, second):
-    return jax.tree.map(jnp.add, first, second)
+    return jnp.stack([peak, mass, first[2] + second[2]])
 
 
 def body(
@@ -475,7 +652,6 @@
     groups, copies = lax.axis_size("fsdp"), lax.axis_size("rep")
     group, copy = lax.axis_index("fsdp"), lax.axis_index("rep")
     lines = lines_of(groups, copies)
-    depth = mats.shape[0]
     table_low = table.astype(BFLOAT)
 
     capacity = 16 + -(-tokens // (16 * groups)) * 16
@@ -516,7 +692,10 @@
         (jnp.int32(1), embedded),
     )[1]
 
-    mats_low = mats.astype(BFLOAT)
+    own_labels = labels_all - group * shard_rows
+    label_rows = product(one_hot(own_labels, shard_rows), table_low)
+    embedded = after(embedded, label_rows)
+
     small = jnp.concatenate([vectors.astype(BFLOAT).reshape(-1), up_bias.astype(BFLOAT)])[None]
 
     def lay(first, second, bit):
@@ -532,23 +711,17 @@
     gains = small[:, :split].reshape(groups, vectors.shape[0], -1)
     gains = jnp.transpose(gains, (1, 0, 2)).reshape(vectors.shape[0], width).astype(FLOAT)
     bias = small[:, split:].reshape(-1).astype(FLOAT)
-    box_mats = gather_weight(
-        jnp.stack([mats_low[0], mats_low[4], mats_low[5]]), lines, ("z", "x", "y", "core")
-    )
-    token_mats = gather_weight(mats_low[1:4], lines, ("z", "y", "x", "core"))
-    out_mat = gather_weight(mats_low[6:7], lines, ("z", "y", "x", "core"))
-    up_low = gather_weight(up.astype(BFLOAT)[None], lines, ("z", "x", "y", "core"))[0]
-    down_low = gather_weight(down.astype(BFLOAT)[None], lines, ("z", "y", "x", "core"))[0]
-    layer_mats = (
-        box_mats[0],
-        token_mats[0],
-        token_mats[1],
-        token_mats[2],
-        box_mats[1],
-        box_mats[2],
-        out_mat[0],
-    )
-    weights = (layer_mats, up_low, down_low, gains, bias)
+    gains, bias = lax.optimization_barrier((gains, bias))
+    rows, hidden = up.shape
+    blocks = hidden // width
+    up_blocks = jnp.transpose(up.astype(BFLOAT).reshape(rows, blocks, width), (1, 0, 2))
+    down_blocks = down.astype(BFLOAT).reshape(blocks, rows, width)
+    packed = jnp.concatenate([up_blocks, down_blocks, mats.astype(BFLOAT)])
+    packed = lax.all_gather(packed, "fsdp", axis=1, tiled=True)
+    layer_mats = packed[2 * blocks :]
+    down_low = packed[blocks : 2 * blocks].reshape(blocks, groups, rows, width)
+    down_low = jnp.transpose(down_low, (1, 0, 2, 3)).reshape(hidden, width)
+    weights = (layer_mats, packed, down_low, gains, bias)
 
     features_low = box_features(boxes, width).astype(BFLOAT)
     place = (product(features_low, layer_mats[0]) + gains[9]).astype(BFLOAT)
@@ -563,13 +736,13 @@
     for axis, name in enumerate(("z", "y", "core")):
         rows_all = gather_line(rows_all, lines[name], axis)
     rows_all = rows_all.reshape(-1, width)
-    logits = times_transposed(rows_all, table_low)
-    mine = labels_all[:, None] - group * shard_rows == jnp.arange(shard_rows)[None, :]
-    peak = jnp.max(logits, axis=1)
-    mass = jnp.sum(jnp.exp(logits - peak[:, None]), axis=1)
-    target = jnp.sum(jnp.where(mine, logits, 0.0), axis=1)
-    peak, mass, target = paired((peak, mass, target), "fsdp", combine_mass)
+    expo, stats = head_logits(rows_all, table_low, own_labels)
+    peak_here = stats[0]
+    products = product(expo, table_low)
+    stats = paired(stats[:3].reshape(3, -1, LANES), "fsdp", combine_mass).reshape(3, -1)
+    peak, mass, target = stats
     log_total = peak + jnp.log(mass)
+    factor = jnp.exp(peak_here - log_total)
 
     is_token = jnp.arange(slot_count) < M_TOK
     valid_all = valid_slots(lengths_all.reshape(-1), slot_count).astype(FLOAT)
@@ -585,55 +758,65 @@
     loss_parts = jnp.stack([sums[0], count_token, sums[1], count_area])
     share = jnp.where(is_token, 1.0 / count_token, 1.0 / count_area)
     weight = (valid * share[None, :]).reshape(-1)
-    grad_logits = (jnp.exp(logits - log_total[:, None]) - mine.astype(FLOAT)).astype(BFLOAT)
-    grad_rows = product(grad_logits, table_low) * weight[:, None]
+    grad_rows = (products * factor[:, None] - label_rows) * weight[:, None]
     grad_rows = grad_rows.reshape(
         lines["z"].count, lines["y"].count, lines["core"].count, -1, width
     )
-    for axis, name in ((2, "core"), (1, "y"), (0, "z")):
-        grad_rows = reduce_line(grad_rows.astype(BFLOAT), lines[name], axis)
-    grad_rows = grad_rows.reshape(-1, width)
-    head_grad = contract_rows(
-        grad_logits, (rows_all.astype(FLOAT) * weight[:, None]).astype(BFLOAT)
-    ).astype(BFLOAT)
-    if copies == 2:
-        head_grad = head_grad.astype(FLOAT) + swap(head_grad, lines["x"]).astype(FLOAT)
-    else:
-        head_grad = lax.psum(head_grad, "rep").astype(FLOAT)
+    own, blocks = sends(grad_rows, lines["core"], 2)
+    weighted = (rows_all.astype(FLOAT) * weight[:, None]).astype(BFLOAT)
+    expo, weighted = after((expo, weighted), *blocks)
+    mine = own_labels[:, None] == jnp.arange(shard_rows)[None, :]
+    grad_logits = expo.astype(FLOAT) * factor[:, None] - mine.astype(FLOAT)
+    own, blocks = sends(received(own, blocks, lines["core"]), lines["y"], 1)
+    grad_logits = after(grad_logits.astype(BFLOAT), *blocks)
+    head_low = contract_rows(grad_logits, weighted).astype(BFLOAT)
+    own, blocks = sends(received(own, blocks, lines["y"]), lines["z"], 0)
+    blocks = list(after(tuple(blocks), head_low))
+    grad_rows = received(own, blocks, lines["z"]).reshape(-1, width)
+    head_parts = [from_other_copies(part, lines) for part in jnp.split(head_low, 4)]
+    grad_rows = after(grad_rows, head_parts[0])
     grad_top = sum(contract_rows(pick, part) for part in two_parts(grad_rows))
 
-    layer_grads, grad_embedded = layer_backward(
-        weights, features_low, lengths, kept, grad_top, lines
-    )
-    mats_grad, up_grad, down_grad, vectors_sum, bias_sum = layer_grads
-    vectors_sum, bias_sum = paired(
-        paired((vectors_sum, bias_sum), "fsdp", add_trees), "rep", add_trees
-    )
+    def compacted(spots, parts):
+        spread = one_hot(spots, groups * capacity)
+        return sum(contract_rows(spread, part) for part in parts).astype(BFLOAT)
+
+    def give(rows):
+        rows = lax.all_to_all(rows.reshape(groups, capacity, width), "fsdp", 0, 0, tiled=True)
+        return rows.reshape(1, groups * capacity, width)
+
+    def over_copies(rows):
+        return gather_line(rows, lines["x"], 0)
+
+    tools = (lambda parts: compacted(places, parts), give, over_copies)
+    layer_grads, lookup_rows, embedded_parts = layer_backward(
+        weights, features_low, lengths, kept, grad_top, head_parts, lines, tools
+    )
+    mats_grad, up_grad, down_grad, small_sum = layer_grads
+    small_sum = paired(small_sum.reshape(-1, LANES), "fsdp", jnp.add)
+    small_sum = paired(small_sum, "rep", jnp.add).reshape(-1)
+    vectors_sum = small_sum[: vectors.shape[0] * width].reshape(-1, width)
+    bias_sum = small_sum[vectors.shape[0] * width :]
     vectors_grad = lax.dynamic_slice_in_dim(
         vectors_sum, group * vectors.shape[1], vectors.shape[1], 1
     )
     bias_grad = lax.dynamic_slice_in_dim(bias_sum, group * up_bias.shape[0], up_bias.shape[0], 0)
-
-    embedded_parts = two_parts(grad_embedded)
-
-    def give(spots):
-        spread = one_hot(spots, groups * capacity)
-        rows = sum(contract_rows(spread, part) for part in embedded_parts).astype(BFLOAT)
-        rows = lax.all_to_all(rows.reshape(groups, capacity, width), "fsdp", 0, 0, tiled=True)
-        return gather_line(rows.reshape(1, groups * capacity, width), lines["x"], 0)
 
     def spread_rows(wanted, rows):
         return contract_rows(
             one_hot(wanted.reshape(-1), shard_rows), rows.reshape(-1, width)
         )
 
-    table_grad = head_grad + spread_rows(asked, give(places))
+    head_grad = head_low.astype(FLOAT) + jnp.concatenate(head_parts).astype(FLOAT)
+    table_grad = head_grad + spread_rows(asked, lookup_rows)
 
     def another(state):
         turn, total = state
         spots, wanted = ask(turn)
         wanted = gather_line(wanted[None], lines["x"], 0)
-        return turn + 1, total + spread_rows(wanted, give(spots))
+        return turn + 1, total + spread_rows(
+            wanted, over_copies(give(compacted(spots, embedded_parts)))
+        )
 
     table_grad = lax.while_loop(lambda state: state[0] < turns, another, (jnp.int32(1), table_grad))[1]
 

time: 826 us -> 658 us (0.80)
  starting transfers between devices: 211 us -> 118 us
  Pallas kernels: 30.2 us -> 69.7 us
  local copies, waits for them, and re-layouts: 85.8 us -> 46.3 us
  other arithmetic: 123 us -> 90.5 us
  matrix products: 110 us -> 80.9 us
  waiting for transfers between devices: 237 us -> 215 us
  between operations: 16.7 us -> 28.7 us
    ppermute x93 -> x42, waiting for transfers between devices: 219 us -> 101 us  [shifted(): return lax.ppermute(value, line.axis, pairs)]
    ppermute x93 -> x42, starting transfers between devices: 143 us -> 70 us  [shifted(): return lax.ppermute(value, line.axis, pairs)]
    pallas_call x0 -> x3, Pallas kernels: none -> 39.6 us  [the longest x1 15.7 us: feed_backward(): pl.pallas_call(feed_back_kernel, grid=(hidden // width,), in_specs=[whole...]
    all_to_all x1, waiting for transfers between devices: 0.01 us -> 33.6 us  [fetch(): lax.all_to_all(rows.reshape(groups, capacity, width), 'fsdp', 0, 0, tiled...]
    ppermute x27 -> x14, waiting for transfers between devices: 16.7 us -> 44.9 us  [paired(): lax.ppermute(v, axis, pairs)]
    all_gather x0 -> x1, waiting for transfers between devices: none -> 25 us  [body(): packed = lax.all_gather(packed, 'fsdp', axis=1, tiled=True)]
    unnamed x348 -> x263, local copies, waits for them, and re-layouts: 37.9 us -> 16.3 us
    select_n x27 -> x7, other arithmetic: 23.6 us -> 4.35 us  [gather_line(): lax.select_n(here, *[pieces[(i - place) % count] for i in range(count)])]
  transfers between devices with their start and end apart: 127 -> 64, of which waited for: 45 -> 31; matrix products, arithmetic and copies ran while one was open for 26% -> 18% of each run, Pallas kernels for 4% -> 3%
where the time goes in v2:
time: 658 us; the launch traced here: 651 us
  waiting for transfers between devices  215 us (33%)
  starting transfers between devices  118 us (18%)
  other arithmetic  90.5 us (14%)
  matrix products  80.9 us (12%)
  Pallas kernels  69.7 us (11%)
  local copies, waits for them, and re-layouts  46.3 us (7%)
  between operations  28.7 us (4%)
    ppermute x42, waiting for transfers between devices, shifted(): return lax.ppermute(value, line.axis, pairs)  101 us
    ppermute x42, starting transfers between devices, shifted(): return lax.ppermute(value, line.axis, pairs)  70 us
    ppermute x14, waiting for transfers between devices, paired(): lax.ppermute(v, axis, pairs)  44.9 us
    dot_general x12, matrix products, product(): return jnp.dot(left, right, preferred_element_type=FLOAT)  42.5 us
    all_to_all x1, waiting for transfers between devices, fetch(): lax.all_to_all(rows.reshape(groups, capacity, width), 'fsdp', 0, 0, tiled...  33.6 us
    pallas_call x2, Pallas kernels, attention_call(): pl.pallas_call(kernel, grid=(pages, width // LANES), in_specs=[pl.BlockSp...  30.1 us
    dot_general x13, matrix products, contract_rows(): lax.dot_general(left, right, (((0,), (0,)), ((), ())), preferred_element_...  27 us
    ppermute x14, starting transfers between devices, paired(): lax.ppermute(v, axis, pairs)  25 us
  transfers between devices with their start and end apart: 64, of which 31 were waited for; matrix products, arithmetic and copies ran while one was open for 18% of the time, Pallas kernels for 3%

profile of v2, /device:TPU:0, one launch (start us, length us, event | category | flops | bytes accessed | tf_op | source)
XLA Modules:
  0.0 650.6 jit_solution(195609693952121780)
XLA Ops:
  37.7 7.8 %all-to-all-done.4 = s32[32,1,178]{2,1,0:T(1,128)S(1)} async-done(((s32[32,1,178]{2,1,0:T(1,128)}), s32[32,1,178]{2,1,0:T(1,128)S(1)}, u32[]{:S(2)}, u32[]{:S(2)}) %all-to-all-start.4) | async-done | bytes 22816 | tf_op jit(solution)/shard_map/all_to_all | solution.py:669
  49.4 4.6 all-to-all-start.5
  55.5 9.0 %fusion.14 = f32[2048,768]{1,0:T(8,128)} fusion(bf16[1920,768]{1,0:T(8,128)(2,1)S(1)} %convert_element_type.417.table_ref, s32[2048]{0:T(1024)S(1)} %bitcast.315), kind=kOutput, calls=%fused_computation.31 | convolution fusion | flops 6043729920 | bytes 9248768 | tf_op jit(solution)/shard_map/dot_general | solution.py:161
  64.5 33.6 %all-to-all-done.5 = bf16[16,48,768]{2,1,0:T(8,128)(2,1)} async-done(((bf16[16,48,768]{2,1,0:T(8,128)(2,1)}), bf16[16,48,768]{2,1,0:T(8,128)(2,1)}, u32[]{:S(2)}, u32[]{:S(2)}) %all-to-all-start.5) | async-done | bytes 1179680 | tf_op jit(solution)/shard_map/all_to_all | solution.py:680
  101.5 25.0 %all-gather.2.cloned.1.call-done.up_ref = bf16[15,768,768]{2,1,0:T(8,128)(2,1)} async-done(((bf16[15,48,768]{2,1,0:T(8,128)(2,1)}), bf16[15,768,768]{2,1,0:T(8,128)(2,1)}) %all-gather.2.cloned.1.call-update) | async-done | bytes 17694736 | tf_op jit(solution)/shard_map/all_gather | solution.py:720
  140.3 11.6 %shard_map.388 = bf16[512,768]{1,0:T(8,128)(2,1)S(1)} custom-call(s32[1]{0:T(128)} %copy.137.length_ref, bf16[512,768]{1,0:T(8,128)(2,1)S(1)} %add_convert_fusion.14.query_ref, bf16[512,768]{1,0:T(8,128)(2,1)S(1)} %convolution_convert_fusion.11.key_ref, bf16[512,768]{1,0:T(8,128)(2,1)S(1)} %add_convert_fusion.13.value_ref, ...), custom_call_target="tpu_custom_call" | custom-call | tf_op jit(solution)/shard_map/pallas_call | solution.py:264
  160.4 11.2 %shard_map.389 = (bf16[512,3072]{1,0:T(8,128)(2,1)S(1)}, f32[512,3072]{1,0:T(8,128)}, f32[512,768]{1,0:T(8,128)S(1)}) custom-call(bf16[512,768]{1,0:T(8,128)(2,1)S(1)} %fusion.25.middle_ref, bf16[15,768,768]{2,1,0:T(8,128)(2,1)} %all-gather.2.cloned.1.call-done.up_ref, f32[1,3072]{1,0:T(1,128)S(1)} %bitcast.261, bf16[3072,768]{1,0:T(8,128)(2,1)} %bitcast.269), custom_call_target="tpu_custom_call" | custom-call | tf_op jit(solution)/shard_map/pallas_call | solution.py:332
  174.4 7.8 %collective-permute-start.6 = (bf16[1,1,1,128,768]{4,3,2,1,0:T(8,128)(2,1)S(1)}, bf16[1,1,1,128,768]{4,3,2,1,0:T(8,128)(2,1)S(1)}, u32[]{:S(2)}, u32[]{:S(2)}) collective-permute-start(bf16[1,1,1,128,768]{4,3,2,1,0:T(8,128)(2,1)S(1)} %fusion.28), channel_id=1, source_target_pairs={{0,8},{2,10},{4,12},{6,14},{8,16},{10,18},{12,20},{14,22},{16,24},... | collective-permute-start | bytes 589832 | tf_op jit(solution)/shard_map/ppermute | solution.py:59
  187.4 6.5 %collective-permute-done.7 = bf16[1,1,1,128,768]{4,3,2,1,0:T(8,128)(2,1)S(1)} collective-permute-done((bf16[1,1,1,128,768]{4,3,2,1,0:T(8,128)(2,1)S(1)}, bf16[1,1,1,128,768]{4,3,2,1,0:T(8,128)(2,1)S(1)}, u32[]{:S(2)}, u32[]{:S(2)}) %collective-permute-start.7) | collective-permute-done | bytes 196640 | tf_op jit(solution)/shard_map/ppermute | solution.py:59
  196.8 17.5 %collective-permute-done.9 = bf16[4,1,1,128,768]{4,3,2,1,0:T(8,128)(2,1)S(1)} collective-permute-done((bf16[4,1,1,128,768]{4,3,2,1,0:T(8,128)(2,1)S(1)}, bf16[4,1,1,128,768]{4,3,2,1,0:T(8,128)(2,1)S(1)}, u32[]{:S(2)}, u32[]{:S(2)}) %collective-permute-start.9) | collective-permute-done | bytes 786464 | tf_op jit(solution)/shard_map/ppermute | solution.py:59
  222.1 12.7 %shard_map.390 = (bf16[2048,1920]{1,0:T(8,128)(2,1)}, f32[8,2048]{1,0:T(8,128)S(1)}) custom-call(bf16[2048,768]{1,0:T(8,128)(2,1)S(1)} %bitcast.260, bf16[1920,768]{1,0:T(8,128)(2,1)S(1)} %copy-done.24, s32[2048,1]{1,0:T(8,128)S(1)} %copy-done.2), custom_call_target="tpu_custom_call" | custom-call | tf_op jit(solution)/shard_map/pallas_call | solution.py:428
  239.9 4.7 collective-permute-start.13
  251.8 10.8 %subtract_multiply_fusion = f32[2048,768]{1,0:T(8,128)S(1)} fusion(f32[2048,768]{1,0:T(8,128)} %fusion.14, bf16[2048,1920]{1,0:T(8,128)(2,1)} %get-tuple-element.256, bf16[1920,768]{1,0:T(8,128)(2,1)} %get-tuple-element.688, f32[2048]{0:T(1024)S(1)} %fusion.105, f32[2048]{0:T(1024)S(1)} %fusion.94), kind=kOutput, calls=%fused_computation.35 | convolution fusion | flops 6044516352 | bytes 23412736 | tf_op jit(solution)/shard_map/dot_general | solution.py:161
  265.8 3.9 subtract_convert_fusion
  271.8 6.6 %convolution_convert_fusion = bf16[1920,768]{1,0:T(8,128)(2,1)S(1)} fusion(bf16[2048,1920]{1,0:T(8,128)(2,1)S(1)} %subtract_convert_fusion, bf16[2048,768]{1,0:T(8,128)(2,1)S(1)} %multiply_convert_fusion), kind=kOutput, calls=%fused_computation.50 | convolution fusion | flops 6041272320 | bytes 13959168 | tf_op jit(solution)/shard_map/dot_general | solution.py:165
  282.2 5.6 collective-permute-done.20
  294.0 4.4 collective-permute-done.21
  298.4 5.0 collective-permute-done.22
  307.4 15.7 %shard_map.391 = (bf16[768,3072]{1,0:T(8,128)(2,1)}, bf16[3072,768]{1,0:T(8,128)(2,1)}, f32[1,3072]{1,0:T(1,128)S(1)}, f32[512,768]{1,0:T(8,128)S(1)}) custom-call(bf16[512,768]{1,0:T(8,128)(2,1)S(1)} %get-tuple-element.400.grad_ref, bf16[512,768]{1,0:T(8,128)(2,1)S(1)} %copy-done.1, bf16[512,3072]{1,0:T(8,128)(2,1)} %copy-done.3, ...), custom_call_target="tpu_custom_call" | custom-call | tf_op jit(solution)/shard_map/pallas_call | solution.py:384
  331.9 14.2 %collective-permute-done.17 = bf16[480,768]{1,0:T(8,128)(2,1)} collective-permute-done((bf16[480,768]{1,0:T(8,128)(2,1)}, bf16[480,768]{1,0:T(8,128)(2,1)}, u32[]{:S(2)}, u32[]{:S(2)}) %collective-permute-start.17) | collective-permute-done | bytes 737312 | tf_op jit(solution)/shard_map/ppermute | solution.py:59
  362.5 18.5 %shard_map.392 = (bf16[512,768]{1,0:T(8,128)(2,1)S(1)}, bf16[512,768]{1,0:T(8,128)(2,1)S(1)}, bf16[512,768]{1,0:T(8,128)(2,1)S(1)}, bf16[512,768]{1,0:T(8,128)(2,1)S(1)}, bf16[512,768]{1,0:T(8,128)(2,1)S(1)}) custom-call(s32[1]{0:T(128)} %copy.137.length_ref, bf16[512,768]{1,0:T(8,128)(2,1)S(1)} %copy-done.10, bf16[512,768]{1,0:T(8,128)(2,1)S(1)} %copy-done.7, ...), custom_call_target="tpu_custom_call" | custom-call | tf_op jit(solution)/shard_map/pallas_call | solution.py:264
  412.2 6.7 %all-to-all-start.6 = ((bf16[16,48,768]{2,1,0:T(8,128)(2,1)}), bf16[16,48,768]{2,1,0:T(8,128)(2,1)S(1)}, u32[]{:S(2)}, u32[]{:S(2)}) async-start(bf16[16,48,768]{2,1,0:T(8,128)(2,1)} %bitcast.297), calls=%async_computation.6 | async-start | bytes 2359296 | tf_op jit(solution)/shard_map/all_to_all | solution.py:785
  430.2 5.2 collective-permute-start.29
  439.6 10.4 %collective-permute-done.27 = bf16[1,1,1,1,192,768]{5,4,3,2,1,0:T(8,128)(2,1)} collective-permute-done((bf16[1,1,1,1,192,768]{5,4,3,2,1,0:T(8,128)(2,1)}, bf16[1,1,1,1,192,768]{5,4,3,2,1,0:T(8,128)(2,1)}, u32[]{:S(2)}, u32[]{:S(2)}) %collective-permute-start.27) | collective-permute-done | bytes 294944 | tf_op jit(solution)/shard_map/ppermute | solution.py:59
  450.0 17.9 %collective-permute-done.28 = bf16[1,1,1,1,192,768]{5,4,3,2,1,0:T(8,128)(2,1)} collective-permute-done((bf16[1,1,1,1,192,768]{5,4,3,2,1,0:T(8,128)(2,1)}, bf16[1,1,1,1,192,768]{5,4,3,2,1,0:T(8,128)(2,1)}, u32[]{:S(2)}, u32[]{:S(2)}) %collective-permute-start.28) | collective-permute-done | bytes 294944 | tf_op jit(solution)/shard_map/ppermute | solution.py:59
  477.8 10.5 %collective-permute-done.53 = f32[90,128]{1,0:T(8,128)S(1)} collective-permute-done((f32[90,128]{1,0:T(8,128)S(1)}, f32[90,128]{1,0:T(8,128)S(1)}, u32[]{:S(2)}, u32[]{:S(2)}) %collective-permute-start.53) | collective-permute-done | bytes 46112 | tf_op jit(solution)/shard_map/ppermute | solution.py:106
  488.3 6.4 collective-permute-start.54
  506.1 21.3 %collective-permute-done.56 = f32[90,128]{1,0:T(8,128)S(1)} collective-permute-done((f32[90,128]{1,0:T(8,128)S(1)}, f32[90,128]{1,0:T(8,128)S(1)}, u32[]{:S(2)}, u32[]{:S(2)}) %collective-permute-start.56) | collective-permute-done | bytes 46112 | tf_op jit(solution)/shard_map/ppermute | solution.py:106
  528.8 5.4 collective-permute-start.48
  545.2 10.8 %collective-permute-done.37 = bf16[4,4,1,1,48,384]{5,4,0,3,2,1:T(8,128)(2,1)S(1)} collective-permute-done((bf16[4,4,1,1,48,384]{5,4,0,3,2,1:T(8,128)(2,1)S(1)}, bf16[4,4,1,1,48,384]{5,4,0,3,2,1:T(8,128)(2,1)S(1)}, u32[]{:S(2)}, u32[]{:S(2)}) %collective-permute-start.37) | collective-permute-done | bytes 589856 | tf_op jit(solution)/shard_map/ppermute | solution.py:59
  560.6 10.4 %add_add_fusion = f32[1920,768]{1,0:T(8,128)} fusion(bf16[1920,768]{1,0:T(8,128)(2,1)S(1)} %copy-done.43, bf16[480,768]{1,0:T(8,128)(2,1)} %collective-permute-done.19, bf16[480,768]{1,0:T(8,128)(2,1)} %collective-permute-done.18, bf16[480,768]{1,0:T(8,128)(2,1)} %collective-permute-done.17, bf16[480,768]{1,0:T(8,128)(2,1)} %collective-permute-done.16, ...), kind=kOutput, calls=%fused_computation.39 | convolution fusion | flops 4549017600 | bytes 14161920 | tf_op jit(solution)/shard_map/dot_general | solution.py:165
  630.3 8.1 %multiply_subtract_fusion = (f32[1920,768]{1,0:T(8,128)}, f32[1920,768]{1,0:T(8,128)}) fusion(f32[1920,768]{1,0:T(8,128)} %param.30, f32[]{:T(128)} %bitcast.82, f32[768]{0:T(1024)S(1)} %get-tuple-element.466, f32[1920]{0:T(1024)S(1)} %multiply_add_fusion.4, f32[1920,768]{1,0:T(8,128)} %get-tuple-element.709, f32[]{:T(128)S(6)} %min.13), kind=kLoop, calls=%fused_computation.37 | loop fusion | flops 8847360 | bytes 23603720 | tf_op jit(solution)/shard_map/sub | solution.py:866
  (626 shorter events, 272.2 us)
Async XLA Ops:
  7.2 119.2 %all-gather.2.cloned.1.call-start = ((), (), s32[]{:S(2)}) async-start(), calls=%async_computation.7 | async-start | bytes 18800640 | tf_op jit(solution)/shard_map/all_gather | solution.py:720
  49.4 48.7 %all-to-all-start.5 = ((bf16[16,48,768]{2,1,0:T(8,128)(2,1)}), bf16[16,48,768]{2,1,0:T(8,128)(2,1)}, u32[]{:S(2)}, u32[]{:S(2)}) async-start(bf16[16,48,768]{2,1,0:T(8,128)(2,1)} %bitcast.298), calls=%async_computation.5 | async-start | bytes 2359296 | tf_op jit(solution)/shard_map/all_to_all | solution.py:680
  174.4 13.1 %collective-permute-start.6 = (bf16[1,1,1,128,768]{4,3,2,1,0:T(8,128)(2,1)S(1)}, bf16[1,1,1,128,768]{4,3,2,1,0:T(8,128)(2,1)S(1)}, u32[]{:S(2)}, u32[]{:S(2)}) collective-permute-start(bf16[1,1,1,128,768]{4,3,2,1,0:T(8,128)(2,1)S(1)} %fusion.28), channel_id=1, source_target_pairs={{0,8},{2,10},{4,12},{6,14},{8,16},{10,18},{12,20},{14,22},{16,24},... | collective-permute-start | bytes 589832 | tf_op jit(solution)/shard_map/ppermute | solution.py:59
  182.2 13.0 %collective-permute-start.8 = (bf16[1,1,1,128,768]{4,3,2,1,0:T(8,128)(2,1)S(1)}, bf16[1,1,1,128,768]{4,3,2,1,0:T(8,128)(2,1)S(1)}, u32[]{:S(2)}, u32[]{:S(2)}) collective-permute-start(bf16[1,1,1,128,768]{4,3,2,1,0:T(8,128)(2,1)S(1)} %fusion.28), channel_id=1, source_target_pairs={{0,24},{2,26},{4,28},{6,30},{8,0},{10,2},{12,4},{14,6},{16,8},{18,... | collective-permute-start | bytes 589832 | tf_op jit(solution)/shard_map/ppermute | solution.py:59
  195.4 18.9 %collective-permute-start.9 = (bf16[4,1,1,128,768]{4,3,2,1,0:T(8,128)(2,1)S(1)}, bf16[4,1,1,128,768]{4,3,2,1,0:T(8,128)(2,1)S(1)}, u32[]{:S(2)}, u32[]{:S(2)}) collective-permute-start(bf16[4,1,1,128,768]{4,3,2,1,0:T(8,128)(2,1)S(1)} %pad_maximum_fusion.7), channel_id=1, source_target_pairs={{0,4},{2,6},{4,0},{6,2},{8,12},{10,14},{12,8},{14,10},{16,20},{18,... | collective-permute-start | bytes 2359304 | tf_op jit(solution)/shard_map/ppermute | solution.py:59
  270.2 17.7 %collective-permute-start.20 = (bf16[4,1,1,128,768]{4,3,2,1,0:T(8,128)(2,1)S(1)}, bf16[4,1,1,128,768]{4,3,2,1,0:T(8,128)(2,1)S(1)}, u32[]{:S(2)}, u32[]{:S(2)}) collective-permute-start(bf16[4,1,1,128,768]{4,3,2,1,0:T(8,128)(2,1)S(1)} %dynamic-slice_convert_fusion.1), channel_id=1, source_target_pairs={{0,4},{2,6},{4,0},{6,2},{8,12},{10,14},{12,8},{14,10},{16,20},{18,... | collective-permute-start | bytes 2359304 | tf_op jit(solution)/shard_map/ppermute | solution.py:59
  280.7 22.8 %collective-permute-start.16 = (bf16[480,768]{1,0:T(8,128)(2,1)S(1)}, bf16[480,768]{1,0:T(8,128)(2,1)}, u32[]{:S(2)}, u32[]{:S(2)}) collective-permute-start(bf16[480,768]{1,0:T(8,128)(2,1)S(1)} %get-tuple-element.427), channel_id=1, source_target_pairs={{0,1},{1,0},{2,3},{3,2},{4,5},{5,4},{6,7},{7,6},{8,9},{9,8},{10,11... | collective-permute-start | bytes 2211848 | tf_op jit(solution)/shard_map/ppermute | solution.py:59
  290.1 13.3 %collective-permute-start.22 = (bf16[1,1,1,128,768]{4,3,2,1,0:T(8,128)(2,1)S(1)}, bf16[1,1,1,128,768]{4,3,2,1,0:T(8,128)(2,1)S(1)}, u32[]{:S(2)}, u32[]{:S(2)}) collective-permute-start(bf16[1,1,1,128,768]{4,3,2,1,0:T(8,128)(2,1)S(1)} %get-tuple-element.260), channel_id=1, source_target_pairs={{0,16},{2,18},{4,20},{6,22},{8,24},{10,26},{12,28},{14,30},{16,0},... | collective-permute-start | bytes 589832 | tf_op jit(solution)/shard_map/ppermute | solution.py:59
  326.5 22.7 %collective-permute-start.24 = (bf16[1,4,2,1,192,768]{5,4,3,2,1,0:T(8,128)(2,1)}, bf16[1,4,2,1,192,768]{5,4,3,2,1,0:T(8,128)(2,1)}, u32[]{:S(2)}, u32[]{:S(2)}) collective-permute-start(bf16[1,4,2,1,192,768]{5,4,3,2,1,0:T(8,128)(2,1)} %constant_dynamic-slice_fusion.23), channel_id=1, source_target_pairs={{0,2},{2,0},{4,6},{6,4},{8,10},{10,8},{12,14},{14,12},{16,18},{18,... | collective-permute-start | bytes 7077896 | tf_op jit(solution)/shard_map/ppermute | solution.py:59
  326.5 19.6 %collective-permute-start.17 = (bf16[480,768]{1,0:T(8,128)(2,1)}, bf16[480,768]{1,0:T(8,128)(2,1)}, u32[]{:S(2)}, u32[]{:S(2)}) collective-permute-start(bf16[480,768]{1,0:T(8,128)(2,1)} %get-tuple-element.426), channel_id=1, source_target_pairs={{0,1},{1,0},{2,3},{3,2},{4,5},{5,4},{6,7},{7,6},{8,9},{9,8},{10,11... | collective-permute-start | bytes 2211848 | tf_op jit(solution)/shard_map/ppermute | solution.py:59
  329.6 27.7 %collective-permute-start.25 = (bf16[1,4,2,1,48,3072]{5,4,3,2,1,0:T(8,128)(2,1)}, bf16[1,4,2,1,48,3072]{5,4,3,2,1,0:T(8,128)(2,1)}, u32[]{:S(2)}, u32[]{:S(2)}) collective-permute-start(bf16[1,4,2,1,48,3072]{5,4,3,2,1,0:T(8,128)(2,1)} %constant_dynamic-slice_fusion.22), channel_id=1, source_target_pairs={{0,2},{2,0},{4,6},{6,4},{8,10},{10,8},{12,14},{14,12},{16,18},{18,... | collective-permute-start | bytes 7077896 | tf_op jit(solution)/shard_map/ppermute | solution.py:59
  329.9 53.3 %collective-permute-start.18 = (bf16[480,768]{1,0:T(8,128)(2,1)}, bf16[480,768]{1,0:T(8,128)(2,1)}, u32[]{:S(2)}, u32[]{:S(2)}) collective-permute-start(bf16[480,768]{1,0:T(8,128)(2,1)} %get-tuple-element.425), channel_id=1, source_target_pairs={{0,1},{1,0},{2,3},{3,2},{4,5},{5,4},{6,7},{7,6},{8,9},{9,8},{10,11... | collective-permute-start | bytes 2211848 | tf_op jit(solution)/shard_map/ppermute | solution.py:59
  330.4 52.8 %collective-permute-start.19 = (bf16[480,768]{1,0:T(8,128)(2,1)}, bf16[480,768]{1,0:T(8,128)(2,1)}, u32[]{:S(2)}, u32[]{:S(2)}) collective-permute-start(bf16[480,768]{1,0:T(8,128)(2,1)} %get-tuple-element.424), channel_id=1, source_target_pairs={{0,1},{1,0},{2,3},{3,2},{4,5},{5,4},{6,7},{7,6},{8,9},{9,8},{10,11... | collective-permute-start | bytes 2211848 | tf_op jit(solution)/shard_map/ppermute | solution.py:59
  352.7 29.2 %collective-permute-start.26 = (bf16[1,4,1,1,192,768]{5,4,3,2,1,0:T(8,128)(2,1)S(1)}, bf16[1,4,1,1,192,768]{5,4,3,2,1,0:T(8,128)(2,1)S(1)}, u32[]{:S(2)}, u32[]{:S(2)}) collective-permute-start(bf16[1,4,1,1,192,768]{5,4,3,2,1,0:T(8,128)(2,1)S(1)} %constant_dynamic-slice_fusion.21), channel_id=1, source_target_pairs={{0,4},{2,6},{4,0},{6,2},{8,12},{10,14},{12,8},{14,10},{16,20},{18,... | collective-permute-start | bytes 3538952 | tf_op jit(solution)/shard_map/ppermute | solution.py:59
  398.0 28.8 %collective-permute-start.32 = (bf16[1,4,2,1,48,1536]{5,4,3,2,1,0:T(8,128)(2,1)}, bf16[1,4,2,1,48,1536]{5,4,3,2,1,0:T(8,128)(2,1)}, u32[]{:S(2)}, u32[]{:S(2)}) collective-permute-start(bf16[1,4,2,1,48,1536]{5,4,3,2,1,0:T(8,128)(2,1)} %constant_dynamic-slice_fusion.20), channel_id=1, source_target_pairs={{0,1},{1,0},{2,3},{3,2},{4,5},{5,4},{6,7},{7,6},{8,9},{9,8},{10,11... | collective-permute-start | bytes 3538952 | tf_op jit(solution)/shard_map/ppermute | solution.py:59
  408.9 26.5 %collective-permute-start.31 = (bf16[3,4,2,1,48,768]{5,4,0,3,2,1:T(8,128)(2,1)}, bf16[3,4,2,1,48,768]{5,4,0,3,2,1:T(8,128)(2,1)}, u32[]{:S(2)}, u32[]{:S(2)}) collective-permute-start(bf16[3,4,2,1,48,768]{5,4,0,3,2,1:T(8,128)(2,1)} %constant_dynamic-slice_fusion.14), channel_id=1, source_target_pairs={{0,2},{2,0},{4,6},{6,4},{8,10},{10,8},{12,14},{14,12},{16,18},{18,... | collective-permute-start | bytes 5308424 | tf_op jit(solution)/shard_map/ppermute | solution.py:59
  412.2 57.7 %all-to-all-start.6 = ((bf16[16,48,768]{2,1,0:T(8,128)(2,1)}), bf16[16,48,768]{2,1,0:T(8,128)(2,1)S(1)}, u32[]{:S(2)}, u32[]{:S(2)}) async-start(bf16[16,48,768]{2,1,0:T(8,128)(2,1)} %bitcast.297), calls=%async_computation.6 | async-start | bytes 2359296 | tf_op jit(solution)/shard_map/all_to_all | solution.py:785
  420.3 29.7 %collective-permute-start.27 = (bf16[1,1,1,1,192,768]{5,4,3,2,1,0:T(8,128)(2,1)}, bf16[1,1,1,1,192,768]{5,4,3,2,1,0:T(8,128)(2,1)}, u32[]{:S(2)}, u32[]{:S(2)}) collective-permute-start(bf16[1,1,1,1,192,768]{5,4,3,2,1,0:T(8,128)(2,1)} %get-tuple-element.437), channel_id=1, source_target_pairs={{0,8},{2,10},{4,12},{6,14},{8,16},{10,18},{12,20},{14,22},{16,24},... | collective-permute-start | bytes 884744 | tf_op jit(solution)/shard_map/ppermute | solution.py:59
  422.3 45.6 %collective-permute-start.28 = (bf16[1,1,1,1,192,768]{5,4,3,2,1,0:T(8,128)(2,1)}, bf16[1,1,1,1,192,768]{5,4,3,2,1,0:T(8,128)(2,1)}, u32[]{:S(2)}, u32[]{:S(2)}) collective-permute-start(bf16[1,1,1,1,192,768]{5,4,3,2,1,0:T(8,128)(2,1)} %get-tuple-element.436), channel_id=1, source_target_pairs={{0,16},{2,18},{4,20},{6,22},{8,24},{10,26},{12,28},{14,30},{16,0},... | collective-permute-start | bytes 884744 | tf_op jit(solution)/shard_map/ppermute | solution.py:59
  425.2 49.6 %collective-permute-start.35 = (bf16[4,4,1,1,48,768]{5,4,0,3,2,1:T(8,128)(2,1)}, bf16[4,4,1,1,48,768]{5,4,0,3,2,1:T(8,128)(2,1)}, u32[]{:S(2)}, u32[]{:S(2)}) collective-permute-start(bf16[4,4,1,1,48,768]{5,4,0,3,2,1:T(8,128)(2,1)} %constant_dynamic-slice_fusion.15), channel_id=1, source_target_pairs={{0,4},{2,6},{4,0},{6,2},{8,12},{10,14},{12,8},{14,10},{16,20},{18,... | collective-permute-start | bytes 3538952 | tf_op jit(solution)/shard_map/ppermute | solution.py:59
  430.2 37.7 %collective-permute-start.29 = (bf16[1,1,1,1,192,768]{5,4,3,2,1,0:T(8,128)(2,1)}, bf16[1,1,1,1,192,768]{5,4,3,2,1,0:T(8,128)(2,1)S(1)}, u32[]{:S(2)}, u32[]{:S(2)}) collective-permute-start(bf16[1,1,1,1,192,768]{5,4,3,2,1,0:T(8,128)(2,1)} %get-tuple-element.435), channel_id=1, source_target_pairs={{0,24},{2,26},{4,28},{6,30},{8,0},{10,2},{12,4},{14,6},{16,8},{18,... | collective-permute-start | bytes 884744 | tf_op jit(solution)/shard_map/ppermute | solution.py:59
  471.3 25.7 %collective-permute-start.46 = (bf16[1,4,1,1,48,1536]{5,4,3,2,1,0:T(8,128)(2,1)}, bf16[1,4,1,1,48,1536]{5,4,3,2,1,0:T(8,128)(2,1)S(1)}, u32[]{:S(2)}, u32[]{:S(2)}) collective-permute-start(bf16[1,4,1,1,48,1536]{5,4,3,2,1,0:T(8,128)(2,1)} %constant_dynamic-slice_fusion.13), channel_id=1, source_target_pairs={{0,4},{2,6},{4,0},{6,2},{8,12},{10,14},{12,8},{14,10},{16,20},{18,... | collective-permute-start | bytes 1769480 | tf_op jit(solution)/shard_map/ppermute | solution.py:59
  472.8 61.5 %collective-permute-start.51 = (bf16[1,192,768]{2,1,0:T(8,128)(2,1)}, bf16[1,192,768]{2,1,0:T(8,128)(2,1)}, u32[]{:S(2)}, u32[]{:S(2)}) collective-permute-start(bf16[1,192,768]{2,1,0:T(8,128)(2,1)} %fusion.67), channel_id=1, source_target_pairs={{0,1},{1,0},{2,3},{3,2},{4,5},{5,4},{6,7},{7,6},{8,9},{9,8},{10,11... | collective-permute-start | bytes 884744 | tf_op jit(solution)/shard_map/ppermute | solution.py:59
  474.2 64.6 %collective-permute-start.34 = (bf16[3,4,2,1,48,384]{5,4,0,3,2,1:T(8,128)(2,1)}, bf16[3,4,2,1,48,384]{5,4,0,3,2,1:T(8,128)(2,1)}, u32[]{:S(2)}, u32[]{:S(2)}) collective-permute-start(bf16[3,4,2,1,48,384]{5,4,0,3,2,1:T(8,128)(2,1)} %constant_dynamic-slice_fusion.12), channel_id=1, source_target_pairs={{0,1},{1,0},{2,3},{3,2},{4,5},{5,4},{6,7},{7,6},{8,9},{9,8},{10,11... | collective-permute-start | bytes 2654216 | tf_op jit(solution)/shard_map/ppermute | solution.py:59
  495.5 61.8 %collective-permute-start.33 = (bf16[1,768,768]{2,1,0:T(8,128)(2,1)S(1)}, bf16[1,768,768]{2,1,0:T(8,128)(2,1)}, u32[]{:S(2)}, u32[]{:S(2)}) collective-permute-start(bf16[1,768,768]{2,1,0:T(8,128)(2,1)S(1)} %bitcast.280), channel_id=1, source_target_pairs={{0,1},{1,0},{2,3},{3,2},{4,5},{5,4},{6,7},{7,6},{8,9},{9,8},{10,11... | collective-permute-start | bytes 3538952 | tf_op jit(solution)/shard_map/ppermute | solution.py:59
  502.0 25.4 %collective-permute-start.56 = (f32[90,128]{1,0:T(8,128)S(1)}, f32[90,128]{1,0:T(8,128)S(1)}, u32[]{:S(2)}, u32[]{:S(2)}) collective-permute-start(f32[90,128]{1,0:T(8,128)S(1)} %add.863), channel_id=1, source_target_pairs={{0,1},{1,0},{2,3},{3,2},{4,5},{5,4},{6,7},{7,6},{8,9},{9,8},{10,11... | collective-permute-start | bytes 138248 | tf_op jit(solution)/shard_map/ppermute | solution.py:106
  504.1 38.3 %collective-permute-start.47 = (bf16[1,1,1,1,48,1536]{5,4,3,2,1,0:T(8,128)(2,1)}, bf16[1,1,1,1,48,1536]{5,4,3,2,1,0:T(8,128)(2,1)S(1)}, u32[]{:S(2)}, u32[]{:S(2)}) collective-permute-start(bf16[1,1,1,1,48,1536]{5,4,3,2,1,0:T(8,128)(2,1)} %get-tuple-element.446), channel_id=1, source_target_pairs={{0,8},{2,10},{4,12},{6,14},{8,16},{10,18},{12,20},{14,22},{16,24},... | collective-permute-start | bytes 442376 | tf_op jit(solution)/shard_map/ppermute | solution.py:59
  528.8 14.2 %collective-permute-start.48 = (bf16[1,1,1,1,48,1536]{5,4,3,2,1,0:T(8,128)(2,1)}, bf16[1,1,1,1,48,1536]{5,4,3,2,1,0:T(8,128)(2,1)S(1)}, u32[]{:S(2)}, u32[]{:S(2)}) collective-permute-start(bf16[1,1,1,1,48,1536]{5,4,3,2,1,0:T(8,128)(2,1)} %get-tuple-element.445), channel_id=1, source_target_pairs={{0,16},{2,18},{4,20},{6,22},{8,24},{10,26},{12,28},{14,30},{16,0},... | collective-permute-start | bytes 442376 | tf_op jit(solution)/shard_map/ppermute | solution.py:59
  540.2 15.8 %collective-permute-start.37 = (bf16[4,4,1,1,48,384]{5,4,0,3,2,1:T(8,128)(2,1)S(1)}, bf16[4,4,1,1,48,384]{5,4,0,3,2,1:T(8,128)(2,1)S(1)}, u32[]{:S(2)}, u32[]{:S(2)}) collective-permute-start(bf16[4,4,1,1,48,384]{5,4,0,3,2,1:T(8,128)(2,1)S(1)} %copy-done.62), channel_id=1, source_target_pairs={{0,1},{1,0},{2,3},{3,2},{4,5},{5,4},{6,7},{7,6},{8,9},{9,8},{10,11... | collective-permute-start | bytes 1769480 | tf_op jit(solution)/shard_map/ppermute | solution.py:59
  542.5 38.0 %collective-permute-start.36 = (bf16[3,4,1,1,48,384]{5,4,0,3,2,1:T(8,128)(2,1)}, bf16[3,4,1,1,48,384]{5,4,0,3,2,1:T(8,128)(2,1)}, u32[]{:S(2)}, u32[]{:S(2)}) collective-permute-start(bf16[3,4,1,1,48,384]{5,4,0,3,2,1:T(8,128)(2,1)} %constant_dynamic-slice_fusion.10), channel_id=1, source_target_pairs={{0,4},{2,6},{4,0},{6,2},{8,12},{10,14},{12,8},{14,10},{16,20},{18,... | collective-permute-start | bytes 1327112 | tf_op jit(solution)/shard_map/ppermute | solution.py:59
  544.6 31.2 %collective-permute-start.50 = (bf16[1,48,1536]{2,1,0:T(8,128)(2,1)}, bf16[1,48,1536]{2,1,0:T(8,128)(2,1)}, u32[]{:S(2)}, u32[]{:S(2)}) collective-permute-start(bf16[1,48,1536]{2,1,0:T(8,128)(2,1)} %fusion.71), channel_id=1, source_target_pairs={{0,1},{1,0},{2,3},{3,2},{4,5},{5,4},{6,7},{7,6},{8,9},{9,8},{10,11... | collective-permute-start | bytes 442376 | tf_op jit(solution)/shard_map/ppermute | solution.py:59
  557.1 25.2 %collective-permute-start.42 = (bf16[4,1,1,1,48,384]{5,4,0,3,2,1:T(8,128)(2,1)}, bf16[4,1,1,1,48,384]{5,4,0,3,2,1:T(8,128)(2,1)}, u32[]{:S(2)}, u32[]{:S(2)}) collective-permute-start(bf16[4,1,1,1,48,384]{5,4,0,3,2,1:T(8,128)(2,1)} %get-tuple-element.449), channel_id=1, source_target_pairs={{0,8},{2,10},{4,12},{6,14},{8,16},{10,18},{12,20},{14,22},{16,24},... | collective-permute-start | bytes 442376 | tf_op jit(solution)/shard_map/ppermute | solution.py:59
  (163 other events, 1899.5 us)
Sparse Core Ops, SparseCore 0:
  10.1 116.2 all-gather.1

commit v3 on v2

v3 whole, which is shorter than its diff:
```python
import math
from typing import NamedTuple

import jax
import jax.numpy as jnp
from jax import lax
from jax.experimental import pallas as pl
from jax.experimental.pallas import tpu as pltpu
from jax.sharding import PartitionSpec as P

HEAD_DIM = 64
PAGE_LEN = 512
M_TOK = 64
M_AREA = 64
STEP = 10


EPSILON = 1e-05
CLIP_NORM = 0.1
LEARN_RATE = 0.02
VECTOR_RATE = 0.3
TINY_TERM = 1e-30
NEGATIVE = -1e30
BFLOAT = jnp.bfloat16
FLOAT = jnp.float32
LANES = 128
DECAY = 1.0 - STEP ** (-0.8)


class Line(NamedTuple):
    axis: str
    total: int
    stride: int
    count: int


def lines_of(groups, copies):
    cores = min(2, groups)
    rest = (groups // cores).bit_length() - 1
    y_count = 1 << (rest // 2)
    z_count = groups // (cores * y_count)
    return {
        "z": Line("fsdp", groups, cores * y_count, z_count),
        "y": Line("fsdp", groups, cores, y_count),
        "core": Line("fsdp", groups, 1, cores),
        "x": Line("rep", copies, 1, copies),
    }


def place_on(line):
    return lax.axis_index(line.axis) // line.stride % line.count


def shifted(value, line, step):
    pairs = []
    for i in range(line.total):
        place = i // line.stride % line.count
        pairs.append((i, i + ((place + step) % line.count - place) * line.stride))
    return lax.ppermute(value, line.axis, pairs)


def gather_line(value, line, axis):
    count = line.count
    if count == 1:
        return value
    here = place_on(line)
    pieces = [value] + [shifted(value, line, step) for step in range(1, count)]
    blocks = []
    for place in range(count):
        blocks.append(lax.select_n(here, *[pieces[(i - place) % count] for i in range(count)]))
    return jnp.concatenate(blocks, axis=axis)


def sends(value, line, axis):
    size = value.shape[axis] // line.count
    here = place_on(line)

    def block(place):
        return lax.dynamic_slice_in_dim(value, place * size, size, axis)

    return block(here), [
        block((here + step) % line.count).astype(BFLOAT) for step in range(1, line.count)
    ]


def received(own, blocks, line):
    total = own.astype(FLOAT)
    for step, value in enumerate(blocks, 1):
        total = total + shifted(value, line, step).astype(FLOAT)
    return total


def reduce_line(value, line, axis):
    return received(*sends(value, line, axis), line)


def after(value, *others):
    return lax.optimization_barrier((value, *others))[0]


def paired(value, axis, combine, beside=None):
    size = lax.axis_size(axis)
    bit = 1
    while bit < size:
        pairs = [(i, i ^ bit) for i in range(size)]
        other = lax.ppermute(value, axis, pairs)
        if beside is not None and bit == 2:
            other = after(other, beside)
        value = combine(value, other)
        bit *= 2
    return value


def by_owner(value, lines):
    count, _, columns = value.shape
    return value.reshape(count, lines["z"].count, lines["y"].count, lines["core"].count, -1, columns)


AXES = {"z": 1, "y": 2, "core": 3, "x": 5}


def part_sends(value, lines, name):
    return sends(value, lines[name], AXES[name])


def part_received(pair, lines, name):
    return received(*pair, lines[name]).astype(BFLOAT)


def both_copies(value, lines):
    if lines["x"].count == 2:
        return value.astype(FLOAT) + shifted(value, lines["x"], 1).astype(FLOAT)
    return lax.psum(value, "rep").astype(FLOAT)


def from_other_copies(value, lines):
    if lines["x"].count == 2:
        return shifted(value, lines["x"], 1)
    return (lax.psum(value, "rep").astype(FLOAT) - value.astype(FLOAT)).astype(BFLOAT)


def layer_norm(value, gain, shift):
    center = value - jnp.mean(value, axis=-1, keepdims=True)
    spread = jnp.mean(center * center, axis=-1, keepdims=True)
    return center * lax.rsqrt(spread + EPSILON) * gain + shift


def box_features(boxes, width):
    count = width // 8
    freqs = jnp.exp(-math.log(10000.0) * jnp.arange(count, dtype=FLOAT) / count)
    angle = boxes.astype(FLOAT)[:, :, None] * freqs[None, None, :]
    waves = jnp.concatenate([jnp.sin(angle), jnp.cos(angle)], axis=2)
    return jnp.transpose(waves, (1, 0, 2)).reshape(boxes.shape[1], width)


def valid_slots(lengths, slot_count):
    n_tok = jnp.minimum(M_TOK, 1 + lengths * M_TOK // PAGE_LEN)
    n_area = jnp.minimum(M_AREA, 1 + lengths * (3 * M_AREA) // (4 * PAGE_LEN))
    index = jnp.arange(slot_count, dtype=jnp.int32)[None, :]
    return jnp.where(index < M_TOK, index < n_tok[:, None], index - M_TOK < n_area[:, None])


def product(left, right):
    return jnp.dot(left, right, preferred_element_type=FLOAT)


def contract_rows(left, right):
    return lax.dot_general(left, right, (((0,), (0,)), ((), ())), preferred_element_type=FLOAT)


def times_transposed(left, right):
    return lax.dot_general(left, right, (((1,), (1,)), ((), ())), preferred_element_type=FLOAT)


def two_parts(value):
    high = value.astype(BFLOAT)
    return high, (value - high.astype(FLOAT)).astype(BFLOAT)


def side(index):
    lane = lax.broadcasted_iota(jnp.int32, (1, LANES), 1)
    return lane // HEAD_DIM == index


def only(mask, value):
    return jnp.where(mask, value, jnp.zeros_like(value))


def attend_kernel(length_ref, query_ref, key_ref, value_ref, box_query_ref, box_key_ref, out_ref):
    length = length_ref[pl.program_id(0)]
    query, key, box_query, box_key = query_ref[...], key_ref[...], box_query_ref[...], box_key_ref[...]
    keys = jnp.concatenate([key, box_key, key], axis=1)
    keep = lax.broadcasted_iota(jnp.int32, (1, key.shape[0]), 1) < length
    scale = jnp.asarray(HEAD_DIM ** (-0.5), BFLOAT)
    mixed = jnp.zeros(out_ref.shape, FLOAT)
    for head in range(LANES // HEAD_DIM):
        mask = side(head)
        own = only(mask, query) * scale
        other = only(mask, box_query) * scale
        score = times_transposed(jnp.concatenate([own, own, other], axis=1), keys)
        score = jnp.where(keep, score, NEGATIVE)
        expo = jnp.exp(score - jnp.max(score, axis=1, keepdims=True))
        prob = (expo * (1.0 / jnp.sum(expo, axis=1, keepdims=True))).astype(BFLOAT)
        mixed = jnp.where(mask, product(prob, value_ref[...]), mixed)
    out_ref[...] = mixed.astype(BFLOAT)


def attend_back_kernel(
    length_ref, query_ref, key_ref, value_ref, box_query_ref, box_key_ref, grad_ref, out_ref
):
    length = length_ref[pl.program_id(0)]
    query, key, value, box_query, box_key = (
        query_ref[...],
        key_ref[...],
        value_ref[...],
        box_query_ref[...],
        box_key_ref[...],
    )
    grad = grad_ref[...]
    rows = key.shape[0]
    keys = jnp.concatenate([key, box_key, key], axis=1)
    both_queries = jnp.concatenate([query, box_query], axis=1)
    both_keys = jnp.concatenate([key, box_key], axis=1)
    keep = lax.broadcasted_iota(jnp.int32, (rows, 1), 0) < length
    scale = jnp.asarray(HEAD_DIM ** (-0.5), BFLOAT)
    outs = [jnp.zeros((rows, LANES), FLOAT) for _ in range(5)]
    for head in range(LANES // HEAD_DIM):
        mask = side(head)
        own = only(mask, query) * scale
        other = only(mask, box_query) * scale
        score = times_transposed(keys, jnp.concatenate([own, own, other], axis=1))
        score = jnp.where(keep, score, NEGATIVE)
        expo = jnp.exp(score - jnp.max(score, axis=0, keepdims=True))
        prob = expo * (1.0 / jnp.sum(expo, axis=0, keepdims=True))
        grad_value = product(prob.astype(BFLOAT), grad)
        grad_prob = times_transposed(only(mask, value), grad)
        grad_score = prob * (grad_prob - jnp.sum(prob * grad_prob, axis=0, keepdims=True))
        low = grad_score.astype(BFLOAT) * scale
        with_queries = product(low, both_queries)
        with_keys = contract_rows(low, both_keys)
        fresh = (
            with_keys[:, :LANES] + with_keys[:, LANES:],
            with_queries[:, :LANES] + with_queries[:, LANES:],
            grad_value,
            with_keys[:, :LANES],
            with_queries[:, :LANES],
        )
        outs = [jnp.where(mask, new, old) for new, old in zip(fresh, outs)]
    for index, out in enumerate(outs):
        out_ref[index] = out.astype(BFLOAT)


FREE = pl.CostEstimate(flops=0, transcendentals=0, bytes_accessed=0)


ROOMY = pltpu.CompilerParams(vmem_limit_bytes=48 * 1024 * 1024)


def attention_call(kernel, lengths, arrays, stacked):
    tokens, width = arrays[0].shape
    pages = lengths.shape[0]
    spec = pl.BlockSpec((tokens // pages, LANES), lambda page, pair: (page, pair))
    out_spec, shape = spec, (tokens, width)
    if stacked:
        shape = (stacked, tokens, width)
        out_spec = pl.BlockSpec(
            (stacked, tokens // pages, LANES), lambda page, pair: (0, page, pair)
        )
    return pl.pallas_call(
        kernel,
        grid=(pages, width // LANES),
        in_specs=[pl.BlockSpec(memory_space=pltpu.SMEM)] + [spec] * len(arrays),
        out_specs=out_spec,
        out_shape=jax.ShapeDtypeStruct(shape, BFLOAT),
        compiler_params=ROOMY,
        cost_estimate=FREE,
    )(lengths, *arrays)


def start_kernel(first_ref, grad_ref, mat_ref, out_ref, place_ref, sums_ref, total):
    step = pl.program_id(0)
    grad = grad_ref[...]
    term = times_transposed(grad, mat_ref[...])
    sums_ref[...] = jnp.sum(grad.astype(FLOAT), axis=0, keepdims=True)

    @pl.when(step == 0)
    def _():
        total[...] = term

    @pl.when(step == 1)
    def _():
        low = (total[...] + term).astype(BFLOAT)
        place_ref[...] = low
        sums_ref[...] = jnp.sum(low.astype(FLOAT), axis=0, keepdims=True)

    @pl.when(step == 2)
    def _():
        out_ref[...] = first_ref[...] + term

    @pl.when(step > 2)
    def _():
        out_ref[...] += term


def start_gradient(grad_first, pieces, packed, first_mat):
    tokens, width = grad_first.shape
    whole = pl.BlockSpec((tokens, width), lambda k: (0, 0))

    def piece(k):
        return jnp.where(k < 2, k + 3, k - 2)

    def mat(k):
        return first_mat + jnp.where(k < 2, k + 4, k - 1)

    return pl.pallas_call(
        start_kernel,
        grid=(5,),
        in_specs=[
            whole,
            pl.BlockSpec((None, tokens, width), lambda k: (piece(k), 0, 0)),
            pl.BlockSpec((None, width, width), lambda k: (mat(k), 0, 0)),
        ],
        out_specs=[whole, whole, pl.BlockSpec((None, 1, width), lambda k: (k, 0, 0))],
        out_shape=[
            jax.ShapeDtypeStruct((tokens, width), FLOAT),
            jax.ShapeDtypeStruct((tokens, width), BFLOAT),
            jax.ShapeDtypeStruct((5, 1, width), FLOAT),
        ],
        scratch_shapes=[pltpu.VMEM((tokens, width), FLOAT)],
        compiler_params=ROOMY,
        cost_estimate=FREE,
    )(grad_first, pieces, packed)


def token_kernel(act_ref, mixed_ref, grad_ref, attended_ref, out_ref):
    @pl.when(pl.program_id(0) < 3)
    def _():
        out_ref[...] = contract_rows(act_ref[...], grad_ref[...]).astype(BFLOAT)

    @pl.when(pl.program_id(0) == 3)
    def _():
        out_ref[...] = contract_rows(mixed_ref[...], attended_ref[...]).astype(BFLOAT)


def token_gradients(act, mixed, pieces, grad_attended):
    tokens, width = act.shape
    whole = pl.BlockSpec((tokens, width), lambda k: (0, 0))
    return pl.pallas_call(
        token_kernel,
        grid=(4,),
        in_specs=[
            whole,
            whole,
            pl.BlockSpec((None, tokens, width), lambda k: (jnp.minimum(k, 2), 0, 0)),
            whole,
        ],
        out_specs=pl.BlockSpec((None, width, width), lambda k: (k, 0, 0)),
        out_shape=jax.ShapeDtypeStruct((4, width, width), BFLOAT),
        compiler_params=ROOMY,
        cost_estimate=FREE,
    )(act, mixed, pieces, grad_attended)


def box_kernel(features_ref, place_ref, grad_ref, grad_place_ref, out_ref):
    @pl.when(pl.program_id(0) < 2)
    def _():
        out_ref[...] = contract_rows(place_ref[...], grad_ref[...]).astype(BFLOAT)

    @pl.when(pl.program_id(0) == 2)
    def _():
        out_ref[...] = contract_rows(features_ref[...], grad_place_ref[...]).astype(BFLOAT)


def box_gradients(features_low, place, pieces, grad_place):
    tokens, width = place.shape
    whole = pl.BlockSpec((tokens, width), lambda k: (0, 0))
    return pl.pallas_call(
        box_kernel,
        grid=(3,),
        in_specs=[
            whole,
            whole,
            pl.BlockSpec((None, tokens, width), lambda k: (jnp.minimum(k, 1) + 3, 0, 0)),
            whole,
        ],
        out_specs=pl.BlockSpec((None, width, width), lambda k: (k, 0, 0)),
        out_shape=jax.ShapeDtypeStruct((3, width, width), BFLOAT),
        compiler_params=ROOMY,
        cost_estimate=FREE,
    )(features_low, place, pieces, grad_place)


class Buckets(NamedTuple):
    owner: jax.Array
    row: jax.Array
    first: jax.Array
    rank: jax.Array
    fullest: jax.Array


def bucket_ids(ids, shard_rows):
    owner, row = ids // shard_rows, ids % shard_rows
    index = jnp.arange(ids.shape[0], dtype=jnp.int32)
    earlier = index[None, :] < index[:, None]
    same = ids[:, None] == ids[None, :]
    first = ~jnp.any(same & earlier, axis=1)
    before = (owner[:, None] == owner[None, :]) & earlier & first[None, :]
    rank = jnp.sum(before.astype(jnp.int32), axis=1)
    rank = jnp.sum(jnp.where(same & first[None, :], rank[None, :], 0), axis=1)
    return Buckets(owner, row, first, rank, jnp.max(rank) + 1)


def bucket_places(buckets, capacity, stride, turn):
    shifted = buckets.rank - turn * capacity
    inside = (shifted >= 0) & (shifted < capacity)
    return jnp.where(inside, buckets.owner * stride + shifted, -1)


def bucket_requests(buckets, places, groups, stride):
    hit = (places[:, None] == jnp.arange(groups * stride)[None, :]) & buckets.first[:, None]
    rows = jnp.sum(jnp.where(hit, buckets.row[:, None] + 1, 0), axis=0) - 1
    return rows.reshape(groups, stride)


def one_hot(index, count):
    return (index[:, None] == jnp.arange(count, dtype=jnp.int32)[None, :]).astype(BFLOAT)


def feed_kernel(middle_ref, up_ref, bias_ref, down_ref, active_ref, slope_ref, out_ref):
    value = product(middle_ref[...], up_ref[...]) + bias_ref[...]
    share = 0.5 * (1.0 + lax.erf(value * math.sqrt(0.5)))
    density = jnp.exp(-0.5 * value * value) * (1.0 / math.sqrt(2.0 * math.pi))
    active = (value * share).astype(BFLOAT)
    active_ref[...] = active
    slope_ref[...] = share + value * density
    out = product(active, down_ref[...])

    @pl.when(pl.program_id(0) == 0)
    def _():
        out_ref[...] = out

    @pl.when(pl.program_id(0) > 0)
    def _():
        out_ref[...] += out


def feed_forward(middle_low, packed, bias):
    tokens, width = middle_low.shape
    hidden = bias.shape[0]
    blocks = hidden // width
    whole = pl.BlockSpec((tokens, width), lambda j: (0, 0))
    columns = pl.BlockSpec((tokens, width), lambda j: (0, j))
    return pl.pallas_call(
        feed_kernel,
        grid=(blocks,),
        in_specs=[
            whole,
            pl.BlockSpec((None, width, width), lambda j: (j, 0, 0)),
            pl.BlockSpec((1, width), lambda j: (0, j)),
            pl.BlockSpec((None, width, width), lambda j: (blocks + j, 0, 0)),
        ],
        out_specs=[columns, columns, whole],
        out_shape=[
            jax.ShapeDtypeStruct((tokens, hidden), BFLOAT),
            jax.ShapeDtypeStruct((tokens, hidden), FLOAT),
            jax.ShapeDtypeStruct((tokens, width), FLOAT),
        ],
        compiler_params=ROOMY,
        cost_estimate=FREE,
    )(middle_low, packed, bias[None], packed)


def feed_back_kernel(
    grad_ref,
    middle_ref,
    active_ref,
    slope_ref,
    up_ref,
    down_ref,
    grads_ref,
    grad_bias_ref,
    out_ref,
):
    grad = grad_ref[...]
    grad_upper = (times_transposed(grad, down_ref[...]) * slope_ref[...]).astype(BFLOAT)
    grad_bias_ref[...] = jnp.sum(grad_upper.astype(FLOAT), axis=0, keepdims=True)
    grads_ref[0] = contract_rows(middle_ref[...], grad_upper).astype(BFLOAT)
    grads_ref[1] = contract_rows(active_ref[...], grad).astype(BFLOAT)
    out = times_transposed(grad_upper, up_ref[...])

    @pl.when(pl.program_id(0) == 0)
    def _():
        out_ref[...] = out

    @pl.when(pl.program_id(0) > 0)
    def _():
        out_ref[...] += out


def feed_backward(grad_feed, middle_low, active, slope, packed):
    tokens, width = middle_low.shape
    hidden = active.shape[1]
    blocks = hidden // width
    whole = pl.BlockSpec((tokens, width), lambda j: (0, 0))
    columns = pl.BlockSpec((tokens, width), lambda j: (0, j))
    return pl.pallas_call(
        feed_back_kernel,
        grid=(blocks,),
        in_specs=[
            whole,
            whole,
            columns,
            columns,
            pl.BlockSpec((None, width, width), lambda j: (j, 0, 0)),
            pl.BlockSpec((None, width, width), lambda j: (blocks + j, 0, 0)),
        ],
        out_specs=[
            pl.BlockSpec((2, None, width, width), lambda j: (0, j, 0, 0)),
            pl.BlockSpec((1, width), lambda j: (0, j)),
            whole,
        ],
        out_shape=[
            jax.ShapeDtypeStruct((2, blocks, width, width), BFLOAT),
            jax.ShapeDtypeStruct((1, hidden), FLOAT),
            jax.ShapeDtypeStruct((tokens, width), FLOAT),
        ],
        compiler_params=ROOMY,
        cost_estimate=FREE,
    )(grad_feed, middle_low, active, slope, packed, packed)


def logits_kernel(rows_ref, table_ref, label_ref, expo_ref, stats_ref):
    logits = times_transposed(rows_ref[...], table_ref[...])
    peak = jnp.max(logits, axis=1, keepdims=True)
    expo = jnp.exp(logits - peak)
    expo_ref[...] = expo.astype(BFLOAT)
    mass = jnp.sum(expo, axis=1, keepdims=True)
    column = lax.broadcasted_iota(jnp.int32, logits.shape, 1)
    target = jnp.sum(jnp.where(column == label_ref[...], logits, 0.0), axis=1, keepdims=True)
    lane = lax.broadcasted_iota(jnp.int32, (logits.shape[0], LANES), 1)
    stats = jnp.where(lane == 0, peak, jnp.where(lane == 1, mass, target))
    stats_ref[...] = stats.T[:8]


def head_logits(rows_all, table_low, own_labels):
    count, width = rows_all.shape
    shard_rows = table_low.shape[0]
    step = 256
    return pl.pallas_call(
        logits_kernel,
        grid=(count // step,),
        in_specs=[
            pl.BlockSpec((step, width), lambda i: (i, 0)),
            pl.BlockSpec((shard_rows, width), lambda i: (0, 0)),
            pl.BlockSpec((step, 1), lambda i: (i, 0)),
        ],
        out_specs=[
            pl.BlockSpec((step, shard_rows), lambda i: (i, 0)),
            pl.BlockSpec((8, step), lambda i: (0, i)),
        ],
        out_shape=[
            jax.ShapeDtypeStruct((count, shard_rows), BFLOAT),
            jax.ShapeDtypeStruct((8, count), FLOAT),
        ],
        compiler_params=ROOMY,
        cost_estimate=FREE,
    )(rows_all, table_low, own_labels[:, None])


def column_sum(value):
    return jnp.sum(value.astype(FLOAT), axis=0)


def layer_forward(weights, embedded, place, box_query, box_key, lengths):
    mats, packed, gains, up_bias = weights
    start_state = layer_norm(embedded, gains[0], gains[1])
    act = start_state.astype(BFLOAT)
    query = (product(act, mats[1]) + gains[6]).astype(BFLOAT)
    keys = product(act, mats[2]).astype(BFLOAT)
    values = (product(act, mats[3]) + gains[7]).astype(BFLOAT)
    mixed = attention_call(attend_kernel, lengths, (query, keys, values, box_query, box_key), 0)
    first_sum = start_state + (product(mixed, mats[6]) + gains[8])
    middle = layer_norm(first_sum, gains[2], gains[3])
    middle_low = middle.astype(BFLOAT)
    active, slope, feed = feed_forward(middle_low, packed, up_bias)
    second_sum = middle + (feed + gains[10])
    kept = (
        embedded,
        act,
        place,
        query,
        keys,
        values,
        box_query,
        box_key,
        mixed,
        first_sum,
        middle_low,
        slope,
        active,
        second_sum,
    )
    return (layer_norm(second_sum, gains[4], gains[5]), kept)


def layer_backward(weights, features_low, lengths, kept, grad_out, head_parts, lines, tools):
    mats, packed, gains, up_bias = weights
    (
        embedded,
        act,
        place,
        query,
        keys,
        values,
        box_query,
        box_key,
        mixed,
        first_sum,
        middle_low,
        slope,
        active,
        second_sum,
    ) = kept
    compacted, give, from_copies, give_rows = tools

    def send(value, name):
        own, blocks = sends(value, lines[name], AXES[name])
        return own, blocks

    def travel(pair, name, *until):
        line = lines[name]
        moved = [shifted(block, line, step) for step, block in enumerate(pair[1], 1)]
        if until:
            moved = list(after(tuple(moved), *until))
        total = pair[0].astype(FLOAT)
        for value in moved:
            total = total + value.astype(FLOAT)
        return total.astype(BFLOAT)

    grad_second, gain_four, gain_five = jax.vjp(layer_norm, second_sum, gains[4], gains[5])[1](
        grad_out
    )
    grad_feed = grad_second.astype(BFLOAT)
    grad_feeds, grad_bias, fed_back = feed_backward(grad_feed, middle_low, active, slope, packed)
    feeds_sum = lax.psum_scatter(grad_feeds, "fsdp", scatter_dimension=2, tiled=True)
    grad_first, gain_two, gain_three = jax.vjp(layer_norm, first_sum, gains[2], gains[3])[1](
        grad_second + fed_back
    )
    grad_attended = grad_first.astype(BFLOAT)
    grad_mixed = times_transposed(grad_attended, mats[6]).astype(BFLOAT)
    pieces = attention_call(
        attend_back_kernel, lengths, (query, keys, values, box_query, box_key, grad_mixed), 5
    )
    pieces = after(pieces, head_parts[2])
    first_mat = packed.shape[0] - mats.shape[0]
    grad_start, grad_place, sums = start_gradient(grad_first, pieces, packed, first_mat)
    grad_start = after(grad_start, head_parts[3])
    grad_embedded, gain_zero, gain_one = jax.vjp(layer_norm, embedded, gains[0], gains[1])[1](
        grad_start
    )
    grad_vectors = jnp.stack(
        [
            gain_zero,
            gain_one,
            gain_two,
            gain_three,
            gain_four,
            gain_five,
            sums[2, 0],
            sums[4, 0],
            column_sum(grad_attended),
            sums[1, 0],
            column_sum(grad_feed),
        ]
    )
    parts = two_parts(grad_embedded)
    compact = compacted(parts, grad_vectors, grad_bias)
    returned = give(compact)
    pieces = after(pieces, compact)
    token_part = token_gradients(act, mixed, pieces, grad_attended)
    token_core = send(by_owner(token_part, lines), "core")
    pieces = after(pieces, *token_core[1])
    box_part = box_gradients(features_low, place, pieces, grad_place)
    token_y = send(travel(token_core, "core", box_part), "y")
    box_part = after(box_part, *token_y[1])
    box_core = send(by_owner(box_part, lines), "core")
    box_x = send(travel(box_core, "core"), "x")
    returned = after(returned, *box_x[1])
    rows = from_copies(returned)
    feeds_sum = after(feeds_sum, returned)
    others = after(tuple(rows[1:]), feeds_sum)
    token_z = send(travel(token_y, "y", feeds_sum), "z")
    box_y = send(travel(box_x, "x", token_z[1][0]), "y")
    spread = [give_rows(0, after(rows[0], *box_y[1]))]
    token_sum = travel(token_z, "z", spread[0])[:, 0, 0, 0]
    box_z = send(travel(box_y, "y", token_sum), "z")
    others = after(others, *box_z[1])
    spread += [give_rows(index, value) for index, value in enumerate(others, 1)]
    box_half = travel(box_z, "z", spread[-1])[:, 0, 0, 0]
    feeds_other = after(from_other_copies(feeds_sum, lines), box_half)
    feeds_sum = feeds_sum.astype(FLOAT) + feeds_other.astype(FLOAT)
    token_mats = both_copies(token_sum, lines)
    box_mats = gather_line(box_half, lines["x"], 2).astype(FLOAT)
    grad_mats = jnp.concatenate([box_mats[2:], token_mats[:3], box_mats[:2], token_mats[3:]])
    return ((grad_mats, feeds_sum), spread, [rows[0], *others], parts)


def combine_mass(first, second):
    peak = jnp.maximum(first[0], second[0])
    mass = first[1] * jnp.exp(first[0] - peak) + second[1] * jnp.exp(second[0] - peak)
    return jnp.stack([peak, mass, first[2] + second[2]])


def body(
    token_ids,
    boxes,
    lengths,
    slots,
    labels,
    table,
    mats,
    up,
    down,
    vectors,
    up_bias,
    table_rows,
    table_cols,
    mats_rows,
    mats_cols,
    up_rows,
    up_cols,
    down_rows,
    down_cols,
    vectors_second,
    up_bias_second,
):
    pages = lengths.shape[0]
    tokens = token_ids.shape[0]
    page_len = tokens // pages
    width = table.shape[1]
    shard_rows = table.shape[0]
    slot_count = slots.shape[1]
    groups, copies = lax.axis_size("fsdp"), lax.axis_size("rep")
    group, copy = lax.axis_index("fsdp"), lax.axis_index("rep")
    lines = lines_of(groups, copies)
    table_low = table.astype(BFLOAT)

    own_small = vectors.size + up_bias.size
    small_rows = -(-own_small // width)
    stride = 16 + -(-tokens // (16 * groups)) * 16
    capacity = stride - 2 * small_rows
    buckets = bucket_ids(token_ids, shard_rows)
    places = bucket_places(buckets, capacity, stride, 0)
    requests = bucket_requests(buckets, places, groups, stride)
    own_news = jnp.concatenate([labels.reshape(-1), lengths, buckets.fullest[None]])
    news = jnp.concatenate(
        [
            jnp.repeat(requests, copies, axis=0),
            jnp.broadcast_to(own_news[None], (groups * copies, own_news.shape[0])),
        ],
        axis=1,
    )
    news = lax.all_to_all(news, ("fsdp", "rep"), 0, 0, tiled=True)
    asked = news[:, :stride].reshape(groups, copies, stride)
    asked = jnp.transpose(asked, (1, 0, 2)).reshape(copies, groups * stride)
    labels_all = news[:, stride : stride + pages * slot_count]
    labels_all = labels_all.reshape(groups, copies, pages * slot_count)
    labels_all = lax.dynamic_index_in_dim(labels_all, copy, 1, False).reshape(-1)
    lengths_all = news[:, stride + pages * slot_count : -1]
    turns = (jnp.max(news[:, -1]) + capacity - 1) // capacity

    def fetch(spots, wanted):
        rows = product(one_hot(wanted, shard_rows), table_low).astype(BFLOAT)
        rows = lax.all_to_all(rows.reshape(groups, stride, width), "fsdp", 0, 0, tiled=True)
        return product(one_hot(spots, groups * stride), rows.reshape(groups * stride, width))

    def ask(turn):
        spots = bucket_places(buckets, capacity, stride, turn)
        wanted = bucket_requests(buckets, spots, groups, stride)
        return spots, lax.all_to_all(wanted, "fsdp", 0, 0, tiled=True).reshape(-1)

    embedded = fetch(places, lax.dynamic_index_in_dim(asked, copy, 0, False))
    embedded = lax.while_loop(
        lambda state: state[0] < turns,
        lambda state: (state[0] + 1, state[1] + fetch(*ask(state[0]))),
        (jnp.int32(1), embedded),
    )[1]

    own_labels = labels_all - group * shard_rows
    label_rows = product(one_hot(own_labels, shard_rows), table_low).astype(BFLOAT)
    embedded = after(embedded, label_rows)

    small = jnp.concatenate([vectors.astype(BFLOAT).reshape(-1), up_bias.astype(BFLOAT)])[None]

    def lay(first, second, bit):
        low = (group & bit) == 0
        return jnp.concatenate([jnp.where(low, first, second), jnp.where(low, second, first)])

    bit = 1
    while bit < groups:
        pairs = [(i, i ^ bit) for i in range(groups)]
        small = lay(small, lax.ppermute(small, "fsdp", pairs), bit)
        bit *= 2
    split = vectors.size
    gains = small[:, :split].reshape(groups, vectors.shape[0], -1)
    gains = jnp.transpose(gains, (1, 0, 2)).reshape(vectors.shape[0], width).astype(FLOAT)
    own_rows, hidden = up.shape
    feed_blocks = hidden // width
    bias = small[:, split:].reshape(groups, feed_blocks, own_rows)
    bias = jnp.transpose(bias, (1, 0, 2)).reshape(-1).astype(FLOAT)
    gains, bias = lax.optimization_barrier((gains, bias))
    up_blocks = up.astype(BFLOAT).reshape(own_rows, groups, feed_blocks, own_rows)
    up_blocks = jnp.transpose(up_blocks, (2, 0, 1, 3)).reshape(feed_blocks, own_rows, width)
    down_blocks = down.astype(BFLOAT).reshape(feed_blocks, own_rows, width)
    packed = jnp.concatenate([up_blocks, down_blocks, mats.astype(BFLOAT)])
    packed = lax.all_gather(packed, "fsdp", axis=1, tiled=True)
    layer_mats = packed[2 * feed_blocks :]
    weights = (layer_mats, packed, gains, bias)

    features_low = box_features(boxes, width).astype(BFLOAT)
    place = (product(features_low, layer_mats[0]) + gains[9]).astype(BFLOAT)
    box_query = product(place, layer_mats[4]).astype(BFLOAT)
    box_key = product(place, layer_mats[5]).astype(BFLOAT)
    top_state, kept = layer_forward(weights, embedded, place, box_query, box_key, lengths)

    where_at = slots * lengths[:, None] // 256 + jnp.arange(pages)[:, None] * page_len
    pick = one_hot(where_at.reshape(-1), tokens)
    rows_low = product(pick, top_state.astype(BFLOAT)).astype(BFLOAT)
    rows_all = rows_low[None, None, None]
    for axis, name in enumerate(("z", "y", "core")):
        rows_all = gather_line(rows_all, lines[name], axis)
    rows_all = rows_all.reshape(-1, width)
    expo, stats = head_logits(rows_all, table_low, own_labels)
    peak_here = stats[0]
    products = product(expo, table_low)
    stats = stats[:3].reshape(3, -1, LANES)
    stats = paired(stats, "fsdp", combine_mass, products).reshape(3, -1)
    products, peak, mass, target = lax.optimization_barrier((products, *stats))
    log_total = peak + jnp.log(mass)
    factor = jnp.exp(peak_here - log_total)

    is_token = jnp.arange(slot_count) < M_TOK
    valid_all = valid_slots(lengths_all.reshape(-1), slot_count).astype(FLOAT)
    count_token = jnp.sum(jnp.where(is_token, valid_all, 0.0))
    count_area = jnp.sum(jnp.where(is_token, 0.0, valid_all))
    valid = valid_all.reshape(groups, copies, pages, slot_count)
    valid = lax.dynamic_index_in_dim(valid, copy, 1, False).reshape(-1, slot_count)
    loss_rows = (log_total - target).reshape(-1, slot_count) * valid
    token_loss = jnp.sum(jnp.where(is_token, loss_rows, 0.0))
    area_loss = jnp.sum(jnp.where(is_token, 0.0, loss_rows))
    figure = jnp.arange(4)
    losses = paired(jnp.where(figure < 2, token_loss, area_loss), "rep", jnp.add)
    loss_parts = jnp.where(figure == 1, count_token, jnp.where(figure == 3, count_area, losses))
    share = jnp.where(is_token, 1.0 / count_token, 1.0 / count_area)
    weight = (valid * share[None, :]).reshape(-1)
    grad_rows = (products * factor[:, None] - label_rows.astype(FLOAT)) * weight[:, None]
    grad_rows = grad_rows.astype(BFLOAT)
    grad_rows = grad_rows.reshape(
        lines["z"].count, lines["y"].count, lines["core"].count, -1, width
    )
    own, blocks = sends(grad_rows, lines["core"], 2)
    weighted = (rows_all.astype(FLOAT) * weight[:, None]).astype(BFLOAT)
    expo, weighted = after((expo, weighted), *blocks)
    mine = own_labels[:, None] == jnp.arange(shard_rows)[None, :]
    grad_logits = expo.astype(FLOAT) * factor[:, None] - mine.astype(FLOAT)
    own, blocks = sends(received(own, blocks, lines["core"]), lines["y"], 1)
    grad_logits = after(grad_logits.astype(BFLOAT), *blocks)
    head_low = contract_rows(grad_logits, weighted).astype(BFLOAT)
    own, blocks = sends(received(own, blocks, lines["y"]), lines["z"], 0)
    blocks = list(after(tuple(blocks), head_low))
    grad_rows = received(own, blocks, lines["z"]).reshape(-1, width)
    head_parts = [from_other_copies(part, lines) for part in jnp.split(head_low, 4)]
    grad_rows = after(grad_rows, *head_parts[:2])
    grad_top = sum(contract_rows(pick, part) for part in two_parts(grad_rows))

    def compacted(spots, parts):
        spread = one_hot(spots, groups * stride)
        return sum(contract_rows(spread, part) for part in parts)

    def compacted_first(parts, grad_vectors, grad_bias):
        small = grad_vectors.reshape(grad_vectors.shape[0], groups, -1)
        small = jnp.transpose(small, (1, 0, 2)).reshape(groups, -1)
        grad_bias = jnp.transpose(grad_bias.reshape(feed_blocks, groups, own_rows), (1, 0, 2))
        small = jnp.concatenate([small, grad_bias.reshape(groups, -1)], axis=1)
        small = jnp.pad(small, ((0, 0), (0, small_rows * width - own_small)))
        small = jnp.stack(two_parts(small.reshape(groups, small_rows, width)), axis=1)
        small = small.reshape(groups, 2 * small_rows, width).astype(FLOAT)
        small = jnp.pad(small, ((0, 0), (capacity, 0), (0, 0))).reshape(groups * stride, width)
        return (compacted(places, parts) + small).astype(BFLOAT)

    def give(rows):
        rows = lax.all_to_all(rows.reshape(groups, stride, width), "fsdp", 0, 0, tiled=True)
        return rows.reshape(groups * stride, width)

    def spread_rows(wanted, rows):
        return contract_rows(one_hot(wanted, shard_rows), rows)

    def small_sum(rows):
        rows = rows.reshape(groups, stride, width)[:, capacity:].astype(FLOAT)
        rows = jnp.sum(rows, axis=0).reshape(2, small_rows * width)
        return (rows[0] + rows[1])[:own_small]

    if copies == 2:
        from_copies = lambda value: [value, shifted(value, lines["x"], 1)]
        copy_order = [copy, 1 - copy]
    else:
        from_copies = lambda value: list(lax.all_gather(value, "rep"))
        copy_order = list(range(copies))
    asked_of = [lax.dynamic_index_in_dim(asked, index, 0, False) for index in copy_order]

    def give_rows(index, rows):
        return spread_rows(asked_of[index], rows)

    tools = (compacted_first, give, from_copies, give_rows)
    layer_grads, spread, given, embedded_parts = layer_backward(
        weights, features_low, lengths, kept, grad_top, head_parts, lines, tools
    )
    mats_grad, feeds_grad = layer_grads
    up_grad = jnp.transpose(feeds_grad[0].reshape(feed_blocks, own_rows, groups, own_rows), (1, 2, 0, 3))
    up_grad = up_grad.reshape(own_rows, hidden)
    down_grad = feeds_grad[1].reshape(hidden // groups, width)
    small = [small_sum(rows) for rows in given]
    small = sum(small[1:], small[0])
    vectors_grad = small[: vectors.size].reshape(vectors.shape)
    bias_grad = small[vectors.size :]

    head_grad = head_low.astype(FLOAT) + jnp.concatenate(head_parts).astype(FLOAT)
    table_grad = head_grad + sum(spread[1:], spread[0])

    def another(state):
        turn, total = state
        spots, wanted = ask(turn)
        given = from_copies(give(compacted(spots, embedded_parts).astype(BFLOAT)))
        spread = [spread_rows(*pair) for pair in zip(from_copies(wanted), given)]
        return turn + 1, total + sum(spread[1:], spread[0])

    table_grad = lax.while_loop(lambda state: state[0] < turns, another, (jnp.int32(1), table_grad))[1]

    depth = mats.shape[0]
    feed_cols = hidden // width
    sizes = [(shard_rows * groups, width)] + [(mats.shape[1] * groups, width)] * depth
    sizes += [(up.shape[0] * groups, hidden), (down.shape[0] * groups, width)]
    row_squares = [jnp.sum(grad * grad, axis=-1) for grad in (table_grad, mats_grad, up_grad, down_grad)]
    items = depth + 3
    lane = jnp.arange(width)
    singles = jnp.pad(jnp.sum(mats_rows, axis=1), (1, width - 1 - depth))
    for index, value in (
        (0, jnp.sum(table_rows)),
        (items - 2, jnp.sum(up_rows)),
        (items - 1, jnp.sum(down_rows)),
        (items, jnp.sum(vectors_grad * vectors_grad)),
        (items + 1, jnp.sum(bias_grad * bias_grad)),
    ):
        singles = jnp.where(lane == index, value, singles)
    sums = jnp.concatenate(
        [
            jnp.sum(table_grad * table_grad, axis=0)[None],
            jnp.sum(mats_grad * mats_grad, axis=1),
            jnp.sum(up_grad * up_grad, axis=0).reshape(feed_cols, width),
            jnp.sum(down_grad * down_grad, axis=0)[None],
            singles[None],
        ]
    )
    cols_old = jnp.concatenate(
        [table_cols[None], mats_cols, up_cols.reshape(feed_cols, width), down_cols[None]]
    )
    sums = paired(sums, "fsdp", jnp.add)
    totals = jnp.sum(sums[:-1], axis=1)
    norm_square = jnp.sum(totals) + sums[-1, items] + sums[-1, items + 1]
    grad_norm = jnp.sqrt(norm_square)
    clip = jnp.minimum(1.0, CLIP_NORM / grad_norm)
    square = clip * clip

    def renewed(old, value):
        return DECAY * old + (1.0 - DECAY) * (value + TINY_TERM)

    first_up, after_up = 1 + depth, 1 + depth + feed_cols
    of_item = [[k] for k in range(first_up)] + [list(range(first_up, after_up)), [after_up]]
    item_totals = jnp.concatenate(
        [totals[:first_up], jnp.sum(totals[first_up:after_up])[None], totals[after_up:]]
    )
    tall = jnp.array([size[0] for size in sizes], FLOAT)
    wide = jnp.array([size[1] for size in sizes], FLOAT)
    means = renewed(sums[-1, :items] / tall, square * item_totals / (tall * wide))
    repeats = [len(rows) for rows in of_item]
    tall_rows = jnp.array([s for size, n in zip(sizes, repeats) for s in [size[0]] * n], FLOAT)
    mean_rows = jnp.concatenate(
        [means[:first_up], jnp.broadcast_to(means[first_up], (feed_cols,)), means[first_up + 1 :]]
    )
    cols_new = renewed(cols_old, square * sums[:-1] / tall_rows[:, None])
    col_factors = lax.rsqrt(cols_new / mean_rows[:, None])
    step = LEARN_RATE * clip

    def updated(grad, param, rows_old, row_square, col_factor):
        rows_new = renewed(rows_old, square * row_square / grad.shape[-1])
        factor = step * lax.rsqrt(rows_new)
        return grad * clip, rows_new, param - grad * factor[..., None] * col_factor[..., None, :]

    up_factor = col_factors[first_up:after_up].reshape(hidden)
    table_out = updated(table_grad, table, table_rows, row_squares[0], col_factors[0])
    mats_out = updated(mats_grad, mats, mats_rows, row_squares[1], col_factors[1:first_up])
    up_out = updated(up_grad, up, up_rows, row_squares[2], up_factor)
    down_out = updated(down_grad, down, down_rows, row_squares[3], col_factors[after_up])
    clipped_vectors = vectors_grad * clip
    vectors_second_new = DECAY * vectors_second + (1.0 - DECAY) * (
        clipped_vectors * clipped_vectors + TINY_TERM
    )
    vectors_new = vectors - VECTOR_RATE * clipped_vectors * lax.rsqrt(vectors_second_new)
    clipped_bias = bias_grad * clip
    bias_second_new = DECAY * up_bias_second + (1.0 - DECAY) * (
        clipped_bias * clipped_bias + TINY_TERM
    )
    bias_new = up_bias - VECTOR_RATE * clipped_bias * lax.rsqrt(bias_second_new)
    return (
        table_out[0],
        table_out[1],
        cols_new[0],
        table_out[2],
        mats_out[0],
        mats_out[1],
        cols_new[1:first_up],
        mats_out[2],
        up_out[0],
        up_out[1],
        cols_new[first_up:after_up].reshape(hidden),
        up_out[2],
        down_out[0],
        down_out[1],
        cols_new[after_up],
        down_out[2],
        clipped_vectors,
        vectors_second_new,
        vectors_new,
        clipped_bias,
        bias_second_new,
        bias_new,
        grad_norm,
        loss_parts,
    )


def solution(mesh):
    return jax.shard_map(
        body,
        mesh=mesh,
        in_specs=(
            P(("fsdp", "rep")),
            P(None, ("fsdp", "rep")),
            P(("fsdp", "rep")),
            P(("fsdp", "rep"), None),
            P(("fsdp", "rep"), None),
            P("fsdp", None),
            P(None, "fsdp", None),
            P("fsdp", None),
            P("fsdp", None),
            P(None, "fsdp"),
            P("fsdp"),
            P("fsdp"),
            P(),
            P(None, "fsdp"),
            P(),
            P("fsdp"),
            P(),
            P("fsdp"),
            P(),
            P(None, "fsdp"),
            P("fsdp"),
        ),
        out_specs=(
            P("fsdp", None),
            P("fsdp"),
            P(),
            P("fsdp", None),
            P(None, "fsdp", None),
            P(None, "fsdp"),
            P(),
            P(None, "fsdp", None),
            P("fsdp", None),
            P("fsdp"),
            P(),
            P("fsdp", None),
            P("fsdp", None),
            P("fsdp"),
            P(),
            P("fsdp", None),
            P(None, "fsdp"),
            P(None, "fsdp"),
            P(None, "fsdp"),
            P("fsdp"),
            P("fsdp"),
            P("fsdp"),
            P(),
            P(),
        ),
        check_vma=False,
    )
```

time: 658 us -> 597 us (0.907)
  starting transfers between devices: 118 us -> 83.8 us
  waiting for transfers between devices: 215 us -> 185 us
  Pallas kernels: 69.7 us -> 87.5 us
  matrix products: 80.9 us -> 66.3 us
    ppermute x14 -> x9, waiting for transfers between devices: 44.9 us -> 6.44 us  [paired(): other = lax.ppermute(value, axis, pairs)]
    ppermute x42 -> x29, waiting for transfers between devices: 101 us -> 65.1 us  [shifted(): return lax.ppermute(value, line.axis, pairs)]
    reduce_scatter x0 -> x1, waiting for transfers between devices: none -> 30.6 us  [layer_backward(): lax.psum_scatter(grad_feeds, 'fsdp', scatter_dimension=2, tiled=True)]
    ppermute x42 -> x29, starting transfers between devices: 70 us -> 46.5 us  [shifted(): return lax.ppermute(value, line.axis, pairs)]
    pallas_call x2 -> x5, Pallas kernels: 26.9 us -> 45.5 us  [the longest x1 15.8 us: feed_backward(): pl.pallas_call(feed_back_kernel, grid=(blocks,), in_specs=[whole, whole,...]
    all_to_all x2, waiting for transfers between devices: 33.6 us -> 47.6 us  [the longest x1 33.9 us: fetch(): lax.all_to_all(rows.reshape(groups, stride, width), 'fsdp', 0, 0, tiled=T...]
    ppermute x14 -> x9, starting transfers between devices: 25 us -> 14.7 us  [paired(): other = lax.ppermute(value, axis, pairs)]
    dot_general x6 -> x1, matrix products: 11.4 us -> 2.55 us  [times_transposed(): lax.dot_general(left, right, (((1,), (1,)), ((), ())), preferred_element_...]
  transfers between devices with their start and end apart: 64 -> 47, of which waited for: 31 -> 24; matrix products, arithmetic and copies ran while one was open for 18% -> 22% of each run, Pallas kernels for 3% -> 6%
where the time goes in v3:
time: 597 us; the launch traced here: 588 us
  waiting for transfers between devices  185 us (31%)
  other arithmetic  97 us (16%)
  Pallas kernels  87.5 us (15%)
  starting transfers between devices  83.8 us (14%)
  matrix products  66.3 us (11%)
  local copies, waits for them, and re-layouts  45.5 us (8%)
  between operations  22.7 us (4%)
    ppermute x29, waiting for transfers between devices, shifted(): return lax.ppermute(value, line.axis, pairs)  65.1 us
    ppermute x29, starting transfers between devices, shifted(): return lax.ppermute(value, line.axis, pairs)  46.5 us
    dot_general x12, matrix products, product(): return jnp.dot(left, right, preferred_element_type=FLOAT)  41.8 us
    all_to_all x1, waiting for transfers between devices, fetch(): lax.all_to_all(rows.reshape(groups, stride, width), 'fsdp', 0, 0, tiled=T...  33.9 us
    reduce_scatter x1, waiting for transfers between devices, layer_backward(): lax.psum_scatter(grad_feeds, 'fsdp', scatter_dimension=2, tiled=True)  30.6 us
    pallas_call x2, Pallas kernels, attention_call(): pl.pallas_call(kernel, grid=(pages, width // LANES), in_specs=[pl.BlockSp...  29.3 us
    all_gather x1, waiting for transfers between devices, body(): packed = lax.all_gather(packed, 'fsdp', axis=1, tiled=True)  24.2 us
    dot_general x7, matrix products, contract_rows(): lax.dot_general(left, right, (((0,), (0,)), ((), ())), preferred_element_...  21.9 us
  transfers between devices with their start and end apart: 47, of which 24 were waited for; matrix products, arithmetic and copies ran while one was open for 22% of the time, Pallas kernels for 6%

profile of v3, /device:TPU:0, one launch (start us, length us, event | category | flops | bytes accessed | tf_op | source)
XLA Modules:
  0.0 588.0 jit_solution(11632928935145923067)
XLA Ops:
  39.6 7.8 %all-to-all-done.4 = s32[32,1,178]{2,1,0:T(1,128)S(1)} async-done(((s32[32,1,178]{2,1,0:T(1,128)}), s32[32,1,178]{2,1,0:T(1,128)S(1)}, u32[]{:S(2)}, u32[]{:S(2)}) %all-to-all-start.4) | async-done | bytes 22816 | tf_op jit(solution)/shard_map/all_to_all | solution.py:763
  51.9 4.4 all-to-all-start.5
  58.1 8.5 %fusion.20 = bf16[2048,768]{1,0:T(8,128)(2,1)} fusion(bf16[1920,768]{1,0:T(8,128)(2,1)S(1)} %convert_element_type.342.table_ref, s32[2048]{0:T(1024)S(1)} %bitcast.218), kind=kOutput, calls=%fused_computation.47 | convolution fusion | flops 6045302784 | bytes 6103040 | tf_op jit(solution)/shard_map/dot_general | solution.py:164
  66.6 33.9 %all-to-all-done.5 = bf16[16,48,768]{2,1,0:T(8,128)(2,1)} async-done(((bf16[16,48,768]{2,1,0:T(8,128)(2,1)}), bf16[16,48,768]{2,1,0:T(8,128)(2,1)}, u32[]{:S(2)}, u32[]{:S(2)}) %all-to-all-start.5) | async-done | bytes 1179680 | tf_op jit(solution)/shard_map/all_to_all | solution.py:774
  104.1 24.2 %all-gather.2.cloned.1.call-done.up_ref.down_ref.mat_ref = bf16[15,768,768]{2,1,0:T(8,128)(2,1)} async-done(((bf16[15,48,768]{2,1,0:T(8,128)(2,1)}), bf16[15,768,768]{2,1,0:T(8,128)(2,1)}) %all-gather.2.cloned.1.call-update) | async-done | bytes 17694736 | tf_op jit(solution)/shard_map/all_gather | solution.py:816
  142.2 11.6 %shard_map.415.mixed_ref = bf16[512,768]{1,0:T(8,128)(2,1)S(1)} custom-call(s32[1]{0:T(128)} %copy.166.length_ref, bf16[512,768]{1,0:T(8,128)(2,1)S(1)} %add_convert_fusion.8.query_ref, bf16[512,768]{1,0:T(8,128)(2,1)S(1)} %convolution_convert_fusion.4.key_ref, bf16[512,768]{1,0:T(8,128)(2,1)S(1)} %add_convert_fusion.7.value_ref, ...), custom_call_target="tpu_custom_call" | custom-call | tf_op jit(solution)/shard_map/pallas_call | solution.py:269
  157.0 11.2 %shard_map.416 = (bf16[512,3072]{1,0:T(8,128)(2,1)S(1)}, f32[512,3072]{1,0:T(8,128)}, f32[512,768]{1,0:T(8,128)S(1)}) custom-call(bf16[512,768]{1,0:T(8,128)(2,1)S(1)} %fusion.30.middle_ref, bf16[15,768,768]{2,1,0:T(8,128)(2,1)} %all-gather.2.cloned.1.call-done.up_ref.down_ref.mat_ref, f32[1,3072]{1,0:T(1,128)S(1)} %bitcast.188, ...), custom_call_target="tpu_custom_call" | custom-call | tf_op jit(solution)/shard_map/pallas_call | solution.py:453
  171.1 7.8 %collective-permute-start.6 = (bf16[1,1,1,128,768]{4,3,2,1,0:T(8,128)(2,1)S(1)}, bf16[1,1,1,128,768]{4,3,2,1,0:T(8,128)(2,1)S(1)}, u32[]{:S(2)}, u32[]{:S(2)}) collective-permute-start(bf16[1,1,1,128,768]{4,3,2,1,0:T(8,128)(2,1)S(1)} %fusion.31), channel_id=1, source_target_pairs={{0,8},{2,10},{4,12},{6,14},{8,16},{10,18},{12,20},{14,22},{16,24},... | collective-permute-start | bytes 589832 | tf_op jit(solution)/shard_map/ppermute | solution.py:59
  184.1 6.6 %collective-permute-done.7 = bf16[1,1,1,128,768]{4,3,2,1,0:T(8,128)(2,1)S(1)} collective-permute-done((bf16[1,1,1,128,768]{4,3,2,1,0:T(8,128)(2,1)S(1)}, bf16[1,1,1,128,768]{4,3,2,1,0:T(8,128)(2,1)S(1)}, u32[]{:S(2)}, u32[]{:S(2)}) %collective-permute-start.7) | collective-permute-done | bytes 196640 | tf_op jit(solution)/shard_map/ppermute | solution.py:59
  193.5 17.6 %collective-permute-done.9 = bf16[4,1,1,128,768]{4,3,2,1,0:T(8,128)(2,1)S(1)} collective-permute-done((bf16[4,1,1,128,768]{4,3,2,1,0:T(8,128)(2,1)S(1)}, bf16[4,1,1,128,768]{4,3,2,1,0:T(8,128)(2,1)S(1)}, u32[]{:S(2)}, u32[]{:S(2)}) %collective-permute-start.9) | collective-permute-done | bytes 786464 | tf_op jit(solution)/shard_map/ppermute | solution.py:59
  218.8 12.7 %shard_map.417 = (bf16[2048,1920]{1,0:T(8,128)(2,1)}, f32[8,2048]{1,0:T(8,128)S(1)}) custom-call(bf16[2048,768]{1,0:T(8,128)(2,1)S(1)} %bitcast.186, bf16[1920,768]{1,0:T(8,128)(2,1)S(1)} %copy-done.31, s32[2048,1]{1,0:T(8,128)S(1)} %copy-done.2), custom_call_target="tpu_custom_call" | custom-call | tf_op jit(solution)/shard_map/pallas_call | solution.py:549
  234.1 10.6 %fusion.105 = f32[2048,768]{1,0:T(8,128)} fusion(bf16[2048,1920]{1,0:T(8,128)(2,1)} %get-tuple-element.302, bf16[1920,768]{1,0:T(8,128)(2,1)S(1)} %copy-done.31), kind=kOutput, calls=%fused_computation.395 | convolution fusion | flops 6039797760 | bytes 17104896 | tf_op jit(solution)/shard_map/dot_general | solution.py:164
  244.7 5.0 collective-permute-start.13
  257.7 5.8 multiply_convert_fusion.1
  265.2 6.3 %subtract_convert_fusion = bf16[2048,1920]{1,0:T(8,128)(2,1)S(1)} fusion(bf16[2048,1920]{1,0:T(8,128)(2,1)} %get-tuple-element.302, f32[2048]{0:T(1024)S(1)} %get-tuple-element.509, s32[2048]{0:T(1024)S(1)} %bitcast.219), kind=kLoop, calls=%fused_computation.30 | loop fusion | flops 23592960 | bytes 15745024 | tf_op jit(solution)/shard_map/convert_element_type | solution.py:867
  273.4 6.6 %convolution_convert_fusion = bf16[1920,768]{1,0:T(8,128)(2,1)S(1)} fusion(bf16[2048,1920]{1,0:T(8,128)(2,1)S(1)} %subtract_convert_fusion, bf16[2048,768]{1,0:T(8,128)(2,1)S(1)} %copy-done.43), kind=kOutput, calls=%fused_computation.48 | convolution fusion | flops 6041272320 | bytes 13959168 | tf_op jit(solution)/shard_map/dot_general | solution.py:168
  284.0 8.0 %collective-permute-done.20 = bf16[4,1,1,128,768]{4,3,2,1,0:T(8,128)(2,1)S(1)} collective-permute-done((bf16[4,1,1,128,768]{4,3,2,1,0:T(8,128)(2,1)S(1)}, bf16[4,1,1,128,768]{4,3,2,1,0:T(8,128)(2,1)S(1)}, u32[]{:S(2)}, u32[]{:S(2)}) %collective-permute-start.20) | collective-permute-done | bytes 786464 | tf_op jit(solution)/shard_map/ppermute | solution.py:59
  298.8 4.3 collective-permute-done.21
  303.1 7.7 %collective-permute-done.22 = bf16[1,1,1,128,768]{4,3,2,1,0:T(8,128)(2,1)} collective-permute-done((bf16[1,1,1,128,768]{4,3,2,1,0:T(8,128)(2,1)}, bf16[1,1,1,128,768]{4,3,2,1,0:T(8,128)(2,1)}, u32[]{:S(2)}, u32[]{:S(2)}) %collective-permute-start.22) | collective-permute-done | bytes 196640 | tf_op jit(solution)/shard_map/ppermute | solution.py:59
  311.9 4.9 collective-permute-done.17
  320.6 15.8 %shard_map.418 = (bf16[2,4,768,768]{3,2,1,0:T(8,128)(2,1)}, f32[1,3072]{1,0:T(1,128)S(1)}, f32[512,768]{1,0:T(8,128)S(1)}) custom-call(bf16[512,768]{1,0:T(8,128)(2,1)S(1)} %get-tuple-element.439.grad_ref, bf16[512,768]{1,0:T(8,128)(2,1)S(1)} %copy-done.1, bf16[512,3072]{1,0:T(8,128)(2,1)} %copy-done.3, f32[512,3072]{1,0:T(8,128)} %get-tuple-element.310.slope_ref, ...), custom_call_target="tpu_custom_call" | custom-call | tf_op jit(solution)/shard_map/pallas_call | solution.py:506
  344.4 17.8 %shard_map.419.grad_ref = bf16[5,512,768]{2,1,0:T(8,128)(2,1)} custom-call(s32[1]{0:T(128)} %copy.166.length_ref, bf16[512,768]{1,0:T(8,128)(2,1)S(1)} %copy-done.13, bf16[512,768]{1,0:T(8,128)(2,1)S(1)} %copy-done.9, bf16[512,768]{1,0:T(8,128)(2,1)S(1)} %copy-done.11, bf16[512,768]{1,0:T(8,128)(2,1)S(1)} %copy-done.7, bf16[512,768]{1,0:T(8,128)(2,1)S(1)} %copy-done.5, ...), custom_call_target="tpu_custom_call" | custom-call | tf_op jit(solution)/shard_map/pallas_call | solution.py:269
  362.2 8.3 %shard_map.420 = (f32[512,768]{1,0:T(8,128)S(1)}, bf16[512,768]{1,0:T(8,128)(2,1)S(1)}, f32[5,1,768]{2,1,0:T(1,128)S(1)}) custom-call(f32[512,768]{1,0:T(8,128)S(1)} %get-tuple-element.442.first_ref, bf16[5,512,768]{2,1,0:T(8,128)(2,1)} %shard_map.419.grad_ref, bf16[15,768,768]{2,1,0:T(8,128)(2,1)} %all-gather.2.cloned.1.call-done.up_ref.down_ref.mat_ref), custom_call_target="tpu_custom_call" | custom-call | tf_op jit(solution)/shard_map/pallas_call | solution.py:315
  380.0 6.3 %shard_map.421 = bf16[4,768,768]{2,1,0:T(8,128)(2,1)} custom-call(bf16[512,768]{1,0:T(8,128)(2,1)S(1)} %copy-done.17, bf16[512,768]{1,0:T(8,128)(2,1)S(1)} %copy-done.15, bf16[5,512,768]{2,1,0:T(8,128)(2,1)} %shard_map.419.grad_ref, bf16[512,768]{1,0:T(8,128)(2,1)S(1)} %get-tuple-element.441.attended_ref), custom_call_target="tpu_custom_call" | custom-call | tf_op jit(solution)/shard_map/pallas_call | solution.py:348
  386.3 4.3 constant_dynamic-slice_fusion.12
  403.4 5.8 all-to-all-start.6
  420.6 13.8 %all-to-all-done.6 = bf16[16,48,768]{2,1,0:T(8,128)(2,1)S(1)} async-done(((bf16[16,48,768]{2,1,0:T(8,128)(2,1)}), bf16[16,48,768]{2,1,0:T(8,128)(2,1)S(1)}, u32[]{:S(2)}, u32[]{:S(2)}) %all-to-all-start.6) | async-done | bytes 1179680 | tf_op jit(solution)/shard_map/all_to_all | solution.py:892
  435.9 30.6 %reduce-scatter.2.cloned.1.call-done = bf16[2,4,48,768]{3,2,1,0:T(8,128)(2,1)} async-done(((bf16[2,4,768,768]{3,2,1,0:T(8,128)(2,1)}), bf16[2,4,48,768]{3,2,1,0:T(8,128)(2,1)}) %reduce-scatter.2.cloned.1.call-update) | async-done | bytes 589840 | tf_op jit(solution)/shard_map/reduce_scatter | solution.py:645
  480.0 10.6 %collective-permute-done.31 = bf16[4,1,1,1,48,768]{5,4,0,3,2,1:T(8,128)(2,1)S(1)} collective-permute-done((bf16[4,1,1,1,48,768]{5,4,0,3,2,1:T(8,128)(2,1)S(1)}, bf16[4,1,1,1,48,768]{5,4,0,3,2,1:T(8,128)(2,1)S(1)}, u32[]{:S(2)}, u32[]{:S(2)}) %collective-permute-start.31) | collective-permute-done | bytes 294944 | tf_op jit(solution)/shard_map/ppermute | solution.py:59
  495.5 6.8 %collective-permute-start.33 = (bf16[3,1,1,1,48,384]{5,4,0,3,2,1:T(8,128)(2,1)}, bf16[3,1,1,1,48,384]{5,4,0,3,2,1:T(8,128)(2,1)}, u32[]{:S(2)}, u32[]{:S(2)}) collective-permute-start(bf16[3,1,1,1,48,384]{5,4,0,3,2,1:T(8,128)(2,1)} %get-tuple-element.492), channel_id=1, source_target_pairs={{0,8},{2,10},{4,12},{6,14},{8,16},{10,18},{12,20},{14,22},{16,24},... | collective-permute-start | bytes 331784 | tf_op jit(solution)/shard_map/ppermute | solution.py:59
  502.4 8.1 %add_add_fusion.1 = f32[1920,768]{1,0:T(8,128)} fusion(f32[1920,768]{1,0:T(8,128)S(1)} %fusion.17, bf16[1920,768]{1,0:T(8,128)(2,1)S(1)} %copy-done.45, bf16[480,768]{1,0:T(8,128)(2,1)S(1)} %copy-done.88, bf16[480,768]{1,0:T(8,128)(2,1)S(1)} %copy-done.86, bf16[480,768]{1,0:T(8,128)(2,1)} %collective-permute-done.17, ...), kind=kOutput, calls=%fused_computation.37 | convolution fusion | flops 2284093440 | bytes 18877440 | tf_op jit(solution)/shard_map/dot_general | solution.py:168
  569.2 7.9 %multiply_subtract_fusion = (f32[1920,768]{1,0:T(8,128)}, f32[1920,768]{1,0:T(8,128)}) fusion(f32[1920,768]{1,0:T(8,128)} %param.33, f32[1920,768]{1,0:T(8,128)} %get-tuple-element.334, f32[768]{0:T(1024)S(1)} %get-tuple-element.358, f32[1920]{0:T(1024)S(1)} %get-tuple-element.430, f32[]{:T(128)S(6)} %min.13), kind=kLoop, calls=%fused_computation.36 | loop fusion | flops 5898240 | bytes 23603716 | tf_op jit(solution)/shard_map/sub | solution.py:997
  (508 shorter events, 224.3 us)
Async XLA Ops:
  7.2 121.1 %all-gather.2.cloned.1.call-start = ((), (), s32[]{:S(2)}) async-start(), calls=%async_computation.8 | async-start | bytes 18800640 | tf_op jit(solution)/shard_map/all_gather | solution.py:816
  35.6 11.8 %all-to-all-start.4 = ((s32[32,1,178]{2,1,0:T(1,128)}), s32[32,1,178]{2,1,0:T(1,128)S(1)}, u32[]{:S(2)}, u32[]{:S(2)}) async-start(s32[32,1,178]{2,1,0:T(1,128)} %all_to_all.40), calls=%async_computation.4 | async-start | bytes 65536 | tf_op jit(solution)/shard_map/all_to_all | solution.py:763
  51.9 48.5 %all-to-all-start.5 = ((bf16[16,48,768]{2,1,0:T(8,128)(2,1)}), bf16[16,48,768]{2,1,0:T(8,128)(2,1)}, u32[]{:S(2)}, u32[]{:S(2)}) async-start(bf16[16,48,768]{2,1,0:T(8,128)(2,1)} %bitcast.204), calls=%async_computation.5 | async-start | bytes 2359296 | tf_op jit(solution)/shard_map/all_to_all | solution.py:774
  56.3 410.1 %reduce-scatter.2.cloned.1.call-start = ((), (), s32[]{:S(2)}) async-start(), calls=%async_computation.9 | async-start | bytes 10027008 | tf_op jit(solution)/shard_map/reduce_scatter | solution.py:645
  171.1 13.0 %collective-permute-start.6 = (bf16[1,1,1,128,768]{4,3,2,1,0:T(8,128)(2,1)S(1)}, bf16[1,1,1,128,768]{4,3,2,1,0:T(8,128)(2,1)S(1)}, u32[]{:S(2)}, u32[]{:S(2)}) collective-permute-start(bf16[1,1,1,128,768]{4,3,2,1,0:T(8,128)(2,1)S(1)} %fusion.31), channel_id=1, source_target_pairs={{0,8},{2,10},{4,12},{6,14},{8,16},{10,18},{12,20},{14,22},{16,24},... | collective-permute-start | bytes 589832 | tf_op jit(solution)/shard_map/ppermute | solution.py:59
  178.9 11.8 %collective-permute-start.7 = (bf16[1,1,1,128,768]{4,3,2,1,0:T(8,128)(2,1)S(1)}, bf16[1,1,1,128,768]{4,3,2,1,0:T(8,128)(2,1)S(1)}, u32[]{:S(2)}, u32[]{:S(2)}) collective-permute-start(bf16[1,1,1,128,768]{4,3,2,1,0:T(8,128)(2,1)S(1)} %fusion.31), channel_id=1, source_target_pairs={{0,16},{2,18},{4,20},{6,22},{8,24},{10,26},{12,28},{14,30},{16,0},... | collective-permute-start | bytes 589832 | tf_op jit(solution)/shard_map/ppermute | solution.py:59
  178.9 13.1 %collective-permute-start.8 = (bf16[1,1,1,128,768]{4,3,2,1,0:T(8,128)(2,1)S(1)}, bf16[1,1,1,128,768]{4,3,2,1,0:T(8,128)(2,1)S(1)}, u32[]{:S(2)}, u32[]{:S(2)}) collective-permute-start(bf16[1,1,1,128,768]{4,3,2,1,0:T(8,128)(2,1)S(1)} %fusion.31), channel_id=1, source_target_pairs={{0,24},{2,26},{4,28},{6,30},{8,0},{10,2},{12,4},{14,6},{16,8},{18,... | collective-permute-start | bytes 589832 | tf_op jit(solution)/shard_map/ppermute | solution.py:59
  192.1 19.0 %collective-permute-start.9 = (bf16[4,1,1,128,768]{4,3,2,1,0:T(8,128)(2,1)S(1)}, bf16[4,1,1,128,768]{4,3,2,1,0:T(8,128)(2,1)S(1)}, u32[]{:S(2)}, u32[]{:S(2)}) collective-permute-start(bf16[4,1,1,128,768]{4,3,2,1,0:T(8,128)(2,1)S(1)} %pad_maximum_fusion.4), channel_id=1, source_target_pairs={{0,4},{2,6},{4,0},{6,2},{8,12},{10,14},{12,8},{14,10},{16,20},{18,... | collective-permute-start | bytes 2359304 | tf_op jit(solution)/shard_map/ppermute | solution.py:59
  232.8 11.9 %collective-permute-start.12 = (f32[3,16,128]{2,1,0:T(8,128)S(1)}, f32[3,16,128]{2,1,0:T(8,128)S(1)}, u32[]{:S(2)}, u32[]{:S(2)}) collective-permute-start(f32[3,16,128]{2,1,0:T(8,128)S(1)} %pad_maximum_fusion.6), channel_id=1, source_target_pairs={{0,4},{2,6},{4,0},{6,2},{8,12},{10,14},{12,8},{14,10},{16,20},{18,... | collective-permute-start | bytes 73736 | tf_op jit(solution)/shard_map/ppermute | solution.py:106
  271.9 20.0 %collective-permute-start.20 = (bf16[4,1,1,128,768]{4,3,2,1,0:T(8,128)(2,1)S(1)}, bf16[4,1,1,128,768]{4,3,2,1,0:T(8,128)(2,1)S(1)}, u32[]{:S(2)}, u32[]{:S(2)}) collective-permute-start(bf16[4,1,1,128,768]{4,3,2,1,0:T(8,128)(2,1)S(1)} %dynamic-slice_convert_fusion), channel_id=1, source_target_pairs={{0,4},{2,6},{4,0},{6,2},{8,12},{10,14},{12,8},{14,10},{16,20},{18,... | collective-permute-start | bytes 2359304 | tf_op jit(solution)/shard_map/ppermute | solution.py:59
  282.0 29.9 %collective-permute-start.16 = (bf16[480,768]{1,0:T(8,128)(2,1)S(1)}, bf16[480,768]{1,0:T(8,128)(2,1)}, u32[]{:S(2)}, u32[]{:S(2)}) collective-permute-start(bf16[480,768]{1,0:T(8,128)(2,1)S(1)} %get-tuple-element.469), channel_id=1, source_target_pairs={{0,1},{1,0},{2,3},{3,2},{4,5},{5,4},{6,7},{7,6},{8,9},{9,8},{10,11... | collective-permute-start | bytes 2211848 | tf_op jit(solution)/shard_map/ppermute | solution.py:59
  283.4 33.4 %collective-permute-start.17 = (bf16[480,768]{1,0:T(8,128)(2,1)S(1)}, bf16[480,768]{1,0:T(8,128)(2,1)}, u32[]{:S(2)}, u32[]{:S(2)}) collective-permute-start(bf16[480,768]{1,0:T(8,128)(2,1)S(1)} %get-tuple-element.468), channel_id=1, source_target_pairs={{0,1},{1,0},{2,3},{3,2},{4,5},{5,4},{6,7},{7,6},{8,9},{9,8},{10,11... | collective-permute-start | bytes 2211848 | tf_op jit(solution)/shard_map/ppermute | solution.py:59
  292.9 10.2 %collective-permute-start.21 = (bf16[1,1,1,128,768]{4,3,2,1,0:T(8,128)(2,1)}, bf16[1,1,1,128,768]{4,3,2,1,0:T(8,128)(2,1)S(1)}, u32[]{:S(2)}, u32[]{:S(2)}) collective-permute-start(bf16[1,1,1,128,768]{4,3,2,1,0:T(8,128)(2,1)} %get-tuple-element.305), channel_id=1, source_target_pairs={{0,8},{2,10},{4,12},{6,14},{8,16},{10,18},{12,20},{14,22},{16,24},... | collective-permute-start | bytes 589832 | tf_op jit(solution)/shard_map/ppermute | solution.py:59
  294.7 16.1 %collective-permute-start.22 = (bf16[1,1,1,128,768]{4,3,2,1,0:T(8,128)(2,1)}, bf16[1,1,1,128,768]{4,3,2,1,0:T(8,128)(2,1)}, u32[]{:S(2)}, u32[]{:S(2)}) collective-permute-start(bf16[1,1,1,128,768]{4,3,2,1,0:T(8,128)(2,1)} %get-tuple-element.306), channel_id=1, source_target_pairs={{0,16},{2,18},{4,20},{6,22},{8,24},{10,26},{12,28},{14,30},{16,0},... | collective-permute-start | bytes 589832 | tf_op jit(solution)/shard_map/ppermute | solution.py:59
  297.6 13.2 %collective-permute-start.23 = (bf16[1,1,1,128,768]{4,3,2,1,0:T(8,128)(2,1)S(1)}, bf16[1,1,1,128,768]{4,3,2,1,0:T(8,128)(2,1)}, u32[]{:S(2)}, u32[]{:S(2)}) collective-permute-start(bf16[1,1,1,128,768]{4,3,2,1,0:T(8,128)(2,1)S(1)} %get-tuple-element.307), channel_id=1, source_target_pairs={{0,24},{2,26},{4,28},{6,30},{8,0},{10,2},{12,4},{14,6},{16,8},{18,... | collective-permute-start | bytes 589832 | tf_op jit(solution)/shard_map/ppermute | solution.py:59
  336.5 25.7 %collective-permute-start.18 = (bf16[480,768]{1,0:T(8,128)(2,1)}, bf16[480,768]{1,0:T(8,128)(2,1)S(1)}, u32[]{:S(2)}, u32[]{:S(2)}) collective-permute-start(bf16[480,768]{1,0:T(8,128)(2,1)} %get-tuple-element.467), channel_id=1, source_target_pairs={{0,1},{1,0},{2,3},{3,2},{4,5},{5,4},{6,7},{7,6},{8,9},{9,8},{10,11... | collective-permute-start | bytes 2211848 | tf_op jit(solution)/shard_map/ppermute | solution.py:59
  338.0 32.7 %collective-permute-start.19 = (bf16[480,768]{1,0:T(8,128)(2,1)}, bf16[480,768]{1,0:T(8,128)(2,1)S(1)}, u32[]{:S(2)}, u32[]{:S(2)}) collective-permute-start(bf16[480,768]{1,0:T(8,128)(2,1)} %get-tuple-element.466), channel_id=1, source_target_pairs={{0,1},{1,0},{2,3},{3,2},{4,5},{5,4},{6,7},{7,6},{8,9},{9,8},{10,11... | collective-permute-start | bytes 2211848 | tf_op jit(solution)/shard_map/ppermute | solution.py:59
  403.4 7.9 %collective-permute-start.25 = (bf16[3,4,2,1,48,768]{5,4,0,3,2,1:T(8,128)(2,1)}, bf16[3,4,2,1,48,768]{5,4,0,3,2,1:T(8,128)(2,1)}, u32[]{:S(2)}, u32[]{:S(2)}) collective-permute-start(bf16[3,4,2,1,48,768]{5,4,0,3,2,1:T(8,128)(2,1)} %copy.142), channel_id=1, source_target_pairs={{0,2},{2,0},{4,6},{6,4},{8,10},{10,8},{12,14},{14,12},{16,18},{18,... | collective-permute-start | bytes 5308424 | tf_op jit(solution)/shard_map/ppermute | solution.py:59
  403.4 31.0 %all-to-all-start.6 = ((bf16[16,48,768]{2,1,0:T(8,128)(2,1)}), bf16[16,48,768]{2,1,0:T(8,128)(2,1)S(1)}, u32[]{:S(2)}, u32[]{:S(2)}) async-start(bf16[16,48,768]{2,1,0:T(8,128)(2,1)} %bitcast.52), calls=%async_computation.6 | async-start | bytes 2359296 | tf_op jit(solution)/shard_map/all_to_all | solution.py:892
  409.1 57.3 %collective-permute-start.27 = (bf16[4,4,1,1,48,768]{5,4,0,3,2,1:T(8,128)(2,1)}, bf16[4,4,1,1,48,768]{5,4,0,3,2,1:T(8,128)(2,1)}, u32[]{:S(2)}, u32[]{:S(2)}) collective-permute-start(bf16[4,4,1,1,48,768]{5,4,0,3,2,1:T(8,128)(2,1)} %constant_dynamic-slice_fusion.11), channel_id=1, source_target_pairs={{0,4},{2,6},{4,0},{6,2},{8,12},{10,14},{12,8},{14,10},{16,20},{18,... | collective-permute-start | bytes 3538952 | tf_op jit(solution)/shard_map/ppermute | solution.py:59
  416.0 53.6 %collective-permute-start.26 = (bf16[3,4,2,1,48,384]{5,4,0,3,2,1:T(8,128)(2,1)}, bf16[3,4,2,1,48,384]{5,4,0,3,2,1:T(8,128)(2,1)}, u32[]{:S(2)}, u32[]{:S(2)}) collective-permute-start(bf16[3,4,2,1,48,384]{5,4,0,3,2,1:T(8,128)(2,1)} %constant_dynamic-slice_fusion.8), channel_id=1, source_target_pairs={{0,1},{1,0},{2,3},{3,2},{4,5},{5,4},{6,7},{7,6},{8,9},{9,8},{10,11... | collective-permute-start | bytes 2654216 | tf_op jit(solution)/shard_map/ppermute | solution.py:59
  434.4 44.0 %collective-permute-start.28 = (bf16[768,768]{1,0:T(8,128)(2,1)S(1)}, bf16[768,768]{1,0:T(8,128)(2,1)}, u32[]{:S(2)}, u32[]{:S(2)}) collective-permute-start(bf16[768,768]{1,0:T(8,128)(2,1)S(1)} %bitcast.201), channel_id=1, source_target_pairs={{0,1},{1,0},{2,3},{3,2},{4,5},{5,4},{6,7},{7,6},{8,9},{9,8},{10,11... | collective-permute-start | bytes 3538952 | tf_op jit(solution)/shard_map/ppermute | solution.py:59
  468.1 11.9 %collective-permute-start.30 = (bf16[4,1,1,1,48,768]{5,4,0,3,2,1:T(8,128)(2,1)S(1)}, bf16[4,1,1,1,48,768]{5,4,0,3,2,1:T(8,128)(2,1)S(1)}, u32[]{:S(2)}, u32[]{:S(2)}) collective-permute-start(bf16[4,1,1,1,48,768]{5,4,0,3,2,1:T(8,128)(2,1)S(1)} %get-tuple-element.479), channel_id=1, source_target_pairs={{0,8},{2,10},{4,12},{6,14},{8,16},{10,18},{12,20},{14,22},{16,24},... | collective-permute-start | bytes 884744 | tf_op jit(solution)/shard_map/ppermute | solution.py:59
  471.1 21.3 %collective-permute-start.29 = (bf16[3,4,1,1,48,384]{5,4,0,3,2,1:T(8,128)(2,1)S(1)}, bf16[3,4,1,1,48,384]{5,4,0,3,2,1:T(8,128)(2,1)S(1)}, u32[]{:S(2)}, u32[]{:S(2)}) collective-permute-start(bf16[3,4,1,1,48,384]{5,4,0,3,2,1:T(8,128)(2,1)S(1)} %constant_dynamic-slice_fusion.6), channel_id=1, source_target_pairs={{0,4},{2,6},{4,0},{6,2},{8,12},{10,14},{12,8},{14,10},{16,20},{18,... | collective-permute-start | bytes 1327112 | tf_op jit(solution)/shard_map/ppermute | solution.py:59
  471.7 19.0 %collective-permute-start.31 = (bf16[4,1,1,1,48,768]{5,4,0,3,2,1:T(8,128)(2,1)S(1)}, bf16[4,1,1,1,48,768]{5,4,0,3,2,1:T(8,128)(2,1)S(1)}, u32[]{:S(2)}, u32[]{:S(2)}) collective-permute-start(bf16[4,1,1,1,48,768]{5,4,0,3,2,1:T(8,128)(2,1)S(1)} %get-tuple-element.478), channel_id=1, source_target_pairs={{0,16},{2,18},{4,20},{6,22},{8,24},{10,26},{12,28},{14,30},{16,0},... | collective-permute-start | bytes 884744 | tf_op jit(solution)/shard_map/ppermute | solution.py:59
  473.4 17.3 %collective-permute-start.32 = (bf16[4,1,1,1,48,768]{5,4,0,3,2,1:T(8,128)(2,1)S(1)}, bf16[4,1,1,1,48,768]{5,4,0,3,2,1:T(8,128)(2,1)S(1)}, u32[]{:S(2)}, u32[]{:S(2)}) collective-permute-start(bf16[4,1,1,1,48,768]{5,4,0,3,2,1:T(8,128)(2,1)S(1)} %get-tuple-element.477), channel_id=1, source_target_pairs={{0,24},{2,26},{4,28},{6,30},{8,0},{10,2},{12,4},{14,6},{16,8},{18,... | collective-permute-start | bytes 884744 | tf_op jit(solution)/shard_map/ppermute | solution.py:59
  478.4 44.8 %collective-permute-start.38 = (bf16[2,4,48,768]{3,2,1,0:T(8,128)(2,1)}, bf16[2,4,48,768]{3,2,1,0:T(8,128)(2,1)}, u32[]{:S(2)}, u32[]{:S(2)}) collective-permute-start(bf16[2,4,48,768]{3,2,1,0:T(8,128)(2,1)} %reduce-scatter.2.cloned.1.call-done), channel_id=1, source_target_pairs={{0,1},{1,0},{2,3},{3,2},{4,5},{5,4},{6,7},{7,6},{8,9},{9,8},{10,11... | collective-permute-start | bytes 1769480 | tf_op jit(solution)/shard_map/ppermute | solution.py:59
  490.8 31.3 %collective-permute-start.37 = (bf16[4,48,768]{2,1,0:T(8,128)(2,1)S(1)}, bf16[4,48,768]{2,1,0:T(8,128)(2,1)}, u32[]{:S(2)}, u32[]{:S(2)}) collective-permute-start(bf16[4,48,768]{2,1,0:T(8,128)(2,1)S(1)} %fusion.43), channel_id=1, source_target_pairs={{0,1},{1,0},{2,3},{3,2},{4,5},{5,4},{6,7},{7,6},{8,9},{9,8},{10,11... | collective-permute-start | bytes 884744 | tf_op jit(solution)/shard_map/ppermute | solution.py:59
  495.5 24.9 %collective-permute-start.33 = (bf16[3,1,1,1,48,384]{5,4,0,3,2,1:T(8,128)(2,1)}, bf16[3,1,1,1,48,384]{5,4,0,3,2,1:T(8,128)(2,1)}, u32[]{:S(2)}, u32[]{:S(2)}) collective-permute-start(bf16[3,1,1,1,48,384]{5,4,0,3,2,1:T(8,128)(2,1)} %get-tuple-element.492), channel_id=1, source_target_pairs={{0,8},{2,10},{4,12},{6,14},{8,16},{10,18},{12,20},{14,22},{16,24},... | collective-permute-start | bytes 331784 | tf_op jit(solution)/shard_map/ppermute | solution.py:59
  510.7 9.7 %collective-permute-start.34 = (bf16[3,1,1,1,48,384]{5,4,0,3,2,1:T(8,128)(2,1)}, bf16[3,1,1,1,48,384]{5,4,0,3,2,1:T(8,128)(2,1)S(1)}, u32[]{:S(2)}, u32[]{:S(2)}) collective-permute-start(bf16[3,1,1,1,48,384]{5,4,0,3,2,1:T(8,128)(2,1)} %get-tuple-element.491), channel_id=1, source_target_pairs={{0,16},{2,18},{4,20},{6,22},{8,24},{10,26},{12,28},{14,30},{16,0},... | collective-permute-start | bytes 331784 | tf_op jit(solution)/shard_map/ppermute | solution.py:59
  512.2 8.2 %collective-permute-start.35 = (bf16[3,1,1,1,48,384]{5,4,0,3,2,1:T(8,128)(2,1)}, bf16[3,1,1,1,48,384]{5,4,0,3,2,1:T(8,128)(2,1)S(1)}, u32[]{:S(2)}, u32[]{:S(2)}) collective-permute-start(bf16[3,1,1,1,48,384]{5,4,0,3,2,1:T(8,128)(2,1)} %get-tuple-element.490), channel_id=1, source_target_pairs={{0,24},{2,26},{4,28},{6,30},{8,0},{10,2},{12,4},{14,6},{16,8},{18,... | collective-permute-start | bytes 331784 | tf_op jit(solution)/shard_map/ppermute | solution.py:59
  538.8 8.7 %collective-permute-start.42 = (f32[14,768]{1,0:T(8,128)S(1)}, f32[14,768]{1,0:T(8,128)S(1)}, u32[]{:S(2)}, u32[]{:S(2)}) collective-permute-start(f32[14,768]{1,0:T(8,128)S(1)} %add.744), channel_id=1, source_target_pairs={{0,16},{2,18},{4,20},{6,22},{8,24},{10,26},{12,28},{14,30},{16,0},... | collective-permute-start | bytes 129032 | tf_op jit(solution)/shard_map/ppermute | solution.py:106
  (105 other events, 752.1 us)
Sparse Core Ops, SparseCore 0:
  11.9 116.3 all-gather.1
  336.6 129.8 reduce-scatter.1

commit v4 on v3

--- a/solution.py
+++ b/solution.py
@@ -186,9 +186,9 @@
     return jnp.where(mask, value, jnp.zeros_like(value))
 
 
-def attend_kernel(length_ref, query_ref, key_ref, value_ref, box_query_ref, box_key_ref, out_ref):
+def attend_kernel(length_ref, stack_ref, out_ref):
     length = length_ref[pl.program_id(0)]
-    query, key, box_query, box_key = query_ref[...], key_ref[...], box_query_ref[...], box_key_ref[...]
+    box_query, box_key, query, key, value = (stack_ref[index] for index in range(1, 6))
     keys = jnp.concatenate([key, box_key, key], axis=1)
     keep = lax.broadcasted_iota(jnp.int32, (1, key.shape[0]), 1) < length
     scale = jnp.asarray(HEAD_DIM ** (-0.5), BFLOAT)
@@ -201,21 +201,13 @@
         score = jnp.where(keep, score, NEGATIVE)
         expo = jnp.exp(score - jnp.max(score, axis=1, keepdims=True))
         prob = (expo * (1.0 / jnp.sum(expo, axis=1, keepdims=True))).astype(BFLOAT)
-        mixed = jnp.where(mask, product(prob, value_ref[...]), mixed)
+        mixed = jnp.where(mask, product(prob, value), mixed)
     out_ref[...] = mixed.astype(BFLOAT)
 
 
-def attend_back_kernel(
-    length_ref, query_ref, key_ref, value_ref, box_query_ref, box_key_ref, grad_ref, out_ref
-):
+def attend_back_kernel(length_ref, stack_ref, grad_ref, out_ref):
     length = length_ref[pl.program_id(0)]
-    query, key, value, box_query, box_key = (
-        query_ref[...],
-        key_ref[...],
-        value_ref[...],
-        box_query_ref[...],
-        box_key_ref[...],
-    )
+    box_query, box_key, query, key, value = (stack_ref[index] for index in range(1, 6))
     grad = grad_ref[...]
     rows = key.shape[0]
     keys = jnp.concatenate([key, box_key, key], axis=1)
@@ -256,25 +248,24 @@
 ROOMY = pltpu.CompilerParams(vmem_limit_bytes=48 * 1024 * 1024)
 
 
-def attention_call(kernel, lengths, arrays, stacked):
-    tokens, width = arrays[0].shape
+def attention_call(kernel, lengths, stack, arrays, stacked):
+    count, tokens, width = stack.shape
     pages = lengths.shape[0]
     spec = pl.BlockSpec((tokens // pages, LANES), lambda page, pair: (page, pair))
-    out_spec, shape = spec, (tokens, width)
-    if stacked:
-        shape = (stacked, tokens, width)
-        out_spec = pl.BlockSpec(
-            (stacked, tokens // pages, LANES), lambda page, pair: (0, page, pair)
-        )
+
+    def stack_spec(count):
+        return pl.BlockSpec((count, tokens // pages, LANES), lambda page, pair: (0, page, pair))
+
+    shape = (stacked, tokens, width) if stacked else (tokens, width)
     return pl.pallas_call(
         kernel,
         grid=(pages, width // LANES),
-        in_specs=[pl.BlockSpec(memory_space=pltpu.SMEM)] + [spec] * len(arrays),
-        out_specs=out_spec,
+        in_specs=[pl.BlockSpec(memory_space=pltpu.SMEM), stack_spec(count)] + [spec] * len(arrays),
+        out_specs=stack_spec(stacked) if stacked else spec,
         out_shape=jax.ShapeDtypeStruct(shape, BFLOAT),
         compiler_params=ROOMY,
         cost_estimate=FREE,
-    )(lengths, *arrays)
+    )(lengths, stack, *arrays)
 
 
 def start_kernel(first_ref, grad_ref, mat_ref, out_ref, place_ref, sums_ref, total):
@@ -371,15 +362,15 @@
         out_ref[...] = contract_rows(features_ref[...], grad_place_ref[...]).astype(BFLOAT)
 
 
-def box_gradients(features_low, place, pieces, grad_place):
-    tokens, width = place.shape
+def box_gradients(features_low, stack, pieces, grad_place):
+    tokens, width = grad_place.shape
     whole = pl.BlockSpec((tokens, width), lambda k: (0, 0))
     return pl.pallas_call(
         box_kernel,
         grid=(3,),
         in_specs=[
             whole,
-            whole,
+            pl.BlockSpec((None, tokens, width), lambda k: (0, 0, 0)),
             pl.BlockSpec((None, tokens, width), lambda k: (jnp.minimum(k, 1) + 3, 0, 0)),
             whole,
         ],
@@ -387,7 +378,51 @@
         out_shape=jax.ShapeDtypeStruct((3, width, width), BFLOAT),
         compiler_params=ROOMY,
         cost_estimate=FREE,
-    )(features_low, place, pieces, grad_place)
+    )(features_low, stack, pieces, grad_place)
+
+
+def project_kernel(features_ref, act_ref, mat_ref, bias_ref, out_ref, place):
+    step = pl.program_id(0)
+
+    @pl.when(step == 0)
+    def _():
+        low = (product(features_ref[...], mat_ref[...]) + bias_ref[...]).astype(BFLOAT)
+        place[...] = low
+        out_ref[...] = low
+
+    @pl.when((step > 0) & (step < 3))
+    def _():
+        out_ref[...] = product(place[...], mat_ref[...]).astype(BFLOAT)
+
+    @pl.when(step >= 3)
+    def _():
+        out_ref[...] = (product(act_ref[...], mat_ref[...]) + bias_ref[...]).astype(BFLOAT)
+
+
+def projections(features_low, act, packed, first_mat, gains):
+    tokens, width = act.shape
+    whole = pl.BlockSpec((tokens, width), lambda k: (0, 0))
+    none = jnp.zeros_like(gains[0])
+    biases = jnp.stack([gains[9], none, none, gains[6], none, gains[7]])[:, None]
+
+    def mat(k):
+        return first_mat + jnp.where(k == 0, 0, jnp.where(k < 3, k + 3, k - 2))
+
+    return pl.pallas_call(
+        project_kernel,
+        grid=(6,),
+        in_specs=[
+            whole,
+            whole,
+            pl.BlockSpec((None, width, width), lambda k: (mat(k), 0, 0)),
+            pl.BlockSpec((None, 1, width), lambda k: (k, 0, 0)),
+        ],
+        out_specs=pl.BlockSpec((None, tokens, width), lambda k: (k, 0, 0)),
+        out_shape=jax.ShapeDtypeStruct((6, tokens, width), BFLOAT),
+        scratch_shapes=[pltpu.VMEM((tokens, width), BFLOAT)],
+        compiler_params=ROOMY,
+        cost_estimate=FREE,
+    )(features_low, act, packed, biases)
 
 
 class Buckets(NamedTuple):
@@ -529,30 +564,26 @@
     )(grad_feed, middle_low, active, slope, packed, packed)
 
 
-def logits_kernel(rows_ref, table_ref, label_ref, expo_ref, stats_ref):
+def logits_kernel(rows_ref, table_ref, expo_ref, stats_ref):
     logits = times_transposed(rows_ref[...], table_ref[...])
     peak = jnp.max(logits, axis=1, keepdims=True)
     expo = jnp.exp(logits - peak)
     expo_ref[...] = expo.astype(BFLOAT)
     mass = jnp.sum(expo, axis=1, keepdims=True)
-    column = lax.broadcasted_iota(jnp.int32, logits.shape, 1)
-    target = jnp.sum(jnp.where(column == label_ref[...], logits, 0.0), axis=1, keepdims=True)
     lane = lax.broadcasted_iota(jnp.int32, (logits.shape[0], LANES), 1)
-    stats = jnp.where(lane == 0, peak, jnp.where(lane == 1, mass, target))
-    stats_ref[...] = stats.T[:8]
-
-
-def head_logits(rows_all, table_low, own_labels):
+    stats_ref[...] = jnp.where(lane == 0, peak, mass).T[:8]
+
+
+def head_logits(rows_all, table_low):
     count, width = rows_all.shape
     shard_rows = table_low.shape[0]
-    step = 256
+    step = min(512, count)
     return pl.pallas_call(
         logits_kernel,
         grid=(count // step,),
         in_specs=[
             pl.BlockSpec((step, width), lambda i: (i, 0)),
             pl.BlockSpec((shard_rows, width), lambda i: (0, 0)),
-            pl.BlockSpec((step, 1), lambda i: (i, 0)),
         ],
         out_specs=[
             pl.BlockSpec((step, shard_rows), lambda i: (i, 0)),
@@ -564,21 +595,19 @@
         ],
         compiler_params=ROOMY,
         cost_estimate=FREE,
-    )(rows_all, table_low, own_labels[:, None])
+    )(rows_all, table_low)
 
 
 def column_sum(value):
     return jnp.sum(value.astype(FLOAT), axis=0)
 
 
-def layer_forward(weights, embedded, place, box_query, box_key, lengths):
+def layer_forward(weights, embedded, features_low, lengths):
     mats, packed, gains, up_bias = weights
     start_state = layer_norm(embedded, gains[0], gains[1])
     act = start_state.astype(BFLOAT)
-    query = (product(act, mats[1]) + gains[6]).astype(BFLOAT)
-    keys = product(act, mats[2]).astype(BFLOAT)
-    values = (product(act, mats[3]) + gains[7]).astype(BFLOAT)
-    mixed = attention_call(attend_kernel, lengths, (query, keys, values, box_query, box_key), 0)
+    stack = projections(features_low, act, packed, packed.shape[0] - mats.shape[0], gains)
+    mixed = attention_call(attend_kernel, lengths, stack, (), 0)
     first_sum = start_state + (product(mixed, mats[6]) + gains[8])
     middle = layer_norm(first_sum, gains[2], gains[3])
     middle_low = middle.astype(BFLOAT)
@@ -587,12 +616,7 @@
     kept = (
         embedded,
         act,
-        place,
-        query,
-        keys,
-        values,
-        box_query,
-        box_key,
+        stack,
         mixed,
         first_sum,
         middle_low,
@@ -608,12 +632,7 @@
     (
         embedded,
         act,
-        place,
-        query,
-        keys,
-        values,
-        box_query,
-        box_key,
+        stack,
         mixed,
         first_sum,
         middle_low,
@@ -649,7 +668,7 @@
     grad_attended = grad_first.astype(BFLOAT)
     grad_mixed = times_transposed(grad_attended, mats[6]).astype(BFLOAT)
     pieces = attention_call(
-        attend_back_kernel, lengths, (query, keys, values, box_query, box_key, grad_mixed), 5
+        attend_back_kernel, lengths, stack, (grad_mixed,), 5
     )
     pieces = after(pieces, head_parts[2])
     first_mat = packed.shape[0] - mats.shape[0]
@@ -680,7 +699,7 @@
     token_part = token_gradients(act, mixed, pieces, grad_attended)
     token_core = send(by_owner(token_part, lines), "core")
     pieces = after(pieces, *token_core[1])
-    box_part = box_gradients(features_low, place, pieces, grad_place)
+    box_part = box_gradients(features_low, stack, pieces, grad_place)
     token_y = send(travel(token_core, "core", box_part), "y")
     box_part = after(box_part, *token_y[1])
     box_core = send(by_owner(box_part, lines), "core")
@@ -692,11 +711,11 @@
     token_z = send(travel(token_y, "y", feeds_sum), "z")
     box_y = send(travel(box_x, "x", token_z[1][0]), "y")
     spread = [give_rows(0, after(rows[0], *box_y[1]))]
-    token_sum = travel(token_z, "z", spread[0])[:, 0, 0, 0]
-    box_z = send(travel(box_y, "y", token_sum), "z")
+    box_z = send(travel(box_y, "y", spread[0]), "z")
     others = after(others, *box_z[1])
     spread += [give_rows(index, value) for index, value in enumerate(others, 1)]
-    box_half = travel(box_z, "z", spread[-1])[:, 0, 0, 0]
+    token_sum = travel(token_z, "z", spread[-1])[:, 0, 0, 0]
+    box_half = travel(box_z, "z", token_sum)[:, 0, 0, 0]
     feeds_other = after(from_other_copies(feeds_sum, lines), box_half)
     feeds_sum = feeds_sum.astype(FLOAT) + feeds_other.astype(FLOAT)
     token_mats = both_copies(token_sum, lines)
@@ -708,7 +727,7 @@
 def combine_mass(first, second):
     peak = jnp.maximum(first[0], second[0])
     mass = first[1] * jnp.exp(first[0] - peak) + second[1] * jnp.exp(second[0] - peak)
-    return jnp.stack([peak, mass, first[2] + second[2]])
+    return jnp.stack([peak, mass])
 
 
 def body(
@@ -790,6 +809,18 @@
     label_rows = product(one_hot(own_labels, shard_rows), table_low).astype(BFLOAT)
     embedded = after(embedded, label_rows)
 
+    depth = mats.shape[0]
+    items = depth + 3
+    lane = jnp.arange(width)
+    singles = jnp.pad(jnp.sum(mats_rows, axis=1), (1, width - 1 - depth))
+    for index, value in (
+        (0, jnp.sum(table_rows)),
+        (items - 2, jnp.sum(up_rows)),
+        (items - 1, jnp.sum(down_rows)),
+    ):
+        singles = jnp.where(lane == index, value, singles)
+    embedded = after(embedded, singles)
+
     small = jnp.concatenate([vectors.astype(BFLOAT).reshape(-1), up_bias.astype(BFLOAT)])[None]
 
     def lay(first, second, bit):
@@ -818,10 +849,7 @@
     weights = (layer_mats, packed, gains, bias)
 
     features_low = box_features(boxes, width).astype(BFLOAT)
-    place = (product(features_low, layer_mats[0]) + gains[9]).astype(BFLOAT)
-    box_query = product(place, layer_mats[4]).astype(BFLOAT)
-    box_key = product(place, layer_mats[5]).astype(BFLOAT)
-    top_state, kept = layer_forward(weights, embedded, place, box_query, box_key, lengths)
+    top_state, kept = layer_forward(weights, embedded, features_low, lengths)
 
     where_at = slots * lengths[:, None] // 256 + jnp.arange(pages)[:, None] * page_len
     pick = one_hot(where_at.reshape(-1), tokens)
@@ -830,12 +858,11 @@
     for axis, name in enumerate(("z", "y", "core")):
         rows_all = gather_line(rows_all, lines[name], axis)
     rows_all = rows_all.reshape(-1, width)
-    expo, stats = head_logits(rows_all, table_low, own_labels)
+    expo, stats = head_logits(rows_all, table_low)
     peak_here = stats[0]
     products = product(expo, table_low)
-    stats = stats[:3].reshape(3, -1, LANES)
-    stats = paired(stats, "fsdp", combine_mass, products).reshape(3, -1)
-    products, peak, mass, target = lax.optimization_barrier((products, *stats))
+    stats = paired(stats[:2].reshape(2, -1, LANES), "fsdp", combine_mass, products).reshape(2, -1)
+    products, peak, mass = lax.optimization_barrier((products, *stats))
     log_total = peak + jnp.log(mass)
     factor = jnp.exp(peak_here - log_total)
 
@@ -843,14 +870,11 @@
     valid_all = valid_slots(lengths_all.reshape(-1), slot_count).astype(FLOAT)
     count_token = jnp.sum(jnp.where(is_token, valid_all, 0.0))
     count_area = jnp.sum(jnp.where(is_token, 0.0, valid_all))
+    figure = jnp.arange(4)
+    counts = jnp.where(figure == 1, count_token, jnp.where(figure == 3, count_area, 0.0))
+    count_token, count_area, counts = lax.optimization_barrier((count_token, count_area, counts))
     valid = valid_all.reshape(groups, copies, pages, slot_count)
     valid = lax.dynamic_index_in_dim(valid, copy, 1, False).reshape(-1, slot_count)
-    loss_rows = (log_total - target).reshape(-1, slot_count) * valid
-    token_loss = jnp.sum(jnp.where(is_token, loss_rows, 0.0))
-    area_loss = jnp.sum(jnp.where(is_token, 0.0, loss_rows))
-    figure = jnp.arange(4)
-    losses = paired(jnp.where(figure < 2, token_loss, area_loss), "rep", jnp.add)
-    loss_parts = jnp.where(figure == 1, count_token, jnp.where(figure == 3, count_area, losses))
     share = jnp.where(is_token, 1.0 / count_token, 1.0 / count_area)
     weight = (valid * share[None, :]).reshape(-1)
     grad_rows = (products * factor[:, None] - label_rows.astype(FLOAT)) * weight[:, None]
@@ -866,10 +890,19 @@
     own, blocks = sends(received(own, blocks, lines["core"]), lines["y"], 1)
     grad_logits = after(grad_logits.astype(BFLOAT), *blocks)
     head_low = contract_rows(grad_logits, weighted).astype(BFLOAT)
+    totals = lax.dynamic_slice_in_dim(log_total * valid.reshape(-1), group * pages * slot_count, pages * slot_count)
+    targets = jnp.sum(after(rows_all, *blocks).astype(FLOAT) * label_rows.astype(FLOAT), axis=1)
+    losses = jnp.sum(totals.reshape(-1, slot_count), axis=0)
+    losses = losses - jnp.sum(targets.reshape(-1, slot_count) * valid, axis=0)
+    token_loss = jnp.sum(jnp.where(is_token, losses, 0.0))
+    area_loss = jnp.sum(jnp.where(is_token, 0.0, losses))
+    singles = jnp.where(lane == items + 1, token_loss, jnp.where(lane == items + 3, area_loss, singles))
     own, blocks = sends(received(own, blocks, lines["y"]), lines["z"], 0)
-    blocks = list(after(tuple(blocks), head_low))
+    blocks = list(after(tuple(blocks), head_low, singles))
     grad_rows = received(own, blocks, lines["z"]).reshape(-1, width)
-    head_parts = [from_other_copies(part, lines) for part in jnp.split(head_low, 4)]
+    fifth = shard_rows // 5
+    cuts = [fifth, 2 * fifth, shard_rows - (shard_rows - 2 * fifth) // 2]
+    head_parts = [from_other_copies(part, lines) for part in jnp.split(head_low, cuts)]
     grad_rows = after(grad_rows, *head_parts[:2])
     grad_top = sum(contract_rows(pick, part) for part in two_parts(grad_rows))
 
@@ -936,22 +969,11 @@
 
     table_grad = lax.while_loop(lambda state: state[0] < turns, another, (jnp.int32(1), table_grad))[1]
 
-    depth = mats.shape[0]
     feed_cols = hidden // width
     sizes = [(shard_rows * groups, width)] + [(mats.shape[1] * groups, width)] * depth
     sizes += [(up.shape[0] * groups, hidden), (down.shape[0] * groups, width)]
     row_squares = [jnp.sum(grad * grad, axis=-1) for grad in (table_grad, mats_grad, up_grad, down_grad)]
-    items = depth + 3
-    lane = jnp.arange(width)
-    singles = jnp.pad(jnp.sum(mats_rows, axis=1), (1, width - 1 - depth))
-    for index, value in (
-        (0, jnp.sum(table_rows)),
-        (items - 2, jnp.sum(up_rows)),
-        (items - 1, jnp.sum(down_rows)),
-        (items, jnp.sum(vectors_grad * vectors_grad)),
-        (items + 1, jnp.sum(bias_grad * bias_grad)),
-    ):
-        singles = jnp.where(lane == index, value, singles)
+    singles = jnp.where(lane == items, jnp.sum(small * small), singles)
     sums = jnp.concatenate(
         [
             jnp.sum(table_grad * table_grad, axis=0)[None],
@@ -965,8 +987,9 @@
         [table_cols[None], mats_cols, up_cols.reshape(feed_cols, width), down_cols[None]]
     )
     sums = paired(sums, "fsdp", jnp.add)
+    loss_parts = counts + paired(sums[-1, items + 1 : items + 5], "rep", jnp.add)
     totals = jnp.sum(sums[:-1], axis=1)
-    norm_square = jnp.sum(totals) + sums[-1, items] + sums[-1, items + 1]
+    norm_square = jnp.sum(totals) + sums[-1, items]
     grad_norm = jnp.sqrt(norm_square)
     clip = jnp.minimum(1.0, CLIP_NORM / grad_norm)
     square = clip * clip

time: 597 us -> 589 us (0.987)
  waiting for transfers between devices: 185 us -> 172 us
  matrix products: 66.3 us -> 57.1 us
  local copies, waits for them, and re-layouts: 45.5 us -> 53.3 us
  Pallas kernels: 87.5 us -> 94.7 us
    reduce_scatter x1, waiting for transfers between devices: 30.6 us -> 11.1 us  [layer_backward(): lax.psum_scatter(grad_feeds, 'fsdp', scatter_dimension=2, tiled=True)]
    dot_general x12 -> x6, matrix products: 41.8 us -> 30.3 us  [product(): return jnp.dot(left, right, preferred_element_type=FLOAT)]
    pallas_call x1 -> x2, Pallas kernels: 3.84 us -> 12.6 us  [the longest x1 8.64 us: projections(): pl.pallas_call(project_kernel, grid=(6,), in_specs=[whole, whole, pl.Bloc...]
    all_to_all x1, waiting for transfers between devices: 13.8 us -> 21.9 us  [give(): lax.all_to_all(rows.reshape(groups, stride, width), 'fsdp', 0, 0, tiled=T...]
    unnamed x185 -> x271, local copies, waits for them, and re-layouts: 15 us -> 21.7 us
    ppermute x29, starting transfers between devices: 46.5 us -> 53.2 us  [shifted(): return lax.ppermute(value, line.axis, pairs)]
  transfers between devices with their start and end apart: 47 -> 47, of which waited for: 24 -> 22; matrix products, arithmetic and copies ran while one was open for 22% -> 26% of each run, Pallas kernels for 6% -> 6%
where the time goes in v4:
time: 589 us; the launch traced here: 580 us
  waiting for transfers between devices  172 us (29%)
  Pallas kernels  94.7 us (16%)
  other arithmetic  94.3 us (16%)
  starting transfers between devices  86.4 us (15%)
  matrix products  57.1 us (10%)
  local copies, waits for them, and re-layouts  53.3 us (9%)
  between operations  22.6 us (4%)
    ppermute x29, waiting for transfers between devices, shifted(): return lax.ppermute(value, line.axis, pairs)  63.5 us
    ppermute x29, starting transfers between devices, shifted(): return lax.ppermute(value, line.axis, pairs)  53.2 us
    all_to_all x1, waiting for transfers between devices, fetch(): lax.all_to_all(rows.reshape(groups, stride, width), 'fsdp', 0, 0, tiled=T...  31.9 us
    dot_general x6, matrix products, product(): return jnp.dot(left, right, preferred_element_type=FLOAT)  30.3 us
    pallas_call x2, Pallas kernels, attention_call(): pl.pallas_call(kernel, grid=(pages, width // LANES), in_specs=[pl.BlockSp...  29.6 us
    dot_general x7, matrix products, contract_rows(): lax.dot_general(left, right, (((0,), (0,)), ((), ())), preferred_element_...  24.4 us
    all_to_all x1, waiting for transfers between devices, give(): lax.all_to_all(rows.reshape(groups, stride, width), 'fsdp', 0, 0, tiled=T...  21.9 us
    unnamed x271, local copies, waits for them, and re-layouts  21.7 us
  transfers between devices with their start and end apart: 47, of which 22 were waited for; matrix products, arithmetic and copies ran while one was open for 26% of the time, Pallas kernels for 6%

profile of v4, /device:TPU:0, one launch (start us, length us, event | category | flops | bytes accessed | tf_op | source)
XLA Modules:
  0.0 580.5 jit_solution(5390810417128440764)
XLA Ops:
  30.6 4.9 convert_element_type.326.table_ref
  40.7 7.7 %all-to-all-done.4 = s32[32,1,178]{2,1,0:T(1,128)S(1)} async-done(((s32[32,1,178]{2,1,0:T(1,128)}), s32[32,1,178]{2,1,0:T(1,128)S(1)}, u32[]{:S(2)}, u32[]{:S(2)}) %all-to-all-start.4) | async-done | bytes 22816 | tf_op jit(solution)/shard_map/all_to_all | solution.py:782
  49.2 5.7 fusion.31
  60.3 10.4 %fusion.23 = bf16[2048,768]{1,0:T(8,128)(2,1)} fusion(bf16[1920,768]{1,0:T(8,128)(2,1)} %convert_element_type.326.table_ref, s32[2048]{0:T(1024)S(1)} %bitcast.193), kind=kOutput, calls=%fused_computation.51 | convolution fusion | flops 6045302784 | bytes 6103040 | tf_op jit(solution)/shard_map/dot_general | solution.py:164
  70.7 31.9 %all-to-all-done.5 = bf16[16,48,768]{2,1,0:T(8,128)(2,1)S(1)} async-done(((bf16[16,48,768]{2,1,0:T(8,128)(2,1)}), bf16[16,48,768]{2,1,0:T(8,128)(2,1)S(1)}, u32[]{:S(2)}, u32[]{:S(2)}) %all-to-all-start.5) | async-done | bytes 1179680 | tf_op jit(solution)/shard_map/all_to_all | solution.py:793
  107.5 20.6 %all-gather.2.cloned.1.call-done.mat_ref.up_ref.down_ref = bf16[15,768,768]{2,1,0:T(8,128)(2,1)} async-done(((bf16[15,48,768]{2,1,0:T(8,128)(2,1)}), bf16[15,768,768]{2,1,0:T(8,128)(2,1)}) %all-gather.2.cloned.1.call-update) | async-done | bytes 17694736 | tf_op jit(solution)/shard_map/all_gather | solution.py:847
  128.1 8.6 %shard_map.415.stack_ref.place_ref = bf16[6,512,768]{2,1,0:T(8,128)(2,1)} custom-call(bf16[512,768]{1,0:T(8,128)(2,1)S(1)} %copy.124.features_ref, bf16[512,768]{1,0:T(8,128)(2,1)S(1)} %fusion.32.act_ref, bf16[15,768,768]{2,1,0:T(8,128)(2,1)} %all-gather.2.cloned.1.call-done.mat_ref.up_ref.down_ref, f32[6,1,768]{2,1,0:T(1,128)S(1)} %broadcast_in_dim.282.bias_ref), custom_call_target="tpu_custom_call" | custom-call | tf_op jit(solution)/shard_map/pallas_call | solution.py:411
  139.1 11.6 %shard_map.416.mixed_ref = bf16[512,768]{1,0:T(8,128)(2,1)S(1)} custom-call(s32[1]{0:T(128)} %copy.167.length_ref, bf16[6,512,768]{2,1,0:T(8,128)(2,1)S(1)} %copy-done), custom_call_target="tpu_custom_call" | custom-call | tf_op jit(solution)/shard_map/pallas_call | solution.py:260
  154.0 11.2 %shard_map.417 = (bf16[512,3072]{1,0:T(8,128)(2,1)S(1)}, f32[512,3072]{1,0:T(8,128)}, f32[512,768]{1,0:T(8,128)S(1)}) custom-call(bf16[512,768]{1,0:T(8,128)(2,1)S(1)} %fusion.33.middle_ref, bf16[15,768,768]{2,1,0:T(8,128)(2,1)} %all-gather.2.cloned.1.call-done.mat_ref.up_ref.down_ref, f32[1,3072]{1,0:T(1,128)S(1)} %bitcast.167, ...), custom_call_target="tpu_custom_call" | custom-call | tf_op jit(solution)/shard_map/pallas_call | solution.py:488
  168.0 7.7 %collective-permute-start.7 = (bf16[1,1,1,128,768]{4,3,2,1,0:T(8,128)(2,1)S(1)}, bf16[1,1,1,128,768]{4,3,2,1,0:T(8,128)(2,1)S(1)}, u32[]{:S(2)}, u32[]{:S(2)}) collective-permute-start(bf16[1,1,1,128,768]{4,3,2,1,0:T(8,128)(2,1)S(1)} %fusion.34), channel_id=1, source_target_pairs={{0,16},{2,18},{4,20},{6,22},{8,24},{10,26},{12,28},{14,30},{16,0},... | collective-permute-start | bytes 589832 | tf_op jit(solution)/shard_map/ppermute | solution.py:59
  178.7 6.9 %collective-permute-done.7 = bf16[1,1,1,128,768]{4,3,2,1,0:T(8,128)(2,1)S(1)} collective-permute-done((bf16[1,1,1,128,768]{4,3,2,1,0:T(8,128)(2,1)S(1)}, bf16[1,1,1,128,768]{4,3,2,1,0:T(8,128)(2,1)S(1)}, u32[]{:S(2)}, u32[]{:S(2)}) %collective-permute-start.7) | collective-permute-done | bytes 196640 | tf_op jit(solution)/shard_map/ppermute | solution.py:59
  185.6 6.2 %collective-permute-done.6 = bf16[1,1,1,128,768]{4,3,2,1,0:T(8,128)(2,1)S(1)} collective-permute-done((bf16[1,1,1,128,768]{4,3,2,1,0:T(8,128)(2,1)S(1)}, bf16[1,1,1,128,768]{4,3,2,1,0:T(8,128)(2,1)S(1)}, u32[]{:S(2)}, u32[]{:S(2)}) %collective-permute-start.6) | collective-permute-done | bytes 196640 | tf_op jit(solution)/shard_map/ppermute | solution.py:59
  193.4 17.5 %collective-permute-done.9 = bf16[4,1,1,128,768]{4,3,2,1,0:T(8,128)(2,1)S(1)} collective-permute-done((bf16[4,1,1,128,768]{4,3,2,1,0:T(8,128)(2,1)S(1)}, bf16[4,1,1,128,768]{4,3,2,1,0:T(8,128)(2,1)S(1)}, u32[]{:S(2)}, u32[]{:S(2)}) %collective-permute-start.9) | collective-permute-done | bytes 786464 | tf_op jit(solution)/shard_map/ppermute | solution.py:59
  219.1 11.2 %shard_map.418 = (bf16[2048,1920]{1,0:T(8,128)(2,1)}, f32[8,2048]{1,0:T(8,128)S(1)}) custom-call(bf16[2048,768]{1,0:T(8,128)(2,1)S(1)} %bitcast.164, bf16[1920,768]{1,0:T(8,128)(2,1)S(1)} %copy-done.30), custom_call_target="tpu_custom_call" | custom-call | tf_op jit(solution)/shard_map/pallas_call | solution.py:581
  233.0 9.1 %fusion.115 = f32[2048,768]{1,0:T(8,128)S(1)} fusion(bf16[2048,1920]{1,0:T(8,128)(2,1)} %get-tuple-element.309, bf16[1920,768]{1,0:T(8,128)(2,1)S(1)} %copy-done.30), kind=kOutput, calls=%fused_computation.390 | convolution fusion | flops 6039797760 | bytes 17104896 | tf_op jit(solution)/shard_map/dot_general | solution.py:164
  257.5 6.3 %subtract_convert_fusion = bf16[2048,1920]{1,0:T(8,128)(2,1)S(1)} fusion(bf16[2048,1920]{1,0:T(8,128)(2,1)} %get-tuple-element.309, f32[2048]{0:T(1024)S(1)} %get-tuple-element.455, s32[2048]{0:T(1024)S(1)} %bitcast.194), kind=kLoop, calls=%fused_computation.30 | loop fusion | flops 23592960 | bytes 15745024 | tf_op jit(solution)/shard_map/convert_element_type | solution.py:891
  266.5 6.6 %convolution_convert_fusion = bf16[1920,768]{1,0:T(8,128)(2,1)S(1)} fusion(bf16[2048,1920]{1,0:T(8,128)(2,1)S(1)} %subtract_convert_fusion, bf16[2048,768]{1,0:T(8,128)(2,1)S(1)} %copy-done.42), kind=kOutput, calls=%fused_computation.52 | convolution fusion | flops 6041272320 | bytes 13959168 | tf_op jit(solution)/shard_map/dot_general | solution.py:168
  276.3 9.5 %collective-permute-done.20 = bf16[4,1,1,128,768]{4,3,2,1,0:T(8,128)(2,1)S(1)} collective-permute-done((bf16[4,1,1,128,768]{4,3,2,1,0:T(8,128)(2,1)S(1)}, bf16[4,1,1,128,768]{4,3,2,1,0:T(8,128)(2,1)S(1)}, u32[]{:S(2)}, u32[]{:S(2)}) %collective-permute-start.20) | collective-permute-done | bytes 786464 | tf_op jit(solution)/shard_map/ppermute | solution.py:59
  296.0 13.1 %collective-permute-done.22 = bf16[1,1,1,128,768]{4,3,2,1,0:T(8,128)(2,1)} collective-permute-done((bf16[1,1,1,128,768]{4,3,2,1,0:T(8,128)(2,1)}, bf16[1,1,1,128,768]{4,3,2,1,0:T(8,128)(2,1)}, u32[]{:S(2)}, u32[]{:S(2)}) %collective-permute-start.22) | collective-permute-done | bytes 196640 | tf_op jit(solution)/shard_map/ppermute | solution.py:59
  314.9 15.8 %shard_map.419 = (bf16[2,4,768,768]{3,2,1,0:T(8,128)(2,1)}, f32[1,3072]{1,0:T(1,128)S(1)}, f32[512,768]{1,0:T(8,128)S(1)}) custom-call(bf16[512,768]{1,0:T(8,128)(2,1)S(1)} %get-tuple-element.446.grad_ref, bf16[512,768]{1,0:T(8,128)(2,1)S(1)} %copy-done.7, bf16[512,3072]{1,0:T(8,128)(2,1)} %copy-done.10, f32[512,3072]{1,0:T(8,128)} %get-tuple-element.318.slope_ref, ...), custom_call_target="tpu_custom_call" | custom-call | tf_op jit(solution)/shard_map/pallas_call | solution.py:541
  346.8 17.9 %shard_map.420.grad_ref = bf16[5,512,768]{2,1,0:T(8,128)(2,1)S(1)} custom-call(s32[1]{0:T(128)} %copy.167.length_ref, bf16[6,512,768]{2,1,0:T(8,128)(2,1)} %shard_map.415.stack_ref.place_ref, bf16[512,768]{1,0:T(8,128)(2,1)S(1)} %convolution_convert_fusion.1.grad_ref), custom_call_target="tpu_custom_call" | custom-call | tf_op jit(solution)/shard_map/pallas_call | solution.py:260
  366.7 8.1 %shard_map.421 = (f32[512,768]{1,0:T(8,128)S(1)}, bf16[512,768]{1,0:T(8,128)(2,1)S(1)}, f32[5,1,768]{2,1,0:T(1,128)S(1)}) custom-call(f32[512,768]{1,0:T(8,128)S(1)} %get-tuple-element.449.first_ref, bf16[5,512,768]{2,1,0:T(8,128)(2,1)} %copy-done.1, bf16[15,768,768]{2,1,0:T(8,128)(2,1)} %all-gather.2.cloned.1.call-done.mat_ref.up_ref.down_ref), custom_call_target="tpu_custom_call" | custom-call | tf_op jit(solution)/shard_map/pallas_call | solution.py:306
  384.0 6.3 %shard_map.422 = bf16[4,768,768]{2,1,0:T(8,128)(2,1)} custom-call(bf16[512,768]{1,0:T(8,128)(2,1)S(1)} %copy-done.5, bf16[512,768]{1,0:T(8,128)(2,1)S(1)} %copy-done.14, bf16[5,512,768]{2,1,0:T(8,128)(2,1)} %copy-done.1, bf16[512,768]{1,0:T(8,128)(2,1)S(1)} %copy-done.12), custom_call_target="tpu_custom_call" | custom-call | tf_op jit(solution)/shard_map/pallas_call | solution.py:339
  404.2 4.6 all-to-all-start.6
  421.4 21.9 %all-to-all-done.6 = bf16[16,48,768]{2,1,0:T(8,128)(2,1)} async-done(((bf16[16,48,768]{2,1,0:T(8,128)(2,1)}), bf16[16,48,768]{2,1,0:T(8,128)(2,1)}, u32[]{:S(2)}, u32[]{:S(2)}) %all-to-all-start.6) | async-done | bytes 1179680 | tf_op jit(solution)/shard_map/all_to_all | solution.py:925
  447.0 11.1 %reduce-scatter.2.cloned.1.call-done = bf16[2,4,48,768]{3,2,1,0:T(8,128)(2,1)} async-done(((bf16[2,4,768,768]{3,2,1,0:T(8,128)(2,1)}), bf16[2,4,48,768]{3,2,1,0:T(8,128)(2,1)}) %reduce-scatter.2.cloned.1.call-update) | async-done | bytes 589840 | tf_op jit(solution)/shard_map/reduce_scatter | solution.py:664
  467.0 4.7 collective-permute-done.28
  471.7 16.0 %collective-permute-start.34 = (bf16[4,1,1,1,48,768]{5,4,0,3,2,1:T(8,128)(2,1)}, bf16[4,1,1,1,48,768]{5,4,0,3,2,1:T(8,128)(2,1)}, u32[]{:S(2)}, u32[]{:S(2)}) collective-permute-start(bf16[4,1,1,1,48,768]{5,4,0,3,2,1:T(8,128)(2,1)} %get-tuple-element.487), channel_id=1, source_target_pairs={{0,16},{2,18},{4,20},{6,22},{8,24},{10,26},{12,28},{14,30},{16,0},... | collective-permute-start | bytes 884744 | tf_op jit(solution)/shard_map/ppermute | solution.py:59
  487.6 4.4 fusion.20
  493.1 8.5 %add_add_fusion.1 = f32[1920,768]{1,0:T(8,128)} fusion(f32[1920,768]{1,0:T(8,128)S(1)} %fusion.20, bf16[1920,768]{1,0:T(8,128)(2,1)S(1)} %copy-done.44, bf16[576,768]{1,0:T(8,128)(2,1)} %collective-permute-done.19, bf16[576,768]{1,0:T(8,128)(2,1)} %collective-permute-done.18, bf16[384,768]{1,0:T(8,128)(2,1)} %collective-permute-done.17, ...), kind=kOutput, calls=%fused_computation.41 | convolution fusion | flops 2284093440 | bytes 18877440 | tf_op jit(solution)/shard_map/dot_general | solution.py:168
  531.8 4.1 collective-permute-done.40
  558.6 8.0 %multiply_subtract_fusion = (f32[1920,768]{1,0:T(8,128)}, f32[1920,768]{1,0:T(8,128)}) fusion(f32[1920,768]{1,0:T(8,128)} %param.33, f32[1920,768]{1,0:T(8,128)} %get-tuple-element.751, f32[768]{0:T(1024)S(1)} %get-tuple-element.366, f32[1920]{0:T(1024)S(1)} %get-tuple-element.435, f32[]{:T(128)S(6)} %min.13), kind=kLoop, calls=%fused_computation.40 | loop fusion | flops 5898240 | bytes 23603716 | tf_op jit(solution)/shard_map/sub | solution.py:1020
  (596 shorter events, 219.9 us)
Async XLA Ops:
  7.2 120.9 %all-gather.2.cloned.1.call-start = ((), (), s32[]{:S(2)}) async-start(), calls=%async_computation.8 | async-start | bytes 18800640 | tf_op jit(solution)/shard_map/all_gather | solution.py:847
  27.2 9.0 %collective-permute-start.5 = (bf16[8,720]{1,0:T(8,128)(2,1)S(1)}, bf16[8,720]{1,0:T(8,128)(2,1)S(1)}, u32[]{:S(2)}, u32[]{:S(2)}) collective-permute-start(bf16[8,720]{1,0:T(8,128)(2,1)S(1)} %pad_maximum_fusion.10), channel_id=1, source_target_pairs={{0,16},{2,18},{4,20},{6,22},{8,24},{10,26},{12,28},{14,30},{16,0},... | collective-permute-start | bytes 34568 | tf_op jit(solution)/shard_map/ppermute | solution.py:833
  36.7 11.8 %all-to-all-start.4 = ((s32[32,1,178]{2,1,0:T(1,128)}), s32[32,1,178]{2,1,0:T(1,128)S(1)}, u32[]{:S(2)}, u32[]{:S(2)}) async-start(s32[32,1,178]{2,1,0:T(1,128)} %all_to_all.40), calls=%async_computation.4 | async-start | bytes 65536 | tf_op jit(solution)/shard_map/all_to_all | solution.py:782
  54.9 47.7 %all-to-all-start.5 = ((bf16[16,48,768]{2,1,0:T(8,128)(2,1)}), bf16[16,48,768]{2,1,0:T(8,128)(2,1)S(1)}, u32[]{:S(2)}, u32[]{:S(2)}) async-start(bf16[16,48,768]{2,1,0:T(8,128)(2,1)} %bitcast.11), calls=%async_computation.5 | async-start | bytes 2359296 | tf_op jit(solution)/shard_map/all_to_all | solution.py:793
  58.6 399.5 %reduce-scatter.2.cloned.1.call-start = ((), (), s32[]{:S(2)}) async-start(), calls=%async_computation.9 | async-start | bytes 10027008 | tf_op jit(solution)/shard_map/reduce_scatter | solution.py:664
  168.0 17.6 %collective-permute-start.7 = (bf16[1,1,1,128,768]{4,3,2,1,0:T(8,128)(2,1)S(1)}, bf16[1,1,1,128,768]{4,3,2,1,0:T(8,128)(2,1)S(1)}, u32[]{:S(2)}, u32[]{:S(2)}) collective-permute-start(bf16[1,1,1,128,768]{4,3,2,1,0:T(8,128)(2,1)S(1)} %fusion.34), channel_id=1, source_target_pairs={{0,16},{2,18},{4,20},{6,22},{8,24},{10,26},{12,28},{14,30},{16,0},... | collective-permute-start | bytes 589832 | tf_op jit(solution)/shard_map/ppermute | solution.py:59
  175.7 9.9 %collective-permute-start.8 = (bf16[1,1,1,128,768]{4,3,2,1,0:T(8,128)(2,1)S(1)}, bf16[1,1,1,128,768]{4,3,2,1,0:T(8,128)(2,1)S(1)}, u32[]{:S(2)}, u32[]{:S(2)}) collective-permute-start(bf16[1,1,1,128,768]{4,3,2,1,0:T(8,128)(2,1)S(1)} %fusion.34), channel_id=1, source_target_pairs={{0,24},{2,26},{4,28},{6,30},{8,0},{10,2},{12,4},{14,6},{16,8},{18,... | collective-permute-start | bytes 589832 | tf_op jit(solution)/shard_map/ppermute | solution.py:59
  178.2 13.6 %collective-permute-start.6 = (bf16[1,1,1,128,768]{4,3,2,1,0:T(8,128)(2,1)S(1)}, bf16[1,1,1,128,768]{4,3,2,1,0:T(8,128)(2,1)S(1)}, u32[]{:S(2)}, u32[]{:S(2)}) collective-permute-start(bf16[1,1,1,128,768]{4,3,2,1,0:T(8,128)(2,1)S(1)} %fusion.34), channel_id=1, source_target_pairs={{0,8},{2,10},{4,12},{6,14},{8,16},{10,18},{12,20},{14,22},{16,24},... | collective-permute-start | bytes 589832 | tf_op jit(solution)/shard_map/ppermute | solution.py:59
  192.0 18.9 %collective-permute-start.9 = (bf16[4,1,1,128,768]{4,3,2,1,0:T(8,128)(2,1)S(1)}, bf16[4,1,1,128,768]{4,3,2,1,0:T(8,128)(2,1)S(1)}, u32[]{:S(2)}, u32[]{:S(2)}) collective-permute-start(bf16[4,1,1,128,768]{4,3,2,1,0:T(8,128)(2,1)S(1)} %pad_maximum_fusion.5), channel_id=1, source_target_pairs={{0,4},{2,6},{4,0},{6,2},{8,12},{10,14},{12,8},{14,10},{16,20},{18,... | collective-permute-start | bytes 2359304 | tf_op jit(solution)/shard_map/ppermute | solution.py:59
  231.7 10.5 %collective-permute-start.12 = (f32[2,16,128]{2,1,0:T(8,128)S(1)}, f32[2,16,128]{2,1,0:T(8,128)S(1)}, u32[]{:S(2)}, u32[]{:S(2)}) collective-permute-start(f32[2,16,128]{2,1,0:T(8,128)S(1)} %pad_maximum_fusion.7), channel_id=1, source_target_pairs={{0,4},{2,6},{4,0},{6,2},{8,12},{10,14},{12,8},{14,10},{16,20},{18,... | collective-permute-start | bytes 49160 | tf_op jit(solution)/shard_map/ppermute | solution.py:106
  265.8 20.0 %collective-permute-start.20 = (bf16[4,1,1,128,768]{4,3,2,1,0:T(8,128)(2,1)S(1)}, bf16[4,1,1,128,768]{4,3,2,1,0:T(8,128)(2,1)S(1)}, u32[]{:S(2)}, u32[]{:S(2)}) collective-permute-start(bf16[4,1,1,128,768]{4,3,2,1,0:T(8,128)(2,1)S(1)} %dynamic-slice_convert_fusion), channel_id=1, source_target_pairs={{0,4},{2,6},{4,0},{6,2},{8,12},{10,14},{12,8},{14,10},{16,20},{18,... | collective-permute-start | bytes 2359304 | tf_op jit(solution)/shard_map/ppermute | solution.py:59
  274.3 36.0 %collective-permute-start.16 = (bf16[384,768]{1,0:T(8,128)(2,1)}, bf16[384,768]{1,0:T(8,128)(2,1)}, u32[]{:S(2)}, u32[]{:S(2)}) collective-permute-start(bf16[384,768]{1,0:T(8,128)(2,1)} %get-tuple-element.478), channel_id=1, source_target_pairs={{0,1},{1,0},{2,3},{3,2},{4,5},{5,4},{6,7},{7,6},{8,9},{9,8},{10,11... | collective-permute-start | bytes 1769480 | tf_op jit(solution)/shard_map/ppermute | solution.py:59
  275.7 34.6 %collective-permute-start.17 = (bf16[384,768]{1,0:T(8,128)(2,1)}, bf16[384,768]{1,0:T(8,128)(2,1)}, u32[]{:S(2)}, u32[]{:S(2)}) collective-permute-start(bf16[384,768]{1,0:T(8,128)(2,1)} %get-tuple-element.477), channel_id=1, source_target_pairs={{0,1},{1,0},{2,3},{3,2},{4,5},{5,4},{6,7},{7,6},{8,9},{9,8},{10,11... | collective-permute-start | bytes 1769480 | tf_op jit(solution)/shard_map/ppermute | solution.py:59
  290.2 18.8 %collective-permute-start.22 = (bf16[1,1,1,128,768]{4,3,2,1,0:T(8,128)(2,1)}, bf16[1,1,1,128,768]{4,3,2,1,0:T(8,128)(2,1)}, u32[]{:S(2)}, u32[]{:S(2)}) collective-permute-start(bf16[1,1,1,128,768]{4,3,2,1,0:T(8,128)(2,1)} %get-tuple-element.314), channel_id=1, source_target_pairs={{0,16},{2,18},{4,20},{6,22},{8,24},{10,26},{12,28},{14,30},{16,0},... | collective-permute-start | bytes 589832 | tf_op jit(solution)/shard_map/ppermute | solution.py:59
  291.5 17.6 %collective-permute-start.21 = (bf16[1,1,1,128,768]{4,3,2,1,0:T(8,128)(2,1)S(1)}, bf16[1,1,1,128,768]{4,3,2,1,0:T(8,128)(2,1)}, u32[]{:S(2)}, u32[]{:S(2)}) collective-permute-start(bf16[1,1,1,128,768]{4,3,2,1,0:T(8,128)(2,1)S(1)} %get-tuple-element.313), channel_id=1, source_target_pairs={{0,8},{2,10},{4,12},{6,14},{8,16},{10,18},{12,20},{14,22},{16,24},... | collective-permute-start | bytes 589832 | tf_op jit(solution)/shard_map/ppermute | solution.py:59
  334.8 31.9 %collective-permute-start.18 = (bf16[576,768]{1,0:T(8,128)(2,1)}, bf16[576,768]{1,0:T(8,128)(2,1)}, u32[]{:S(2)}, u32[]{:S(2)}) collective-permute-start(bf16[576,768]{1,0:T(8,128)(2,1)} %get-tuple-element.476), channel_id=1, source_target_pairs={{0,1},{1,0},{2,3},{3,2},{4,5},{5,4},{6,7},{7,6},{8,9},{9,8},{10,11... | collective-permute-start | bytes 2654216 | tf_op jit(solution)/shard_map/ppermute | solution.py:59
  336.2 38.6 %collective-permute-start.19 = (bf16[576,768]{1,0:T(8,128)(2,1)}, bf16[576,768]{1,0:T(8,128)(2,1)}, u32[]{:S(2)}, u32[]{:S(2)}) collective-permute-start(bf16[576,768]{1,0:T(8,128)(2,1)} %get-tuple-element.475), channel_id=1, source_target_pairs={{0,1},{1,0},{2,3},{3,2},{4,5},{5,4},{6,7},{7,6},{8,9},{9,8},{10,11... | collective-permute-start | bytes 2654216 | tf_op jit(solution)/shard_map/ppermute | solution.py:59
  404.0 11.7 %collective-permute-start.25 = (bf16[3,4,2,1,48,768]{5,4,0,3,2,1:T(8,128)(2,1)}, bf16[3,4,2,1,48,768]{5,4,0,3,2,1:T(8,128)(2,1)}, u32[]{:S(2)}, u32[]{:S(2)}) collective-permute-start(bf16[3,4,2,1,48,768]{5,4,0,3,2,1:T(8,128)(2,1)} %copy.143), channel_id=1, source_target_pairs={{0,2},{2,0},{4,6},{6,4},{8,10},{10,8},{12,14},{14,12},{16,18},{18,... | collective-permute-start | bytes 5308424 | tf_op jit(solution)/shard_map/ppermute | solution.py:59
  404.2 39.1 %all-to-all-start.6 = ((bf16[16,48,768]{2,1,0:T(8,128)(2,1)}), bf16[16,48,768]{2,1,0:T(8,128)(2,1)}, u32[]{:S(2)}, u32[]{:S(2)}) async-start(bf16[16,48,768]{2,1,0:T(8,128)(2,1)} %bitcast.176), calls=%async_computation.6 | async-start | bytes 2359296 | tf_op jit(solution)/shard_map/all_to_all | solution.py:925
  410.8 47.3 %collective-permute-start.27 = (bf16[4,4,1,1,48,768]{5,4,0,3,2,1:T(8,128)(2,1)}, bf16[4,4,1,1,48,768]{5,4,0,3,2,1:T(8,128)(2,1)}, u32[]{:S(2)}, u32[]{:S(2)}) collective-permute-start(bf16[4,4,1,1,48,768]{5,4,0,3,2,1:T(8,128)(2,1)} %constant_dynamic-slice_fusion.11), channel_id=1, source_target_pairs={{0,4},{2,6},{4,0},{6,2},{8,12},{10,14},{12,8},{14,10},{16,20},{18,... | collective-permute-start | bytes 3538952 | tf_op jit(solution)/shard_map/ppermute | solution.py:59
  420.0 40.5 %collective-permute-start.26 = (bf16[3,4,2,1,48,384]{5,4,0,3,2,1:T(8,128)(2,1)}, bf16[3,4,2,1,48,384]{5,4,0,3,2,1:T(8,128)(2,1)}, u32[]{:S(2)}, u32[]{:S(2)}) collective-permute-start(bf16[3,4,2,1,48,384]{5,4,0,3,2,1:T(8,128)(2,1)} %constant_dynamic-slice_fusion.8), channel_id=1, source_target_pairs={{0,1},{1,0},{2,3},{3,2},{4,5},{5,4},{6,7},{7,6},{8,9},{9,8},{10,11... | collective-permute-start | bytes 2654216 | tf_op jit(solution)/shard_map/ppermute | solution.py:59
  443.3 28.4 %collective-permute-start.28 = (bf16[768,768]{1,0:T(8,128)(2,1)}, bf16[768,768]{1,0:T(8,128)(2,1)}, u32[]{:S(2)}, u32[]{:S(2)}) collective-permute-start(bf16[768,768]{1,0:T(8,128)(2,1)} %bitcast.46), channel_id=1, source_target_pairs={{0,1},{1,0},{2,3},{3,2},{4,5},{5,4},{6,7},{7,6},{8,9},{9,8},{10,11... | collective-permute-start | bytes 3538952 | tf_op jit(solution)/shard_map/ppermute | solution.py:59
  462.8 29.2 %collective-permute-start.29 = (bf16[3,4,1,1,48,384]{5,4,0,3,2,1:T(8,128)(2,1)S(1)}, bf16[3,4,1,1,48,384]{5,4,0,3,2,1:T(8,128)(2,1)S(1)}, u32[]{:S(2)}, u32[]{:S(2)}) collective-permute-start(bf16[3,4,1,1,48,384]{5,4,0,3,2,1:T(8,128)(2,1)S(1)} %constant_dynamic-slice_fusion.6), channel_id=1, source_target_pairs={{0,4},{2,6},{4,0},{6,2},{8,12},{10,14},{12,8},{14,10},{16,20},{18,... | collective-permute-start | bytes 1327112 | tf_op jit(solution)/shard_map/ppermute | solution.py:59
  464.4 43.5 %collective-permute-start.33 = (bf16[4,1,1,1,48,768]{5,4,0,3,2,1:T(8,128)(2,1)}, bf16[4,1,1,1,48,768]{5,4,0,3,2,1:T(8,128)(2,1)}, u32[]{:S(2)}, u32[]{:S(2)}) collective-permute-start(bf16[4,1,1,1,48,768]{5,4,0,3,2,1:T(8,128)(2,1)} %get-tuple-element.488), channel_id=1, source_target_pairs={{0,8},{2,10},{4,12},{6,14},{8,16},{10,18},{12,20},{14,22},{16,24},... | collective-permute-start | bytes 884744 | tf_op jit(solution)/shard_map/ppermute | solution.py:59
  466.2 57.1 %collective-permute-start.38 = (bf16[2,4,48,768]{3,2,1,0:T(8,128)(2,1)}, bf16[2,4,48,768]{3,2,1,0:T(8,128)(2,1)}, u32[]{:S(2)}, u32[]{:S(2)}) collective-permute-start(bf16[2,4,48,768]{3,2,1,0:T(8,128)(2,1)} %reduce-scatter.2.cloned.1.call-done), channel_id=1, source_target_pairs={{0,1},{1,0},{2,3},{3,2},{4,5},{5,4},{6,7},{7,6},{8,9},{9,8},{10,11... | collective-permute-start | bytes 1769480 | tf_op jit(solution)/shard_map/ppermute | solution.py:59
  471.7 36.3 %collective-permute-start.34 = (bf16[4,1,1,1,48,768]{5,4,0,3,2,1:T(8,128)(2,1)}, bf16[4,1,1,1,48,768]{5,4,0,3,2,1:T(8,128)(2,1)}, u32[]{:S(2)}, u32[]{:S(2)}) collective-permute-start(bf16[4,1,1,1,48,768]{5,4,0,3,2,1:T(8,128)(2,1)} %get-tuple-element.487), channel_id=1, source_target_pairs={{0,16},{2,18},{4,20},{6,22},{8,24},{10,26},{12,28},{14,30},{16,0},... | collective-permute-start | bytes 884744 | tf_op jit(solution)/shard_map/ppermute | solution.py:59
  501.9 10.3 %collective-permute-start.35 = (bf16[4,1,1,1,48,768]{5,4,0,3,2,1:T(8,128)(2,1)S(1)}, bf16[4,1,1,1,48,768]{5,4,0,3,2,1:T(8,128)(2,1)S(1)}, u32[]{:S(2)}, u32[]{:S(2)}) collective-permute-start(bf16[4,1,1,1,48,768]{5,4,0,3,2,1:T(8,128)(2,1)S(1)} %get-tuple-element.486), channel_id=1, source_target_pairs={{0,24},{2,26},{4,28},{6,30},{8,0},{10,2},{12,4},{14,6},{16,8},{18,... | collective-permute-start | bytes 884744 | tf_op jit(solution)/shard_map/ppermute | solution.py:59
  501.9 19.6 %collective-permute-start.30 = (bf16[3,1,1,1,48,384]{5,4,0,3,2,1:T(8,128)(2,1)}, bf16[3,1,1,1,48,384]{5,4,0,3,2,1:T(8,128)(2,1)S(1)}, u32[]{:S(2)}, u32[]{:S(2)}) collective-permute-start(bf16[3,1,1,1,48,384]{5,4,0,3,2,1:T(8,128)(2,1)} %get-tuple-element.501), channel_id=1, source_target_pairs={{0,8},{2,10},{4,12},{6,14},{8,16},{10,18},{12,20},{14,22},{16,24},... | collective-permute-start | bytes 331784 | tf_op jit(solution)/shard_map/ppermute | solution.py:59
  507.9 13.6 %collective-permute-start.31 = (bf16[3,1,1,1,48,384]{5,4,0,3,2,1:T(8,128)(2,1)S(1)}, bf16[3,1,1,1,48,384]{5,4,0,3,2,1:T(8,128)(2,1)S(1)}, u32[]{:S(2)}, u32[]{:S(2)}) collective-permute-start(bf16[3,1,1,1,48,384]{5,4,0,3,2,1:T(8,128)(2,1)S(1)} %copy-done.66), channel_id=1, source_target_pairs={{0,16},{2,18},{4,20},{6,22},{8,24},{10,26},{12,28},{14,30},{16,0},... | collective-permute-start | bytes 331784 | tf_op jit(solution)/shard_map/ppermute | solution.py:59
  508.0 13.5 %collective-permute-start.32 = (bf16[3,1,1,1,48,384]{5,4,0,3,2,1:T(8,128)(2,1)S(1)}, bf16[3,1,1,1,48,384]{5,4,0,3,2,1:T(8,128)(2,1)S(1)}, u32[]{:S(2)}, u32[]{:S(2)}) collective-permute-start(bf16[3,1,1,1,48,384]{5,4,0,3,2,1:T(8,128)(2,1)S(1)} %copy-done.65), channel_id=1, source_target_pairs={{0,24},{2,26},{4,28},{6,30},{8,0},{10,2},{12,4},{14,6},{16,8},{18,... | collective-permute-start | bytes 331784 | tf_op jit(solution)/shard_map/ppermute | solution.py:59
  514.1 14.1 %collective-permute-start.37 = (bf16[4,48,768]{2,1,0:T(8,128)(2,1)}, bf16[4,48,768]{2,1,0:T(8,128)(2,1)S(1)}, u32[]{:S(2)}, u32[]{:S(2)}) collective-permute-start(bf16[4,48,768]{2,1,0:T(8,128)(2,1)} %fusion.48), channel_id=1, source_target_pairs={{0,1},{1,0},{2,3},{3,2},{4,5},{5,4},{6,7},{7,6},{8,9},{9,8},{10,11... | collective-permute-start | bytes 884744 | tf_op jit(solution)/shard_map/ppermute | solution.py:59
  557.4 14.2 %collective-permute-start.43 = (f32[4]{0:T(128)S(1)}, f32[4]{0:T(128)S(1)}, u32[]{:S(2)}, u32[]{:S(2)}) collective-permute-start(f32[4]{0:T(128)S(1)} %slice_bitcast_fusion.4), channel_id=1, source_target_pairs={{0,1},{1,0},{2,3},{3,2},{4,5},{5,4},{6,7},{7,6},{8,9},{9,8},{10,11... | collective-permute-start | bytes 56 | tf_op jit(solution)/shard_map/ppermute | solution.py:106
  (148 other events, 1637.0 us)
Sparse Core Ops, SparseCore 0:
  11.8 116.2 all-gather.1
  332.0 126.0 reduce-scatter.1

commit v5 on v4

--- a/solution.py
+++ b/solution.py
@@ -245,7 +245,7 @@
 FREE = pl.CostEstimate(flops=0, transcendentals=0, bytes_accessed=0)
 
 
-ROOMY = pltpu.CompilerParams(vmem_limit_bytes=48 * 1024 * 1024)
+ROOMY = pltpu.CompilerParams(vmem_limit_bytes=36 * 1024 * 1024)
 
 
 def attention_call(kernel, lengths, stack, arrays, stacked):
@@ -810,15 +810,13 @@
     embedded = after(embedded, label_rows)
 
     depth = mats.shape[0]
-    items = depth + 3
+    first_up, after_up = 1 + depth, 1 + depth + up_cols.shape[0] // width
+    items = after_up + 1
     lane = jnp.arange(width)
-    singles = jnp.pad(jnp.sum(mats_rows, axis=1), (1, width - 1 - depth))
-    for index, value in (
-        (0, jnp.sum(table_rows)),
-        (items - 2, jnp.sum(up_rows)),
-        (items - 1, jnp.sum(down_rows)),
-    ):
-        singles = jnp.where(lane == index, value, singles)
+    singles = jnp.pad(jnp.sum(mats_rows, axis=1), (1, width - first_up))
+    singles = jnp.where(lane == 0, jnp.sum(table_rows), singles)
+    singles = jnp.where((lane >= first_up) & (lane < after_up), jnp.sum(up_rows), singles)
+    singles = jnp.where(lane == after_up, jnp.sum(down_rows), singles)
     embedded = after(embedded, singles)
 
     small = jnp.concatenate([vectors.astype(BFLOAT).reshape(-1), up_bias.astype(BFLOAT)])[None]
@@ -997,18 +995,16 @@
     def renewed(old, value):
         return DECAY * old + (1.0 - DECAY) * (value + TINY_TERM)
 
-    first_up, after_up = 1 + depth, 1 + depth + feed_cols
-    of_item = [[k] for k in range(first_up)] + [list(range(first_up, after_up)), [after_up]]
-    item_totals = jnp.concatenate(
-        [totals[:first_up], jnp.sum(totals[first_up:after_up])[None], totals[after_up:]]
-    )
-    tall = jnp.array([size[0] for size in sizes], FLOAT)
-    wide = jnp.array([size[1] for size in sizes], FLOAT)
-    means = renewed(sums[-1, :items] / tall, square * item_totals / (tall * wide))
-    repeats = [len(rows) for rows in of_item]
-    tall_rows = jnp.array([s for size, n in zip(sizes, repeats) for s in [size[0]] * n], FLOAT)
-    mean_rows = jnp.concatenate(
-        [means[:first_up], jnp.broadcast_to(means[first_up], (feed_cols,)), means[first_up + 1 :]]
+    repeats = [1] * first_up + [feed_cols, 1]
+    tall_rows, wide_rows = (
+        jnp.array([size[k] for size, n in zip(sizes, repeats) for _ in range(n)], FLOAT)
+        for k in range(2)
+    )
+    row = jnp.arange(items)
+    of_up = (row >= first_up) & (row < after_up)
+    item_totals = jnp.where(of_up, jnp.sum(jnp.where(of_up, totals, 0.0)), totals)
+    mean_rows = renewed(
+        sums[-1, :items] / tall_rows, square * item_totals / (tall_rows * wide_rows)
     )
     cols_new = renewed(cols_old, square * sums[:-1] / tall_rows[:, None])
     col_factors = lax.rsqrt(cols_new / mean_rows[:, None])

time: 589 us -> 572 us (0.971)
  starting transfers between devices: 86.4 us -> 75.9 us
  Pallas kernels: 94.7 us -> 85.5 us
    reduce_scatter x1, waiting for transfers between devices: 11.1 us -> 28.9 us  [layer_backward(): lax.psum_scatter(grad_feeds, 'fsdp', scatter_dimension=2, tiled=True)]
    ppermute x29, starting transfers between devices: 53.2 us -> 38.7 us  [shifted(): return lax.ppermute(value, line.axis, pairs)]
    all_to_all x1, waiting for transfers between devices: 21.9 us -> 12.5 us  [give(): lax.all_to_all(rows.reshape(groups, stride, width), 'fsdp', 0, 0, tiled=T...]
    unnamed x271 -> x231, local copies, waits for them, and re-layouts: 21.7 us -> 25.8 us
where the time goes in v5:
time: 572 us; the launch traced here: 564 us
  waiting for transfers between devices  175 us (31%)
  other arithmetic  97.6 us (17%)
  Pallas kernels  85.5 us (15%)
  starting transfers between devices  75.9 us (13%)
  matrix products  54.3 us (9%)
  local copies, waits for them, and re-layouts  53 us (9%)
  between operations  22.2 us (4%)
    ppermute x29, waiting for transfers between devices, shifted(): return lax.ppermute(value, line.axis, pairs)  61 us
    ppermute x29, starting transfers between devices, shifted(): return lax.ppermute(value, line.axis, pairs)  38.7 us
    all_to_all x1, waiting for transfers between devices, fetch(): lax.all_to_all(rows.reshape(groups, stride, width), 'fsdp', 0, 0, tiled=T...  31.8 us
    pallas_call x2, Pallas kernels, attention_call(): pl.pallas_call(kernel, grid=(pages, width // LANES), in_specs=[pl.BlockSp...  29.3 us
    reduce_scatter x1, waiting for transfers between devices, layer_backward(): lax.psum_scatter(grad_feeds, 'fsdp', scatter_dimension=2, tiled=True)  28.9 us
    dot_general x6, matrix products, product(): return jnp.dot(left, right, preferred_element_type=FLOAT)  28 us
    unnamed x231, local copies, waits for them, and re-layouts  25.8 us
    dot_general x7, matrix products, contract_rows(): lax.dot_general(left, right, (((0,), (0,)), ((), ())), preferred_element_...  23.8 us
  transfers between devices with their start and end apart: 47, of which 22 were waited for; matrix products, arithmetic and copies ran while one was open for 26% of the time, Pallas kernels for 6%

profile of v5, /device:TPU:0, one launch (start us, length us, event | category | flops | bytes accessed | tf_op | source)
XLA Modules:
  0.0 564.1 jit_solution(2401114968110751945)
XLA Ops:
  30.6 4.6 convert_element_type.326.table_ref
  36.4 3.9 all-to-all-start.4
  40.4 7.7 %all-to-all-done.4 = s32[32,1,178]{2,1,0:T(1,128)S(1)} async-done(((s32[32,1,178]{2,1,0:T(1,128)}), s32[32,1,178]{2,1,0:T(1,128)S(1)}, u32[]{:S(2)}, u32[]{:S(2)}) %all-to-all-start.4) | async-done | bytes 22816 | tf_op jit(solution)/shard_map/all_to_all | solution.py:782
  48.9 5.7 %fusion.31 = bf16[768,768]{1,0:T(8,128)(2,1)} fusion(bf16[1920,768]{1,0:T(8,128)(2,1)} %convert_element_type.326.table_ref, s32[768]{0:T(1024)S(1)} %get-tuple-element.386), kind=kOutput, calls=%fused_computation.93 | convolution fusion | flops 2266988544 | bytes 4131840 | tf_op jit(solution)/shard_map/dot_general | solution.py:164
  60.0 10.4 %fusion.23 = bf16[2048,768]{1,0:T(8,128)(2,1)} fusion(bf16[1920,768]{1,0:T(8,128)(2,1)} %convert_element_type.326.table_ref, s32[2048]{0:T(1024)S(1)} %bitcast.194), kind=kOutput, calls=%fused_computation.51 | convolution fusion | flops 6045302784 | bytes 6103040 | tf_op jit(solution)/shard_map/dot_general | solution.py:164
  70.5 31.8 %all-to-all-done.5 = bf16[16,48,768]{2,1,0:T(8,128)(2,1)S(1)} async-done(((bf16[16,48,768]{2,1,0:T(8,128)(2,1)}), bf16[16,48,768]{2,1,0:T(8,128)(2,1)S(1)}, u32[]{:S(2)}, u32[]{:S(2)}) %all-to-all-start.5) | async-done | bytes 1179680 | tf_op jit(solution)/shard_map/all_to_all | solution.py:793
  108.8 19.3 %all-gather.2.cloned.1.call-done.mat_ref.up_ref.down_ref = bf16[15,768,768]{2,1,0:T(8,128)(2,1)} async-done(((bf16[15,48,768]{2,1,0:T(8,128)(2,1)}), bf16[15,768,768]{2,1,0:T(8,128)(2,1)}) %all-gather.2.cloned.1.call-update) | async-done | bytes 17694736 | tf_op jit(solution)/shard_map/all_gather | solution.py:845
  128.1 7.2 %shard_map.406.stack_ref.place_ref = bf16[6,512,768]{2,1,0:T(8,128)(2,1)S(1)} custom-call(bf16[512,768]{1,0:T(8,128)(2,1)S(1)} %copy.123.features_ref, bf16[512,768]{1,0:T(8,128)(2,1)S(1)} %fusion.32.act_ref, bf16[15,768,768]{2,1,0:T(8,128)(2,1)} %all-gather.2.cloned.1.call-done.mat_ref.up_ref.down_ref, f32[6,1,768]{2,1,0:T(1,128)S(1)} %broadcast_in_dim.284.bias_ref), custom_call_target="tpu_custom_call" | custom-call | tf_op jit(solution)/shard_map/pallas_call | solution.py:411
  135.3 11.7 %shard_map.407.mixed_ref = bf16[512,768]{1,0:T(8,128)(2,1)S(1)} custom-call(s32[1]{0:T(128)} %copy.166.length_ref, bf16[6,512,768]{2,1,0:T(8,128)(2,1)S(1)} %shard_map.406.stack_ref.place_ref), custom_call_target="tpu_custom_call" | custom-call | tf_op jit(solution)/shard_map/pallas_call | solution.py:260
  150.2 9.9 %shard_map.408 = (bf16[512,3072]{1,0:T(8,128)(2,1)S(1)}, f32[512,3072]{1,0:T(8,128)S(1)}, f32[512,768]{1,0:T(8,128)S(1)}) custom-call(bf16[512,768]{1,0:T(8,128)(2,1)S(1)} %fusion.33.middle_ref, bf16[15,768,768]{2,1,0:T(8,128)(2,1)} %all-gather.2.cloned.1.call-done.mat_ref.up_ref.down_ref, f32[1,3072]{1,0:T(1,128)S(1)} %bitcast.168, ...), custom_call_target="tpu_custom_call" | custom-call | tf_op jit(solution)/shard_map/pallas_call | solution.py:488
  165.6 7.7 %collective-permute-start.7 = (bf16[1,1,1,128,768]{4,3,2,1,0:T(8,128)(2,1)S(1)}, bf16[1,1,1,128,768]{4,3,2,1,0:T(8,128)(2,1)S(1)}, u32[]{:S(2)}, u32[]{:S(2)}) collective-permute-start(bf16[1,1,1,128,768]{4,3,2,1,0:T(8,128)(2,1)S(1)} %fusion.34), channel_id=1, source_target_pairs={{0,16},{2,18},{4,20},{6,22},{8,24},{10,26},{12,28},{14,30},{16,0},... | collective-permute-start | bytes 589832 | tf_op jit(solution)/shard_map/ppermute | solution.py:59
  175.9 7.2 %collective-permute-done.7 = bf16[1,1,1,128,768]{4,3,2,1,0:T(8,128)(2,1)S(1)} collective-permute-done((bf16[1,1,1,128,768]{4,3,2,1,0:T(8,128)(2,1)S(1)}, bf16[1,1,1,128,768]{4,3,2,1,0:T(8,128)(2,1)S(1)}, u32[]{:S(2)}, u32[]{:S(2)}) %collective-permute-start.7) | collective-permute-done | bytes 196640 | tf_op jit(solution)/shard_map/ppermute | solution.py:59
  184.5 5.0 collective-permute-done.6
  193.0 17.8 %collective-permute-done.9 = bf16[4,1,1,128,768]{4,3,2,1,0:T(8,128)(2,1)} collective-permute-done((bf16[4,1,1,128,768]{4,3,2,1,0:T(8,128)(2,1)}, bf16[4,1,1,128,768]{4,3,2,1,0:T(8,128)(2,1)}, u32[]{:S(2)}, u32[]{:S(2)}) %collective-permute-start.9) | collective-permute-done | bytes 786464 | tf_op jit(solution)/shard_map/ppermute | solution.py:59
  223.0 9.9 %shard_map.409 = (bf16[2048,1920]{1,0:T(8,128)(2,1)S(1)}, f32[8,2048]{1,0:T(8,128)S(1)}) custom-call(bf16[2048,768]{1,0:T(8,128)(2,1)S(1)} %bitcast.164, bf16[1920,768]{1,0:T(8,128)(2,1)S(1)} %copy-done.30), custom_call_target="tpu_custom_call" | custom-call | tf_op jit(solution)/shard_map/pallas_call | solution.py:581
  235.8 6.7 %fusion.115 = f32[2048,768]{1,0:T(8,128)S(1)} fusion(bf16[2048,1920]{1,0:T(8,128)(2,1)S(1)} %get-tuple-element.309, bf16[1920,768]{1,0:T(8,128)(2,1)S(1)} %copy-done.30), kind=kOutput, calls=%fused_computation.391 | convolution fusion | flops 6039797760 | bytes 17104896 | tf_op jit(solution)/shard_map/dot_general | solution.py:164
  257.9 6.3 %subtract_convert_fusion = bf16[2048,1920]{1,0:T(8,128)(2,1)S(1)} fusion(bf16[2048,1920]{1,0:T(8,128)(2,1)} %copy-done.5, f32[2048]{0:T(1024)S(1)} %get-tuple-element.455, s32[2048]{0:T(1024)S(1)} %bitcast.195), kind=kLoop, calls=%fused_computation.30 | loop fusion | flops 23592960 | bytes 15745024 | tf_op jit(solution)/shard_map/convert_element_type | solution.py:889
  266.7 6.6 %convolution_convert_fusion = bf16[1920,768]{1,0:T(8,128)(2,1)S(1)} fusion(bf16[2048,1920]{1,0:T(8,128)(2,1)S(1)} %subtract_convert_fusion, bf16[2048,768]{1,0:T(8,128)(2,1)S(1)} %copy-done.44), kind=kOutput, calls=%fused_computation.52 | convolution fusion | flops 6041272320 | bytes 13959168 | tf_op jit(solution)/shard_map/dot_general | solution.py:168
  276.3 10.0 %collective-permute-done.20 = bf16[4,1,1,128,768]{4,3,2,1,0:T(8,128)(2,1)S(1)} collective-permute-done((bf16[4,1,1,128,768]{4,3,2,1,0:T(8,128)(2,1)S(1)}, bf16[4,1,1,128,768]{4,3,2,1,0:T(8,128)(2,1)S(1)}, u32[]{:S(2)}, u32[]{:S(2)}) %collective-permute-start.20) | collective-permute-done | bytes 786464 | tf_op jit(solution)/shard_map/ppermute | solution.py:59
  295.8 13.7 %collective-permute-done.22 = bf16[1,1,1,128,768]{4,3,2,1,0:T(8,128)(2,1)} collective-permute-done((bf16[1,1,1,128,768]{4,3,2,1,0:T(8,128)(2,1)}, bf16[1,1,1,128,768]{4,3,2,1,0:T(8,128)(2,1)}, u32[]{:S(2)}, u32[]{:S(2)}) %collective-permute-start.22) | collective-permute-done | bytes 196640 | tf_op jit(solution)/shard_map/ppermute | solution.py:59
  317.4 15.4 %shard_map.410 = (bf16[2,4,768,768]{3,2,1,0:T(8,128)(2,1)}, f32[1,3072]{1,0:T(1,128)S(1)}, f32[512,768]{1,0:T(8,128)S(1)}) custom-call(bf16[512,768]{1,0:T(8,128)(2,1)S(1)} %get-tuple-element.446.grad_ref, bf16[512,768]{1,0:T(8,128)(2,1)S(1)} %fusion.33.middle_ref, bf16[512,3072]{1,0:T(8,128)(2,1)S(1)} %copy-done.11, f32[512,3072]{1,0:T(8,128)S(1)} %copy-done.9, ...), custom_call_target="tpu_custom_call" | custom-call | tf_op jit(solution)/shard_map/pallas_call | solution.py:541
  349.1 17.6 %shard_map.411.grad_ref = bf16[5,512,768]{2,1,0:T(8,128)(2,1)S(1)} custom-call(s32[1]{0:T(128)} %copy.166.length_ref, bf16[6,512,768]{2,1,0:T(8,128)(2,1)S(1)} %bitcast.161, bf16[512,768]{1,0:T(8,128)(2,1)S(1)} %convolution_convert_fusion.1.grad_ref), custom_call_target="tpu_custom_call" | custom-call | tf_op jit(solution)/shard_map/pallas_call | solution.py:260
  366.7 8.0 %shard_map.412 = (f32[512,768]{1,0:T(8,128)S(1)}, bf16[512,768]{1,0:T(8,128)(2,1)S(1)}, f32[5,1,768]{2,1,0:T(1,128)S(1)}) custom-call(f32[512,768]{1,0:T(8,128)S(1)} %get-tuple-element.449.first_ref, bf16[5,512,768]{2,1,0:T(8,128)(2,1)S(1)} %shard_map.411.grad_ref, bf16[15,768,768]{2,1,0:T(8,128)(2,1)} %all-gather.2.cloned.1.call-done.mat_ref.up_ref.down_ref), custom_call_target="tpu_custom_call" | custom-call | tf_op jit(solution)/shard_map/pallas_call | solution.py:306
  399.0 4.9 all-to-all-start.6
  416.6 12.5 %all-to-all-done.6 = bf16[16,48,768]{2,1,0:T(8,128)(2,1)} async-done(((bf16[16,48,768]{2,1,0:T(8,128)(2,1)}), bf16[16,48,768]{2,1,0:T(8,128)(2,1)}, u32[]{:S(2)}, u32[]{:S(2)}) %all-to-all-start.6) | async-done | bytes 1179680 | tf_op jit(solution)/shard_map/all_to_all | solution.py:923
  432.3 28.9 %reduce-scatter.2.cloned.1.call-done = bf16[2,4,48,768]{3,2,1,0:T(8,128)(2,1)} async-done(((bf16[2,4,768,768]{3,2,1,0:T(8,128)(2,1)}), bf16[2,4,48,768]{3,2,1,0:T(8,128)(2,1)}) %reduce-scatter.2.cloned.1.call-update) | async-done | bytes 589840 | tf_op jit(solution)/shard_map/reduce_scatter | solution.py:664
  470.4 4.4 fusion.20
  478.2 8.5 %add_add_fusion.1 = f32[1920,768]{1,0:T(8,128)} fusion(f32[1920,768]{1,0:T(8,128)S(1)} %fusion.20, bf16[1920,768]{1,0:T(8,128)(2,1)S(1)} %copy-done.46, bf16[576,768]{1,0:T(8,128)(2,1)} %collective-permute-done.19, bf16[576,768]{1,0:T(8,128)(2,1)} %collective-permute-done.18, bf16[384,768]{1,0:T(8,128)(2,1)} %collective-permute-done.17, ...), kind=kOutput, calls=%fused_computation.41 | convolution fusion | flops 2284093440 | bytes 18877440 | tf_op jit(solution)/shard_map/dot_general | solution.py:168
  489.6 4.0 multiply_reduce_fusion
  503.1 4.0 fusion.85
  521.2 3.9 collective-permute-start.41
  542.3 8.0 %multiply_subtract_fusion = (f32[1920,768]{1,0:T(8,128)}, f32[1920,768]{1,0:T(8,128)}) fusion(f32[1920,768]{1,0:T(8,128)} %param.32, f32[1920,768]{1,0:T(8,128)} %get-tuple-element.750, f32[768]{0:T(1024)S(1)} %get-tuple-element.366, f32[1920]{0:T(1024)S(1)} %get-tuple-element.435, f32[]{:T(128)S(6)} %min.13), kind=kLoop, calls=%fused_computation.40 | loop fusion | flops 5898240 | bytes 23603716 | tf_op jit(solution)/shard_map/sub | solution.py:1016
  (554 shorter events, 219.0 us)
Async XLA Ops:
  7.2 120.9 %all-gather.2.cloned.1.call-start = ((), (), s32[]{:S(2)}) async-start(), calls=%async_computation.8 | async-start | bytes 18800640 | tf_op jit(solution)/shard_map/all_gather | solution.py:845
  27.2 8.7 %collective-permute-start.5 = (bf16[8,720]{1,0:T(8,128)(2,1)S(1)}, bf16[8,720]{1,0:T(8,128)(2,1)S(1)}, u32[]{:S(2)}, u32[]{:S(2)}) collective-permute-start(bf16[8,720]{1,0:T(8,128)(2,1)S(1)} %pad_maximum_fusion.10), channel_id=1, source_target_pairs={{0,16},{2,18},{4,20},{6,22},{8,24},{10,26},{12,28},{14,30},{16,0},... | collective-permute-start | bytes 34568 | tf_op jit(solution)/shard_map/ppermute | solution.py:831
  36.4 11.8 %all-to-all-start.4 = ((s32[32,1,178]{2,1,0:T(1,128)}), s32[32,1,178]{2,1,0:T(1,128)S(1)}, u32[]{:S(2)}, u32[]{:S(2)}) async-start(s32[32,1,178]{2,1,0:T(1,128)} %all_to_all.40), calls=%async_computation.4 | async-start | bytes 65536 | tf_op jit(solution)/shard_map/all_to_all | solution.py:782
  54.5 47.8 %all-to-all-start.5 = ((bf16[16,48,768]{2,1,0:T(8,128)(2,1)}), bf16[16,48,768]{2,1,0:T(8,128)(2,1)S(1)}, u32[]{:S(2)}, u32[]{:S(2)}) async-start(bf16[16,48,768]{2,1,0:T(8,128)(2,1)} %bitcast.181), calls=%async_computation.5 | async-start | bytes 2359296 | tf_op jit(solution)/shard_map/all_to_all | solution.py:793
  58.3 402.9 %reduce-scatter.2.cloned.1.call-start = ((), (), s32[]{:S(2)}) async-start(), calls=%async_computation.9 | async-start | bytes 10027008 | tf_op jit(solution)/shard_map/reduce_scatter | solution.py:664
  165.6 17.5 %collective-permute-start.7 = (bf16[1,1,1,128,768]{4,3,2,1,0:T(8,128)(2,1)S(1)}, bf16[1,1,1,128,768]{4,3,2,1,0:T(8,128)(2,1)S(1)}, u32[]{:S(2)}, u32[]{:S(2)}) collective-permute-start(bf16[1,1,1,128,768]{4,3,2,1,0:T(8,128)(2,1)S(1)} %fusion.34), channel_id=1, source_target_pairs={{0,16},{2,18},{4,20},{6,22},{8,24},{10,26},{12,28},{14,30},{16,0},... | collective-permute-start | bytes 589832 | tf_op jit(solution)/shard_map/ppermute | solution.py:59
  173.2 9.9 %collective-permute-start.8 = (bf16[1,1,1,128,768]{4,3,2,1,0:T(8,128)(2,1)S(1)}, bf16[1,1,1,128,768]{4,3,2,1,0:T(8,128)(2,1)S(1)}, u32[]{:S(2)}, u32[]{:S(2)}) collective-permute-start(bf16[1,1,1,128,768]{4,3,2,1,0:T(8,128)(2,1)S(1)} %fusion.34), channel_id=1, source_target_pairs={{0,24},{2,26},{4,28},{6,30},{8,0},{10,2},{12,4},{14,6},{16,8},{18,... | collective-permute-start | bytes 589832 | tf_op jit(solution)/shard_map/ppermute | solution.py:59
  175.7 13.7 %collective-permute-start.6 = (bf16[1,1,1,128,768]{4,3,2,1,0:T(8,128)(2,1)S(1)}, bf16[1,1,1,128,768]{4,3,2,1,0:T(8,128)(2,1)}, u32[]{:S(2)}, u32[]{:S(2)}) collective-permute-start(bf16[1,1,1,128,768]{4,3,2,1,0:T(8,128)(2,1)S(1)} %fusion.34), channel_id=1, source_target_pairs={{0,8},{2,10},{4,12},{6,14},{8,16},{10,18},{12,20},{14,22},{16,24},... | collective-permute-start | bytes 589832 | tf_op jit(solution)/shard_map/ppermute | solution.py:59
  191.6 19.1 %collective-permute-start.9 = (bf16[4,1,1,128,768]{4,3,2,1,0:T(8,128)(2,1)}, bf16[4,1,1,128,768]{4,3,2,1,0:T(8,128)(2,1)}, u32[]{:S(2)}, u32[]{:S(2)}) collective-permute-start(bf16[4,1,1,128,768]{4,3,2,1,0:T(8,128)(2,1)} %pad_maximum_fusion.5), channel_id=1, source_target_pairs={{0,4},{2,6},{4,0},{6,2},{8,12},{10,14},{12,8},{14,10},{16,20},{18,... | collective-permute-start | bytes 2359304 | tf_op jit(solution)/shard_map/ppermute | solution.py:59
  234.4 8.1 %collective-permute-start.12 = (f32[2,16,128]{2,1,0:T(8,128)S(1)}, f32[2,16,128]{2,1,0:T(8,128)S(1)}, u32[]{:S(2)}, u32[]{:S(2)}) collective-permute-start(f32[2,16,128]{2,1,0:T(8,128)S(1)} %pad_maximum_fusion.7), channel_id=1, source_target_pairs={{0,4},{2,6},{4,0},{6,2},{8,12},{10,14},{12,8},{14,10},{16,20},{18,... | collective-permute-start | bytes 49160 | tf_op jit(solution)/shard_map/ppermute | solution.py:106
  266.3 20.0 %collective-permute-start.20 = (bf16[4,1,1,128,768]{4,3,2,1,0:T(8,128)(2,1)S(1)}, bf16[4,1,1,128,768]{4,3,2,1,0:T(8,128)(2,1)S(1)}, u32[]{:S(2)}, u32[]{:S(2)}) collective-permute-start(bf16[4,1,1,128,768]{4,3,2,1,0:T(8,128)(2,1)S(1)} %dynamic-slice_convert_fusion), channel_id=1, source_target_pairs={{0,4},{2,6},{4,0},{6,2},{8,12},{10,14},{12,8},{14,10},{16,20},{18,... | collective-permute-start | bytes 2359304 | tf_op jit(solution)/shard_map/ppermute | solution.py:59
  274.3 36.5 %collective-permute-start.16 = (bf16[384,768]{1,0:T(8,128)(2,1)}, bf16[384,768]{1,0:T(8,128)(2,1)}, u32[]{:S(2)}, u32[]{:S(2)}) collective-permute-start(bf16[384,768]{1,0:T(8,128)(2,1)} %get-tuple-element.478), channel_id=1, source_target_pairs={{0,1},{1,0},{2,3},{3,2},{4,5},{5,4},{6,7},{7,6},{8,9},{9,8},{10,11... | collective-permute-start | bytes 1769480 | tf_op jit(solution)/shard_map/ppermute | solution.py:59
  275.7 35.1 %collective-permute-start.17 = (bf16[384,768]{1,0:T(8,128)(2,1)S(1)}, bf16[384,768]{1,0:T(8,128)(2,1)}, u32[]{:S(2)}, u32[]{:S(2)}) collective-permute-start(bf16[384,768]{1,0:T(8,128)(2,1)S(1)} %get-tuple-element.477), channel_id=1, source_target_pairs={{0,1},{1,0},{2,3},{3,2},{4,5},{5,4},{6,7},{7,6},{8,9},{9,8},{10,11... | collective-permute-start | bytes 1769480 | tf_op jit(solution)/shard_map/ppermute | solution.py:59
  290.1 19.4 %collective-permute-start.22 = (bf16[1,1,1,128,768]{4,3,2,1,0:T(8,128)(2,1)}, bf16[1,1,1,128,768]{4,3,2,1,0:T(8,128)(2,1)}, u32[]{:S(2)}, u32[]{:S(2)}) collective-permute-start(bf16[1,1,1,128,768]{4,3,2,1,0:T(8,128)(2,1)} %get-tuple-element.314), channel_id=1, source_target_pairs={{0,16},{2,18},{4,20},{6,22},{8,24},{10,26},{12,28},{14,30},{16,0},... | collective-permute-start | bytes 589832 | tf_op jit(solution)/shard_map/ppermute | solution.py:59
  291.9 17.6 %collective-permute-start.21 = (bf16[1,1,1,128,768]{4,3,2,1,0:T(8,128)(2,1)S(1)}, bf16[1,1,1,128,768]{4,3,2,1,0:T(8,128)(2,1)}, u32[]{:S(2)}, u32[]{:S(2)}) collective-permute-start(bf16[1,1,1,128,768]{4,3,2,1,0:T(8,128)(2,1)S(1)} %get-tuple-element.313), channel_id=1, source_target_pairs={{0,8},{2,10},{4,12},{6,14},{8,16},{10,18},{12,20},{14,22},{16,24},... | collective-permute-start | bytes 589832 | tf_op jit(solution)/shard_map/ppermute | solution.py:59
  336.9 29.8 %collective-permute-start.18 = (bf16[576,768]{1,0:T(8,128)(2,1)}, bf16[576,768]{1,0:T(8,128)(2,1)}, u32[]{:S(2)}, u32[]{:S(2)}) collective-permute-start(bf16[576,768]{1,0:T(8,128)(2,1)} %get-tuple-element.476), channel_id=1, source_target_pairs={{0,1},{1,0},{2,3},{3,2},{4,5},{5,4},{6,7},{7,6},{8,9},{9,8},{10,11... | collective-permute-start | bytes 2654216 | tf_op jit(solution)/shard_map/ppermute | solution.py:59
  338.3 38.3 %collective-permute-start.19 = (bf16[576,768]{1,0:T(8,128)(2,1)}, bf16[576,768]{1,0:T(8,128)(2,1)}, u32[]{:S(2)}, u32[]{:S(2)}) collective-permute-start(bf16[576,768]{1,0:T(8,128)(2,1)} %get-tuple-element.475), channel_id=1, source_target_pairs={{0,1},{1,0},{2,3},{3,2},{4,5},{5,4},{6,7},{7,6},{8,9},{9,8},{10,11... | collective-permute-start | bytes 2654216 | tf_op jit(solution)/shard_map/ppermute | solution.py:59
  398.9 11.9 %collective-permute-start.25 = (bf16[3,4,2,1,48,768]{5,4,0,3,2,1:T(8,128)(2,1)}, bf16[3,4,2,1,48,768]{5,4,0,3,2,1:T(8,128)(2,1)}, u32[]{:S(2)}, u32[]{:S(2)}) collective-permute-start(bf16[3,4,2,1,48,768]{5,4,0,3,2,1:T(8,128)(2,1)} %copy.142), channel_id=1, source_target_pairs={{0,2},{2,0},{4,6},{6,4},{8,10},{10,8},{12,14},{14,12},{16,18},{18,... | collective-permute-start | bytes 5308424 | tf_op jit(solution)/shard_map/ppermute | solution.py:59
  399.0 30.1 %all-to-all-start.6 = ((bf16[16,48,768]{2,1,0:T(8,128)(2,1)}), bf16[16,48,768]{2,1,0:T(8,128)(2,1)}, u32[]{:S(2)}, u32[]{:S(2)}) async-start(bf16[16,48,768]{2,1,0:T(8,128)(2,1)} %bitcast.176), calls=%async_computation.6 | async-start | bytes 2359296 | tf_op jit(solution)/shard_map/all_to_all | solution.py:923
  406.0 55.2 %collective-permute-start.27 = (bf16[4,4,1,1,48,768]{5,4,0,3,2,1:T(8,128)(2,1)}, bf16[4,4,1,1,48,768]{5,4,0,3,2,1:T(8,128)(2,1)}, u32[]{:S(2)}, u32[]{:S(2)}) collective-permute-start(bf16[4,4,1,1,48,768]{5,4,0,3,2,1:T(8,128)(2,1)} %constant_dynamic-slice_fusion.11), channel_id=1, source_target_pairs={{0,4},{2,6},{4,0},{6,2},{8,12},{10,14},{12,8},{14,10},{16,20},{18,... | collective-permute-start | bytes 3538952 | tf_op jit(solution)/shard_map/ppermute | solution.py:59
  415.1 48.5 %collective-permute-start.26 = (bf16[3,4,2,1,48,384]{5,4,0,3,2,1:T(8,128)(2,1)}, bf16[3,4,2,1,48,384]{5,4,0,3,2,1:T(8,128)(2,1)}, u32[]{:S(2)}, u32[]{:S(2)}) collective-permute-start(bf16[3,4,2,1,48,384]{5,4,0,3,2,1:T(8,128)(2,1)} %constant_dynamic-slice_fusion.8), channel_id=1, source_target_pairs={{0,1},{1,0},{2,3},{3,2},{4,5},{5,4},{6,7},{7,6},{8,9},{9,8},{10,11... | collective-permute-start | bytes 2654216 | tf_op jit(solution)/shard_map/ppermute | solution.py:59
  429.2 40.2 %collective-permute-start.28 = (bf16[768,768]{1,0:T(8,128)(2,1)}, bf16[768,768]{1,0:T(8,128)(2,1)}, u32[]{:S(2)}, u32[]{:S(2)}) collective-permute-start(bf16[768,768]{1,0:T(8,128)(2,1)} %bitcast.46), channel_id=1, source_target_pairs={{0,1},{1,0},{2,3},{3,2},{4,5},{5,4},{6,7},{7,6},{8,9},{9,8},{10,11... | collective-permute-start | bytes 3538952 | tf_op jit(solution)/shard_map/ppermute | solution.py:59
  466.0 11.2 %collective-permute-start.29 = (bf16[3,4,1,1,48,384]{5,4,0,3,2,1:T(8,128)(2,1)S(1)}, bf16[3,4,1,1,48,384]{5,4,0,3,2,1:T(8,128)(2,1)S(1)}, u32[]{:S(2)}, u32[]{:S(2)}) collective-permute-start(bf16[3,4,1,1,48,384]{5,4,0,3,2,1:T(8,128)(2,1)S(1)} %constant_dynamic-slice_fusion.6), channel_id=1, source_target_pairs={{0,4},{2,6},{4,0},{6,2},{8,12},{10,14},{12,8},{14,10},{16,20},{18,... | collective-permute-start | bytes 1327112 | tf_op jit(solution)/shard_map/ppermute | solution.py:59
  466.5 27.0 %collective-permute-start.33 = (bf16[4,1,1,1,48,768]{5,4,0,3,2,1:T(8,128)(2,1)}, bf16[4,1,1,1,48,768]{5,4,0,3,2,1:T(8,128)(2,1)}, u32[]{:S(2)}, u32[]{:S(2)}) collective-permute-start(bf16[4,1,1,1,48,768]{5,4,0,3,2,1:T(8,128)(2,1)} %get-tuple-element.488), channel_id=1, source_target_pairs={{0,8},{2,10},{4,12},{6,14},{8,16},{10,18},{12,20},{14,22},{16,24},... | collective-permute-start | bytes 884744 | tf_op jit(solution)/shard_map/ppermute | solution.py:59
  467.9 40.7 %collective-permute-start.38 = (bf16[2,4,48,768]{3,2,1,0:T(8,128)(2,1)}, bf16[2,4,48,768]{3,2,1,0:T(8,128)(2,1)}, u32[]{:S(2)}, u32[]{:S(2)}) collective-permute-start(bf16[2,4,48,768]{3,2,1,0:T(8,128)(2,1)} %reduce-scatter.2.cloned.1.call-done), channel_id=1, source_target_pairs={{0,1},{1,0},{2,3},{3,2},{4,5},{5,4},{6,7},{7,6},{8,9},{9,8},{10,11... | collective-permute-start | bytes 1769480 | tf_op jit(solution)/shard_map/ppermute | solution.py:59
  469.4 25.9 %collective-permute-start.34 = (bf16[4,1,1,1,48,768]{5,4,0,3,2,1:T(8,128)(2,1)}, bf16[4,1,1,1,48,768]{5,4,0,3,2,1:T(8,128)(2,1)}, u32[]{:S(2)}, u32[]{:S(2)}) collective-permute-start(bf16[4,1,1,1,48,768]{5,4,0,3,2,1:T(8,128)(2,1)} %get-tuple-element.487), channel_id=1, source_target_pairs={{0,16},{2,18},{4,20},{6,22},{8,24},{10,26},{12,28},{14,30},{16,0},... | collective-permute-start | bytes 884744 | tf_op jit(solution)/shard_map/ppermute | solution.py:59
  487.0 10.6 %collective-permute-start.35 = (bf16[4,1,1,1,48,768]{5,4,0,3,2,1:T(8,128)(2,1)S(1)}, bf16[4,1,1,1,48,768]{5,4,0,3,2,1:T(8,128)(2,1)S(1)}, u32[]{:S(2)}, u32[]{:S(2)}) collective-permute-start(bf16[4,1,1,1,48,768]{5,4,0,3,2,1:T(8,128)(2,1)S(1)} %get-tuple-element.486), channel_id=1, source_target_pairs={{0,24},{2,26},{4,28},{6,30},{8,0},{10,2},{12,4},{14,6},{16,8},{18,... | collective-permute-start | bytes 884744 | tf_op jit(solution)/shard_map/ppermute | solution.py:59
  489.6 17.5 %collective-permute-start.30 = (bf16[3,1,1,1,48,384]{5,4,0,3,2,1:T(8,128)(2,1)}, bf16[3,1,1,1,48,384]{5,4,0,3,2,1:T(8,128)(2,1)S(1)}, u32[]{:S(2)}, u32[]{:S(2)}) collective-permute-start(bf16[3,1,1,1,48,384]{5,4,0,3,2,1:T(8,128)(2,1)} %get-tuple-element.501), channel_id=1, source_target_pairs={{0,8},{2,10},{4,12},{6,14},{8,16},{10,18},{12,20},{14,22},{16,24},... | collective-permute-start | bytes 331784 | tf_op jit(solution)/shard_map/ppermute | solution.py:59
  493.6 13.5 %collective-permute-start.31 = (bf16[3,1,1,1,48,384]{5,4,0,3,2,1:T(8,128)(2,1)S(1)}, bf16[3,1,1,1,48,384]{5,4,0,3,2,1:T(8,128)(2,1)S(1)}, u32[]{:S(2)}, u32[]{:S(2)}) collective-permute-start(bf16[3,1,1,1,48,384]{5,4,0,3,2,1:T(8,128)(2,1)S(1)} %copy-done.70), channel_id=1, source_target_pairs={{0,16},{2,18},{4,20},{6,22},{8,24},{10,26},{12,28},{14,30},{16,0},... | collective-permute-start | bytes 331784 | tf_op jit(solution)/shard_map/ppermute | solution.py:59
  495.3 11.8 %collective-permute-start.32 = (bf16[3,1,1,1,48,384]{5,4,0,3,2,1:T(8,128)(2,1)S(1)}, bf16[3,1,1,1,48,384]{5,4,0,3,2,1:T(8,128)(2,1)S(1)}, u32[]{:S(2)}, u32[]{:S(2)}) collective-permute-start(bf16[3,1,1,1,48,384]{5,4,0,3,2,1:T(8,128)(2,1)S(1)} %copy-done.69), channel_id=1, source_target_pairs={{0,24},{2,26},{4,28},{6,30},{8,0},{10,2},{12,4},{14,6},{16,8},{18,... | collective-permute-start | bytes 331784 | tf_op jit(solution)/shard_map/ppermute | solution.py:59
  499.4 14.1 %collective-permute-start.37 = (bf16[4,48,768]{2,1,0:T(8,128)(2,1)}, bf16[4,48,768]{2,1,0:T(8,128)(2,1)S(1)}, u32[]{:S(2)}, u32[]{:S(2)}) collective-permute-start(bf16[4,48,768]{2,1,0:T(8,128)(2,1)} %fusion.48), channel_id=1, source_target_pairs={{0,1},{1,0},{2,3},{3,2},{4,5},{5,4},{6,7},{7,6},{8,9},{9,8},{10,11... | collective-permute-start | bytes 884744 | tf_op jit(solution)/shard_map/ppermute | solution.py:59
  540.8 14.5 %collective-permute-start.43 = (f32[4]{0:T(128)S(1)}, f32[4]{0:T(128)S(1)}, u32[]{:S(2)}, u32[]{:S(2)}) collective-permute-start(f32[4]{0:T(128)S(1)} %slice_bitcast_fusion.4), channel_id=1, source_target_pairs={{0,1},{1,0},{2,3},{3,2},{4,5},{5,4},{6,7},{7,6},{8,9},{9,8},{10,11... | collective-permute-start | bytes 56 | tf_op jit(solution)/shard_map/ppermute | solution.py:106
  (128 other events, 765.7 us)
Sparse Core Ops, SparseCore 0:
  11.8 116.2 all-gather.1
  334.1 127.0 reduce-scatter.1

commit v6 on v5

--- a/solution.py
+++ b/solution.py
@@ -245,7 +245,7 @@
 FREE = pl.CostEstimate(flops=0, transcendentals=0, bytes_accessed=0)
 
 
-ROOMY = pltpu.CompilerParams(vmem_limit_bytes=36 * 1024 * 1024)
+ROOMY = pltpu.CompilerParams(vmem_limit_bytes=30 * 1024 * 1024)
 
 
 def attention_call(kernel, lengths, stack, arrays, stacked):

time: 572 us -> 579 us (1.012)
  local copies, waits for them, and re-layouts: 53 us -> 62.7 us
    unnamed x231 -> x235, local copies, waits for them, and re-layouts: 25.8 us -> 35.4 us
where the time goes in v6:
time: 579 us; the launch traced here: 571 us
  waiting for transfers between devices  175 us (30%)
  other arithmetic  97.6 us (17%)
  Pallas kernels  82.3 us (14%)
  starting transfers between devices  75.8 us (13%)
  local copies, waits for them, and re-layouts  62.7 us (11%)
  matrix products  54.5 us (9%)
  between operations  22.2 us (4%)
    ppermute x29, waiting for transfers between devices, shifted(): return lax.ppermute(value, line.axis, pairs)  61 us
    ppermute x29, starting transfers between devices, shifted(): return lax.ppermute(value, line.axis, pairs)  38.7 us
    unnamed x235, local copies, waits for them, and re-layouts  35.4 us
    all_to_all x1, waiting for transfers between devices, fetch(): lax.all_to_all(rows.reshape(groups, stride, width), 'fsdp', 0, 0, tiled=T...  31.8 us
    pallas_call x2, Pallas kernels, attention_call(): pl.pallas_call(kernel, grid=(pages, width // LANES), in_specs=[pl.BlockSp...  29.2 us
    reduce_scatter x1, waiting for transfers between devices, layer_backward(): lax.psum_scatter(grad_feeds, 'fsdp', scatter_dimension=2, tiled=True)  28.8 us
    dot_general x6, matrix products, product(): return jnp.dot(left, right, preferred_element_type=FLOAT)  28.2 us
    dot_general x7, matrix products, contract_rows(): lax.dot_general(left, right, (((0,), (0,)), ((), ())), preferred_element_...  23.8 us
  transfers between devices with their start and end apart: 47, of which 22 were waited for; matrix products, arithmetic and copies ran while one was open for 26% of the time, Pallas kernels for 6%

profile of v6, /device:TPU:0, one launch (start us, length us, event | category | flops | bytes accessed | tf_op | source)
XLA Modules:
  0.0 570.6 jit_solution(9999482556723465381)
XLA Ops:
  30.6 4.6 convert_element_type.326.table_ref
  36.4 3.9 all-to-all-start.4
  40.4 7.7 %all-to-all-done.4 = s32[32,1,178]{2,1,0:T(1,128)S(1)} async-done(((s32[32,1,178]{2,1,0:T(1,128)}), s32[32,1,178]{2,1,0:T(1,128)S(1)}, u32[]{:S(2)}, u32[]{:S(2)}) %all-to-all-start.4) | async-done | bytes 22816 | tf_op jit(solution)/shard_map/all_to_all | solution.py:782
  48.9 5.7 fusion.31
  60.0 10.4 %fusion.23 = bf16[2048,768]{1,0:T(8,128)(2,1)} fusion(bf16[1920,768]{1,0:T(8,128)(2,1)} %convert_element_type.326.table_ref, s32[2048]{0:T(1024)S(1)} %bitcast.194), kind=kOutput, calls=%fused_computation.51 | convolution fusion | flops 6045302784 | bytes 6103040 | tf_op jit(solution)/shard_map/dot_general | solution.py:164
  70.5 31.8 %all-to-all-done.5 = bf16[16,48,768]{2,1,0:T(8,128)(2,1)S(1)} async-done(((bf16[16,48,768]{2,1,0:T(8,128)(2,1)}), bf16[16,48,768]{2,1,0:T(8,128)(2,1)S(1)}, u32[]{:S(2)}, u32[]{:S(2)}) %all-to-all-start.5) | async-done | bytes 1179680 | tf_op jit(solution)/shard_map/all_to_all | solution.py:793
  108.8 19.3 %all-gather.2.cloned.1.call-done.mat_ref.up_ref.down_ref = bf16[15,768,768]{2,1,0:T(8,128)(2,1)} async-done(((bf16[15,48,768]{2,1,0:T(8,128)(2,1)}), bf16[15,768,768]{2,1,0:T(8,128)(2,1)}) %all-gather.2.cloned.1.call-update) | async-done | bytes 17694736 | tf_op jit(solution)/shard_map/all_gather | solution.py:845
  128.1 6.0 %copy-done = bf16[15,768,768]{2,1,0:T(8,128)(2,1)S(1)} copy-done((bf16[15,768,768]{2,1,0:T(8,128)(2,1)S(1)}, bf16[15,768,768]{2,1,0:T(8,128)(2,1)}, u32[]{:S(2)}) %copy-start) | copy-done | bytes 17694744
  134.1 4.8 shard_map.406.stack_ref.place_ref
  139.0 11.7 %shard_map.407.mixed_ref = bf16[512,768]{1,0:T(8,128)(2,1)S(1)} custom-call(s32[1]{0:T(128)} %copy.166.length_ref, bf16[6,512,768]{2,1,0:T(8,128)(2,1)S(1)} %shard_map.406.stack_ref.place_ref), custom_call_target="tpu_custom_call" | custom-call | tf_op jit(solution)/shard_map/pallas_call | solution.py:260
  153.8 9.9 %shard_map.408 = (bf16[512,3072]{1,0:T(8,128)(2,1)S(1)}, f32[512,3072]{1,0:T(8,128)S(1)}, f32[512,768]{1,0:T(8,128)S(1)}) custom-call(bf16[512,768]{1,0:T(8,128)(2,1)S(1)} %fusion.33.middle_ref, bf16[15,768,768]{2,1,0:T(8,128)(2,1)} %all-gather.2.cloned.1.call-done.mat_ref.up_ref.down_ref, f32[1,3072]{1,0:T(1,128)S(1)} %bitcast.168, ...), custom_call_target="tpu_custom_call" | custom-call | tf_op jit(solution)/shard_map/pallas_call | solution.py:488
  169.2 7.7 %collective-permute-start.7 = (bf16[1,1,1,128,768]{4,3,2,1,0:T(8,128)(2,1)S(1)}, bf16[1,1,1,128,768]{4,3,2,1,0:T(8,128)(2,1)S(1)}, u32[]{:S(2)}, u32[]{:S(2)}) collective-permute-start(bf16[1,1,1,128,768]{4,3,2,1,0:T(8,128)(2,1)S(1)} %fusion.34), channel_id=1, source_target_pairs={{0,16},{2,18},{4,20},{6,22},{8,24},{10,26},{12,28},{14,30},{16,0},... | collective-permute-start | bytes 589832 | tf_op jit(solution)/shard_map/ppermute | solution.py:59
  179.6 7.2 %collective-permute-done.7 = bf16[1,1,1,128,768]{4,3,2,1,0:T(8,128)(2,1)S(1)} collective-permute-done((bf16[1,1,1,128,768]{4,3,2,1,0:T(8,128)(2,1)S(1)}, bf16[1,1,1,128,768]{4,3,2,1,0:T(8,128)(2,1)S(1)}, u32[]{:S(2)}, u32[]{:S(2)}) %collective-permute-start.7) | collective-permute-done | bytes 196640 | tf_op jit(solution)/shard_map/ppermute | solution.py:59
  188.1 5.0 collective-permute-done.6
  196.6 17.8 %collective-permute-done.9 = bf16[4,1,1,128,768]{4,3,2,1,0:T(8,128)(2,1)} collective-permute-done((bf16[4,1,1,128,768]{4,3,2,1,0:T(8,128)(2,1)}, bf16[4,1,1,128,768]{4,3,2,1,0:T(8,128)(2,1)}, u32[]{:S(2)}, u32[]{:S(2)}) %collective-permute-start.9) | collective-permute-done | bytes 786464 | tf_op jit(solution)/shard_map/ppermute | solution.py:59
  226.7 9.9 %shard_map.409 = (bf16[2048,1920]{1,0:T(8,128)(2,1)S(1)}, f32[8,2048]{1,0:T(8,128)S(1)}) custom-call(bf16[2048,768]{1,0:T(8,128)(2,1)S(1)} %bitcast.164, bf16[1920,768]{1,0:T(8,128)(2,1)S(1)} %copy-done.32), custom_call_target="tpu_custom_call" | custom-call | tf_op jit(solution)/shard_map/pallas_call | solution.py:581
  239.5 6.9 %fusion.115 = f32[2048,768]{1,0:T(8,128)S(1)} fusion(bf16[2048,1920]{1,0:T(8,128)(2,1)S(1)} %get-tuple-element.309, bf16[1920,768]{1,0:T(8,128)(2,1)S(1)} %copy-done.32), kind=kOutput, calls=%fused_computation.391 | convolution fusion | flops 6039797760 | bytes 17104896 | tf_op jit(solution)/shard_map/dot_general | solution.py:164
  261.8 6.3 %subtract_convert_fusion = bf16[2048,1920]{1,0:T(8,128)(2,1)S(1)} fusion(bf16[2048,1920]{1,0:T(8,128)(2,1)} %copy-done.7, f32[2048]{0:T(1024)S(1)} %get-tuple-element.455, s32[2048]{0:T(1024)S(1)} %bitcast.195), kind=kLoop, calls=%fused_computation.30 | loop fusion | flops 23592960 | bytes 15745024 | tf_op jit(solution)/shard_map/convert_element_type | solution.py:889
  270.6 6.6 %convolution_convert_fusion = bf16[1920,768]{1,0:T(8,128)(2,1)S(1)} fusion(bf16[2048,1920]{1,0:T(8,128)(2,1)S(1)} %subtract_convert_fusion, bf16[2048,768]{1,0:T(8,128)(2,1)S(1)} %copy-done.46), kind=kOutput, calls=%fused_computation.52 | convolution fusion | flops 6041272320 | bytes 13959168 | tf_op jit(solution)/shard_map/dot_general | solution.py:168
  280.2 10.0 %collective-permute-done.20 = bf16[4,1,1,128,768]{4,3,2,1,0:T(8,128)(2,1)S(1)} collective-permute-done((bf16[4,1,1,128,768]{4,3,2,1,0:T(8,128)(2,1)S(1)}, bf16[4,1,1,128,768]{4,3,2,1,0:T(8,128)(2,1)S(1)}, u32[]{:S(2)}, u32[]{:S(2)}) %collective-permute-start.20) | collective-permute-done | bytes 786464 | tf_op jit(solution)/shard_map/ppermute | solution.py:59
  299.7 13.7 %collective-permute-done.22 = bf16[1,1,1,128,768]{4,3,2,1,0:T(8,128)(2,1)} collective-permute-done((bf16[1,1,1,128,768]{4,3,2,1,0:T(8,128)(2,1)}, bf16[1,1,1,128,768]{4,3,2,1,0:T(8,128)(2,1)}, u32[]{:S(2)}, u32[]{:S(2)}) %collective-permute-start.22) | collective-permute-done | bytes 196640 | tf_op jit(solution)/shard_map/ppermute | solution.py:59
  321.3 14.5 %shard_map.410 = (bf16[2,4,768,768]{3,2,1,0:T(8,128)(2,1)S(1)}, f32[1,3072]{1,0:T(1,128)S(1)}, f32[512,768]{1,0:T(8,128)S(1)}) custom-call(bf16[512,768]{1,0:T(8,128)(2,1)S(1)} %get-tuple-element.446.grad_ref, bf16[512,768]{1,0:T(8,128)(2,1)S(1)} %fusion.33.middle_ref, bf16[512,3072]{1,0:T(8,128)(2,1)S(1)} %copy-done.13, f32[512,3072]{1,0:T(8,128)S(1)} %copy-done.11, ...), custom_call_target="tpu_custom_call" | custom-call | tf_op jit(solution)/shard_map/pallas_call | solution.py:541
  355.8 17.6 %shard_map.411.grad_ref = bf16[5,512,768]{2,1,0:T(8,128)(2,1)S(1)} custom-call(s32[1]{0:T(128)} %copy.166.length_ref, bf16[6,512,768]{2,1,0:T(8,128)(2,1)S(1)} %bitcast.161, bf16[512,768]{1,0:T(8,128)(2,1)S(1)} %convolution_convert_fusion.1.grad_ref), custom_call_target="tpu_custom_call" | custom-call | tf_op jit(solution)/shard_map/pallas_call | solution.py:260
  373.5 8.0 %shard_map.412 = (f32[512,768]{1,0:T(8,128)S(1)}, bf16[512,768]{1,0:T(8,128)(2,1)S(1)}, f32[5,1,768]{2,1,0:T(1,128)S(1)}) custom-call(f32[512,768]{1,0:T(8,128)S(1)} %get-tuple-element.449.first_ref, bf16[5,512,768]{2,1,0:T(8,128)(2,1)S(1)} %shard_map.411.grad_ref, bf16[15,768,768]{2,1,0:T(8,128)(2,1)} %all-gather.2.cloned.1.call-done.mat_ref.up_ref.down_ref), custom_call_target="tpu_custom_call" | custom-call | tf_op jit(solution)/shard_map/pallas_call | solution.py:306
  405.8 4.9 all-to-all-start.6
  423.4 12.6 %all-to-all-done.6 = bf16[16,48,768]{2,1,0:T(8,128)(2,1)} async-done(((bf16[16,48,768]{2,1,0:T(8,128)(2,1)}), bf16[16,48,768]{2,1,0:T(8,128)(2,1)}, u32[]{:S(2)}, u32[]{:S(2)}) %all-to-all-start.6) | async-done | bytes 1179680 | tf_op jit(solution)/shard_map/all_to_all | solution.py:923
  439.1 28.8 %reduce-scatter.2.cloned.1.call-done = bf16[2,4,48,768]{3,2,1,0:T(8,128)(2,1)} async-done(((bf16[2,4,768,768]{3,2,1,0:T(8,128)(2,1)}), bf16[2,4,48,768]{3,2,1,0:T(8,128)(2,1)}) %reduce-scatter.2.cloned.1.call-update) | async-done | bytes 589840 | tf_op jit(solution)/shard_map/reduce_scatter | solution.py:664
  477.1 4.4 fusion.20
  484.9 8.5 %add_add_fusion.1 = f32[1920,768]{1,0:T(8,128)} fusion(f32[1920,768]{1,0:T(8,128)S(1)} %fusion.20, bf16[1920,768]{1,0:T(8,128)(2,1)S(1)} %copy-done.48, bf16[576,768]{1,0:T(8,128)(2,1)} %collective-permute-done.19, bf16[576,768]{1,0:T(8,128)(2,1)} %collective-permute-done.18, bf16[384,768]{1,0:T(8,128)(2,1)} %collective-permute-done.17, ...), kind=kOutput, calls=%fused_computation.41 | convolution fusion | flops 2284093440 | bytes 18877440 | tf_op jit(solution)/shard_map/dot_general | solution.py:168
  496.3 4.0 multiply_reduce_fusion
  509.9 4.0 fusion.85
  548.9 8.0 %multiply_subtract_fusion = (f32[1920,768]{1,0:T(8,128)}, f32[1920,768]{1,0:T(8,128)}) fusion(f32[1920,768]{1,0:T(8,128)} %param.32, f32[1920,768]{1,0:T(8,128)} %get-tuple-element.750, f32[768]{0:T(1024)S(1)} %get-tuple-element.366, f32[1920]{0:T(1024)S(1)} %get-tuple-element.435, f32[]{:T(128)S(6)} %min.13), kind=kLoop, calls=%fused_computation.40 | loop fusion | flops 5898240 | bytes 23603716 | tf_op jit(solution)/shard_map/sub | solution.py:1016
  (558 shorter events, 226.5 us)
Async XLA Ops:
  7.2 120.9 %all-gather.2.cloned.1.call-start = ((), (), s32[]{:S(2)}) async-start(), calls=%async_computation.8 | async-start | bytes 18800640 | tf_op jit(solution)/shard_map/all_gather | solution.py:845
  27.2 8.7 %collective-permute-start.5 = (bf16[8,720]{1,0:T(8,128)(2,1)S(1)}, bf16[8,720]{1,0:T(8,128)(2,1)S(1)}, u32[]{:S(2)}, u32[]{:S(2)}) collective-permute-start(bf16[8,720]{1,0:T(8,128)(2,1)S(1)} %pad_maximum_fusion.10), channel_id=1, source_target_pairs={{0,16},{2,18},{4,20},{6,22},{8,24},{10,26},{12,28},{14,30},{16,0},... | collective-permute-start | bytes 34568 | tf_op jit(solution)/shard_map/ppermute | solution.py:831
  36.4 11.8 %all-to-all-start.4 = ((s32[32,1,178]{2,1,0:T(1,128)}), s32[32,1,178]{2,1,0:T(1,128)S(1)}, u32[]{:S(2)}, u32[]{:S(2)}) async-start(s32[32,1,178]{2,1,0:T(1,128)} %all_to_all.40), calls=%async_computation.4 | async-start | bytes 65536 | tf_op jit(solution)/shard_map/all_to_all | solution.py:782
  54.6 47.8 %all-to-all-start.5 = ((bf16[16,48,768]{2,1,0:T(8,128)(2,1)}), bf16[16,48,768]{2,1,0:T(8,128)(2,1)S(1)}, u32[]{:S(2)}, u32[]{:S(2)}) async-start(bf16[16,48,768]{2,1,0:T(8,128)(2,1)} %bitcast.181), calls=%async_computation.5 | async-start | bytes 2359296 | tf_op jit(solution)/shard_map/all_to_all | solution.py:793
  58.3 409.7 %reduce-scatter.2.cloned.1.call-start = ((), (), s32[]{:S(2)}) async-start(), calls=%async_computation.9 | async-start | bytes 10027008 | tf_op jit(solution)/shard_map/reduce_scatter | solution.py:664
  169.2 17.5 %collective-permute-start.7 = (bf16[1,1,1,128,768]{4,3,2,1,0:T(8,128)(2,1)S(1)}, bf16[1,1,1,128,768]{4,3,2,1,0:T(8,128)(2,1)S(1)}, u32[]{:S(2)}, u32[]{:S(2)}) collective-permute-start(bf16[1,1,1,128,768]{4,3,2,1,0:T(8,128)(2,1)S(1)} %fusion.34), channel_id=1, source_target_pairs={{0,16},{2,18},{4,20},{6,22},{8,24},{10,26},{12,28},{14,30},{16,0},... | collective-permute-start | bytes 589832 | tf_op jit(solution)/shard_map/ppermute | solution.py:59
  176.9 9.9 %collective-permute-start.8 = (bf16[1,1,1,128,768]{4,3,2,1,0:T(8,128)(2,1)S(1)}, bf16[1,1,1,128,768]{4,3,2,1,0:T(8,128)(2,1)S(1)}, u32[]{:S(2)}, u32[]{:S(2)}) collective-permute-start(bf16[1,1,1,128,768]{4,3,2,1,0:T(8,128)(2,1)S(1)} %fusion.34), channel_id=1, source_target_pairs={{0,24},{2,26},{4,28},{6,30},{8,0},{10,2},{12,4},{14,6},{16,8},{18,... | collective-permute-start | bytes 589832 | tf_op jit(solution)/shard_map/ppermute | solution.py:59
  179.4 13.7 %collective-permute-start.6 = (bf16[1,1,1,128,768]{4,3,2,1,0:T(8,128)(2,1)S(1)}, bf16[1,1,1,128,768]{4,3,2,1,0:T(8,128)(2,1)}, u32[]{:S(2)}, u32[]{:S(2)}) collective-permute-start(bf16[1,1,1,128,768]{4,3,2,1,0:T(8,128)(2,1)S(1)} %fusion.34), channel_id=1, source_target_pairs={{0,8},{2,10},{4,12},{6,14},{8,16},{10,18},{12,20},{14,22},{16,24},... | collective-permute-start | bytes 589832 | tf_op jit(solution)/shard_map/ppermute | solution.py:59
  195.3 19.1 %collective-permute-start.9 = (bf16[4,1,1,128,768]{4,3,2,1,0:T(8,128)(2,1)}, bf16[4,1,1,128,768]{4,3,2,1,0:T(8,128)(2,1)}, u32[]{:S(2)}, u32[]{:S(2)}) collective-permute-start(bf16[4,1,1,128,768]{4,3,2,1,0:T(8,128)(2,1)} %pad_maximum_fusion.5), channel_id=1, source_target_pairs={{0,4},{2,6},{4,0},{6,2},{8,12},{10,14},{12,8},{14,10},{16,20},{18,... | collective-permute-start | bytes 2359304 | tf_op jit(solution)/shard_map/ppermute | solution.py:59
  238.1 8.3 %collective-permute-start.12 = (f32[2,16,128]{2,1,0:T(8,128)S(1)}, f32[2,16,128]{2,1,0:T(8,128)S(1)}, u32[]{:S(2)}, u32[]{:S(2)}) collective-permute-start(f32[2,16,128]{2,1,0:T(8,128)S(1)} %pad_maximum_fusion.7), channel_id=1, source_target_pairs={{0,4},{2,6},{4,0},{6,2},{8,12},{10,14},{12,8},{14,10},{16,20},{18,... | collective-permute-start | bytes 49160 | tf_op jit(solution)/shard_map/ppermute | solution.py:106
  270.1 20.0 %collective-permute-start.20 = (bf16[4,1,1,128,768]{4,3,2,1,0:T(8,128)(2,1)S(1)}, bf16[4,1,1,128,768]{4,3,2,1,0:T(8,128)(2,1)S(1)}, u32[]{:S(2)}, u32[]{:S(2)}) collective-permute-start(bf16[4,1,1,128,768]{4,3,2,1,0:T(8,128)(2,1)S(1)} %dynamic-slice_convert_fusion), channel_id=1, source_target_pairs={{0,4},{2,6},{4,0},{6,2},{8,12},{10,14},{12,8},{14,10},{16,20},{18,... | collective-permute-start | bytes 2359304 | tf_op jit(solution)/shard_map/ppermute | solution.py:59
  278.2 36.5 %collective-permute-start.16 = (bf16[384,768]{1,0:T(8,128)(2,1)}, bf16[384,768]{1,0:T(8,128)(2,1)}, u32[]{:S(2)}, u32[]{:S(2)}) collective-permute-start(bf16[384,768]{1,0:T(8,128)(2,1)} %get-tuple-element.478), channel_id=1, source_target_pairs={{0,1},{1,0},{2,3},{3,2},{4,5},{5,4},{6,7},{7,6},{8,9},{9,8},{10,11... | collective-permute-start | bytes 1769480 | tf_op jit(solution)/shard_map/ppermute | solution.py:59
  279.6 35.1 %collective-permute-start.17 = (bf16[384,768]{1,0:T(8,128)(2,1)S(1)}, bf16[384,768]{1,0:T(8,128)(2,1)}, u32[]{:S(2)}, u32[]{:S(2)}) collective-permute-start(bf16[384,768]{1,0:T(8,128)(2,1)S(1)} %get-tuple-element.477), channel_id=1, source_target_pairs={{0,1},{1,0},{2,3},{3,2},{4,5},{5,4},{6,7},{7,6},{8,9},{9,8},{10,11... | collective-permute-start | bytes 1769480 | tf_op jit(solution)/shard_map/ppermute | solution.py:59
  294.0 19.4 %collective-permute-start.22 = (bf16[1,1,1,128,768]{4,3,2,1,0:T(8,128)(2,1)}, bf16[1,1,1,128,768]{4,3,2,1,0:T(8,128)(2,1)}, u32[]{:S(2)}, u32[]{:S(2)}) collective-permute-start(bf16[1,1,1,128,768]{4,3,2,1,0:T(8,128)(2,1)} %get-tuple-element.314), channel_id=1, source_target_pairs={{0,16},{2,18},{4,20},{6,22},{8,24},{10,26},{12,28},{14,30},{16,0},... | collective-permute-start | bytes 589832 | tf_op jit(solution)/shard_map/ppermute | solution.py:59
  295.8 17.6 %collective-permute-start.21 = (bf16[1,1,1,128,768]{4,3,2,1,0:T(8,128)(2,1)S(1)}, bf16[1,1,1,128,768]{4,3,2,1,0:T(8,128)(2,1)}, u32[]{:S(2)}, u32[]{:S(2)}) collective-permute-start(bf16[1,1,1,128,768]{4,3,2,1,0:T(8,128)(2,1)S(1)} %get-tuple-element.313), channel_id=1, source_target_pairs={{0,8},{2,10},{4,12},{6,14},{8,16},{10,18},{12,20},{14,22},{16,24},... | collective-permute-start | bytes 589832 | tf_op jit(solution)/shard_map/ppermute | solution.py:59
  343.6 29.8 %collective-permute-start.18 = (bf16[576,768]{1,0:T(8,128)(2,1)}, bf16[576,768]{1,0:T(8,128)(2,1)}, u32[]{:S(2)}, u32[]{:S(2)}) collective-permute-start(bf16[576,768]{1,0:T(8,128)(2,1)} %get-tuple-element.476), channel_id=1, source_target_pairs={{0,1},{1,0},{2,3},{3,2},{4,5},{5,4},{6,7},{7,6},{8,9},{9,8},{10,11... | collective-permute-start | bytes 2654216 | tf_op jit(solution)/shard_map/ppermute | solution.py:59
  345.1 38.3 %collective-permute-start.19 = (bf16[576,768]{1,0:T(8,128)(2,1)}, bf16[576,768]{1,0:T(8,128)(2,1)}, u32[]{:S(2)}, u32[]{:S(2)}) collective-permute-start(bf16[576,768]{1,0:T(8,128)(2,1)} %get-tuple-element.475), channel_id=1, source_target_pairs={{0,1},{1,0},{2,3},{3,2},{4,5},{5,4},{6,7},{7,6},{8,9},{9,8},{10,11... | collective-permute-start | bytes 2654216 | tf_op jit(solution)/shard_map/ppermute | solution.py:59
  405.7 11.9 %collective-permute-start.25 = (bf16[3,4,2,1,48,768]{5,4,0,3,2,1:T(8,128)(2,1)}, bf16[3,4,2,1,48,768]{5,4,0,3,2,1:T(8,128)(2,1)}, u32[]{:S(2)}, u32[]{:S(2)}) collective-permute-start(bf16[3,4,2,1,48,768]{5,4,0,3,2,1:T(8,128)(2,1)} %copy.142), channel_id=1, source_target_pairs={{0,2},{2,0},{4,6},{6,4},{8,10},{10,8},{12,14},{14,12},{16,18},{18,... | collective-permute-start | bytes 5308424 | tf_op jit(solution)/shard_map/ppermute | solution.py:59
  405.8 30.1 %all-to-all-start.6 = ((bf16[16,48,768]{2,1,0:T(8,128)(2,1)}), bf16[16,48,768]{2,1,0:T(8,128)(2,1)}, u32[]{:S(2)}, u32[]{:S(2)}) async-start(bf16[16,48,768]{2,1,0:T(8,128)(2,1)} %bitcast.176), calls=%async_computation.6 | async-start | bytes 2359296 | tf_op jit(solution)/shard_map/all_to_all | solution.py:923
  412.8 55.1 %collective-permute-start.27 = (bf16[4,4,1,1,48,768]{5,4,0,3,2,1:T(8,128)(2,1)}, bf16[4,4,1,1,48,768]{5,4,0,3,2,1:T(8,128)(2,1)}, u32[]{:S(2)}, u32[]{:S(2)}) collective-permute-start(bf16[4,4,1,1,48,768]{5,4,0,3,2,1:T(8,128)(2,1)} %constant_dynamic-slice_fusion.11), channel_id=1, source_target_pairs={{0,4},{2,6},{4,0},{6,2},{8,12},{10,14},{12,8},{14,10},{16,20},{18,... | collective-permute-start | bytes 3538952 | tf_op jit(solution)/shard_map/ppermute | solution.py:59
  421.9 48.5 %collective-permute-start.26 = (bf16[3,4,2,1,48,384]{5,4,0,3,2,1:T(8,128)(2,1)}, bf16[3,4,2,1,48,384]{5,4,0,3,2,1:T(8,128)(2,1)}, u32[]{:S(2)}, u32[]{:S(2)}) collective-permute-start(bf16[3,4,2,1,48,384]{5,4,0,3,2,1:T(8,128)(2,1)} %constant_dynamic-slice_fusion.8), channel_id=1, source_target_pairs={{0,1},{1,0},{2,3},{3,2},{4,5},{5,4},{6,7},{7,6},{8,9},{9,8},{10,11... | collective-permute-start | bytes 2654216 | tf_op jit(solution)/shard_map/ppermute | solution.py:59
  436.0 40.2 %collective-permute-start.28 = (bf16[768,768]{1,0:T(8,128)(2,1)}, bf16[768,768]{1,0:T(8,128)(2,1)}, u32[]{:S(2)}, u32[]{:S(2)}) collective-permute-start(bf16[768,768]{1,0:T(8,128)(2,1)} %bitcast.46), channel_id=1, source_target_pairs={{0,1},{1,0},{2,3},{3,2},{4,5},{5,4},{6,7},{7,6},{8,9},{9,8},{10,11... | collective-permute-start | bytes 3538952 | tf_op jit(solution)/shard_map/ppermute | solution.py:59
  472.7 11.1 %collective-permute-start.29 = (bf16[3,4,1,1,48,384]{5,4,0,3,2,1:T(8,128)(2,1)S(1)}, bf16[3,4,1,1,48,384]{5,4,0,3,2,1:T(8,128)(2,1)S(1)}, u32[]{:S(2)}, u32[]{:S(2)}) collective-permute-start(bf16[3,4,1,1,48,384]{5,4,0,3,2,1:T(8,128)(2,1)S(1)} %constant_dynamic-slice_fusion.6), channel_id=1, source_target_pairs={{0,4},{2,6},{4,0},{6,2},{8,12},{10,14},{12,8},{14,10},{16,20},{18,... | collective-permute-start | bytes 1327112 | tf_op jit(solution)/shard_map/ppermute | solution.py:59
  473.3 27.0 %collective-permute-start.33 = (bf16[4,1,1,1,48,768]{5,4,0,3,2,1:T(8,128)(2,1)}, bf16[4,1,1,1,48,768]{5,4,0,3,2,1:T(8,128)(2,1)}, u32[]{:S(2)}, u32[]{:S(2)}) collective-permute-start(bf16[4,1,1,1,48,768]{5,4,0,3,2,1:T(8,128)(2,1)} %get-tuple-element.488), channel_id=1, source_target_pairs={{0,8},{2,10},{4,12},{6,14},{8,16},{10,18},{12,20},{14,22},{16,24},... | collective-permute-start | bytes 884744 | tf_op jit(solution)/shard_map/ppermute | solution.py:59
  474.7 40.8 %collective-permute-start.38 = (bf16[2,4,48,768]{3,2,1,0:T(8,128)(2,1)}, bf16[2,4,48,768]{3,2,1,0:T(8,128)(2,1)}, u32[]{:S(2)}, u32[]{:S(2)}) collective-permute-start(bf16[2,4,48,768]{3,2,1,0:T(8,128)(2,1)} %reduce-scatter.2.cloned.1.call-done), channel_id=1, source_target_pairs={{0,1},{1,0},{2,3},{3,2},{4,5},{5,4},{6,7},{7,6},{8,9},{9,8},{10,11... | collective-permute-start | bytes 1769480 | tf_op jit(solution)/shard_map/ppermute | solution.py:59
  476.2 25.9 %collective-permute-start.34 = (bf16[4,1,1,1,48,768]{5,4,0,3,2,1:T(8,128)(2,1)}, bf16[4,1,1,1,48,768]{5,4,0,3,2,1:T(8,128)(2,1)}, u32[]{:S(2)}, u32[]{:S(2)}) collective-permute-start(bf16[4,1,1,1,48,768]{5,4,0,3,2,1:T(8,128)(2,1)} %get-tuple-element.487), channel_id=1, source_target_pairs={{0,16},{2,18},{4,20},{6,22},{8,24},{10,26},{12,28},{14,30},{16,0},... | collective-permute-start | bytes 884744 | tf_op jit(solution)/shard_map/ppermute | solution.py:59
  493.6 10.7 %collective-permute-start.35 = (bf16[4,1,1,1,48,768]{5,4,0,3,2,1:T(8,128)(2,1)S(1)}, bf16[4,1,1,1,48,768]{5,4,0,3,2,1:T(8,128)(2,1)S(1)}, u32[]{:S(2)}, u32[]{:S(2)}) collective-permute-start(bf16[4,1,1,1,48,768]{5,4,0,3,2,1:T(8,128)(2,1)S(1)} %get-tuple-element.486), channel_id=1, source_target_pairs={{0,24},{2,26},{4,28},{6,30},{8,0},{10,2},{12,4},{14,6},{16,8},{18,... | collective-permute-start | bytes 884744 | tf_op jit(solution)/shard_map/ppermute | solution.py:59
  496.3 17.5 %collective-permute-start.30 = (bf16[3,1,1,1,48,384]{5,4,0,3,2,1:T(8,128)(2,1)}, bf16[3,1,1,1,48,384]{5,4,0,3,2,1:T(8,128)(2,1)S(1)}, u32[]{:S(2)}, u32[]{:S(2)}) collective-permute-start(bf16[3,1,1,1,48,384]{5,4,0,3,2,1:T(8,128)(2,1)} %get-tuple-element.501), channel_id=1, source_target_pairs={{0,8},{2,10},{4,12},{6,14},{8,16},{10,18},{12,20},{14,22},{16,24},... | collective-permute-start | bytes 331784 | tf_op jit(solution)/shard_map/ppermute | solution.py:59
  500.3 13.5 %collective-permute-start.31 = (bf16[3,1,1,1,48,384]{5,4,0,3,2,1:T(8,128)(2,1)S(1)}, bf16[3,1,1,1,48,384]{5,4,0,3,2,1:T(8,128)(2,1)S(1)}, u32[]{:S(2)}, u32[]{:S(2)}) collective-permute-start(bf16[3,1,1,1,48,384]{5,4,0,3,2,1:T(8,128)(2,1)S(1)} %copy-done.72), channel_id=1, source_target_pairs={{0,16},{2,18},{4,20},{6,22},{8,24},{10,26},{12,28},{14,30},{16,0},... | collective-permute-start | bytes 331784 | tf_op jit(solution)/shard_map/ppermute | solution.py:59
  502.0 11.8 %collective-permute-start.32 = (bf16[3,1,1,1,48,384]{5,4,0,3,2,1:T(8,128)(2,1)S(1)}, bf16[3,1,1,1,48,384]{5,4,0,3,2,1:T(8,128)(2,1)S(1)}, u32[]{:S(2)}, u32[]{:S(2)}) collective-permute-start(bf16[3,1,1,1,48,384]{5,4,0,3,2,1:T(8,128)(2,1)S(1)} %copy-done.71), channel_id=1, source_target_pairs={{0,24},{2,26},{4,28},{6,30},{8,0},{10,2},{12,4},{14,6},{16,8},{18,... | collective-permute-start | bytes 331784 | tf_op jit(solution)/shard_map/ppermute | solution.py:59
  506.2 14.1 %collective-permute-start.37 = (bf16[4,48,768]{2,1,0:T(8,128)(2,1)}, bf16[4,48,768]{2,1,0:T(8,128)(2,1)S(1)}, u32[]{:S(2)}, u32[]{:S(2)}) collective-permute-start(bf16[4,48,768]{2,1,0:T(8,128)(2,1)} %fusion.48), channel_id=1, source_target_pairs={{0,1},{1,0},{2,3},{3,2},{4,5},{5,4},{6,7},{7,6},{8,9},{9,8},{10,11... | collective-permute-start | bytes 884744 | tf_op jit(solution)/shard_map/ppermute | solution.py:59
  547.5 14.4 %collective-permute-start.43 = (f32[4]{0:T(128)S(1)}, f32[4]{0:T(128)S(1)}, u32[]{:S(2)}, u32[]{:S(2)}) collective-permute-start(f32[4]{0:T(128)S(1)} %slice_bitcast_fusion.4), channel_id=1, source_target_pairs={{0,1},{1,0},{2,3},{3,2},{4,5},{5,4},{6,7},{7,6},{8,9},{9,8},{10,11... | collective-permute-start | bytes 56 | tf_op jit(solution)/shard_map/ppermute | solution.py:106
  (130 other events, 774.4 us)
Sparse Core Ops, SparseCore 0:
  11.8 116.2 all-gather.1
  340.8 127.0 reduce-scatter.1
